TPU v7x, 32 devices: a whole 2x2x4 slice. The times are simulated.
32 devices in a mesh: fsdp: 4 (over y, x), ctx: 4 (over z), tp: 2 (over core).
Axes of the slice: x: 2, y: 2, z: 4, core: 2. Of those that a mesh axis runs over, the one named last changes fastest.
Arguments:
- tokens: bfloat16 [3072, 2048], P(('fsdp', 'ctx')), may hold values from -6 to 6
- cotangent: bfloat16 [3072, 2048], P(('fsdp', 'ctx')), may hold values from -6 to 6
- attn_ids: int32 [3072, 2], P(('fsdp', 'ctx')), may hold values from 0 to 3, all different within a row; in each aligned block of 192 rows (0 to 191, 192 to 383, ...) at most 144 rows name the same one
- mlp_ids: int32 [3072, 2], P(('fsdp', 'ctx')), may hold values from 0 to 3, all different within a row; in each aligned block of 192 rows (0 to 191, 192 to 383, ...) at most 144 rows name the same one
- span_ids: int32 [4, 2], replicated, may hold values from 0 to 7, as said below
- attn_gain: bfloat16 [2048], P('ctx'), may hold values from 0.25 to 1.75
- attn_router: bfloat16 [2048, 4], P('ctx'), may hold values from -0.09375 to 0.09375
- kv_weight: bfloat16 [2, 2048, 2048], P(None, 'ctx', ('fsdp', 'tp')), may hold values from -0.125 to 0.125
- query_weight: bfloat16 [4, 2048, 2048], P(None, 'ctx', ('fsdp', 'tp')), may hold values from -0.125 to 0.125
- output_weight: bfloat16 [4, 2048, 2048], P(None, 'ctx', ('fsdp', 'tp')), may hold values from -2 to 2
- mlp_gain: bfloat16 [2048], P('ctx'), may hold values from 0.25 to 1.75
- mlp_router: bfloat16 [2048, 4], P('ctx'), may hold values from -0.09375 to 0.09375
- gate_up_weight: bfloat16 [4, 2, 2048, 5632], P(None, None, 'ctx', ('fsdp', 'tp')), may hold values from -0.125 to 0.125
- down_weight: bfloat16 [4, 2048, 5632], P(None, 'ctx', ('fsdp', 'tp')), may hold values from -0.078125 to 0.078125
Outputs:
- layer_out: bfloat16 [3072, 2048], P(('fsdp', 'ctx'))
- grad_tokens: bfloat16 [3072, 2048], P(('fsdp', 'ctx'))
- grad_attn_gain: float32 [2048], P(('fsdp', 'ctx'))
- grad_attn_router: float32 [2048, 4], P(('fsdp', 'ctx'))
- grad_kv_weight: float32 [2, 2048, 2048], P(None, 'ctx', ('fsdp', 'tp'))
- grad_query_weight: float32 [4, 2048, 2048], P(None, 'ctx', ('fsdp', 'tp'))
- grad_output_weight: float32 [4, 2048, 2048], P(None, 'ctx', ('fsdp', 'tp'))
- grad_mlp_gain: float32 [2048], P(('fsdp', 'ctx'))
- grad_mlp_router: float32 [2048, 4], P(('fsdp', 'ctx'))
- grad_gate_up: float32 [4, 2, 2048, 5632], P(None, None, 'ctx', ('fsdp', 'tp'))
- grad_down: float32 [4, 2048, 5632], P(None, 'ctx', ('fsdp', 'tp'))
Inputs may be any that keep to these rules, and one draw needn't show every extreme that they name: `attn_ids`: each row names two different experts; among the 192 rows of one device no expert is named more than 144 times, a bound that some block reaches. `mlp_ids`: each row names two different experts; among the 192 rows of one device no expert is named more than 144 times, a bound that some block reaches. `span_ids`: row c holds p and 2 * 4 - 1 - p for a p below 4; every span number appears once.
All inputs are finite; a program needn't handle non-finite values.
Results may differ from a plain program's by a relative error of at most 0.025.
Values may be sent and summed in bfloat16 or wider, within the bound.
A program may use at most 448 MiB of HBM per device.

v0:
```python
import math

import jax
import jax.numpy as jnp
from jax import lax
from jax.sharding import PartitionSpec as P

DH = 128


EPSILON = 1e-06
ROPE_BASE = 10000.0
MASKED = -1e30
HIGH = lax.Precision.HIGHEST


def for_sending(array):
    return jax.tree.map(lambda a: a.astype(jnp.bfloat16) if a.dtype == jnp.float32 else a, array)


def positions(span_ids, tok_rows):
    half_len = tok_rows // 2
    offsets = jnp.arange(tok_rows, dtype=jnp.int32)
    upper_part = (offsets >= half_len).astype(jnp.int32)
    within = offsets - upper_part * half_len
    span_of = span_ids[:, 0:1] * (1 - upper_part)[None, :] + span_ids[:, 1:2] * upper_part[None, :]
    return (span_of * half_len + within[None, :]).reshape(-1)


def rotation(place):
    freqs = ROPE_BASE ** (-jnp.arange(DH // 2, dtype=jnp.float32) / (DH // 2))
    angles = place.astype(jnp.float32)[:, None] * freqs[None, :]
    return (jnp.cos(angles), jnp.sin(angles))


def rope(values, cosine_table, sine_table, transpose_it):
    row_count = values.shape[0]
    halves = values.reshape(row_count, -1, 2, DH // 2)
    lower_half = halves[:, :, 0]
    upper_half = halves[:, :, 1]
    cosine_wide = cosine_table[:, None, :]
    sine_wide = sine_table[:, None, :]
    if transpose_it:
        turned = jnp.stack(
            [
                lower_half * cosine_wide + upper_half * sine_wide,
                upper_half * cosine_wide - lower_half * sine_wide,
            ],
            axis=2,
        )
    else:
        turned = jnp.stack(
            [
                lower_half * cosine_wide - upper_half * sine_wide,
                upper_half * cosine_wide + lower_half * sine_wide,
            ],
            axis=2,
        )
    return turned.reshape(row_count, -1)


def dispatch_maps(expert_ids, experts, capacity, groups):
    flat_ids = expert_ids.reshape(groups, -1)
    per_group = flat_ids.shape[1]
    onehot = (flat_ids[:, :, None] == jnp.arange(experts, dtype=jnp.int32)[None, None, :]).astype(
        jnp.int32
    )
    ranks = jnp.cumsum(onehot, axis=1) - onehot
    rank_of = jnp.sum(ranks * onehot, axis=2)
    group_of = jnp.arange(groups, dtype=jnp.int32)[:, None]
    flat_slot = (flat_ids * (groups * capacity) + group_of * capacity + rank_of).reshape(-1)
    slot_total = groups * per_group
    source = (
        jnp.zeros((experts * groups * capacity,), jnp.int32)
        .at[flat_slot]
        .set(jnp.arange(slot_total, dtype=jnp.int32))
    )
    filled = jnp.zeros((experts * groups * capacity,), jnp.float32).at[flat_slot].set(1.0)
    return (flat_slot, source, filled)


def to_blocks(row_values, source, filled, experts):
    picked = row_values[source] * filled[:, None].astype(row_values.dtype)
    return picked.reshape(experts, -1, row_values.shape[1])


def from_blocks(blocks, flat_slot):
    return blocks.reshape(-1, blocks.shape[-1])[flat_slot]


def to_heads(rows, groups, heads_here):
    length = rows.shape[0] // groups
    return (
        rows.reshape(groups, length, heads_here, DH)
        .transpose(0, 2, 1, 3)
        .reshape(groups * heads_here, length, DH)
    )


def from_heads(heads, groups, heads_here):
    length = heads.shape[1]
    return (
        heads.reshape(groups, heads_here, length, DH)
        .transpose(0, 2, 1, 3)
        .reshape(groups * length, heads_here * DH)
    )


def chosen_gates(normed, router, expert_ids, experts):
    logits = jnp.dot(normed, router, preferred_element_type=jnp.float32)
    onehot = (expert_ids[:, :, None] == jnp.arange(experts, dtype=jnp.int32)[None, None, :]).astype(
        jnp.float32
    )
    picked = jnp.sum(onehot * logits[:, None, :], axis=-1)
    return (jax.nn.softmax(picked, axis=-1), onehot)


def router_back(gates, grad_gates, onehot):
    inner = gates * (grad_gates - jnp.sum(gates * grad_gates, axis=-1, keepdims=True))
    return jnp.sum(onehot * inner[:, :, None], axis=1)


def tensor_total(values):
    return jax.tree.map(lambda part: part.astype(jnp.float32), lax.psum(for_sending(values), "tp"))


def owner_total(values):
    return jax.tree.map(
        lambda part: part.astype(jnp.float32),
        lax.psum_scatter(for_sending(values), "fsdp", scatter_dimension=0, tiled=True),
    )


def gather_rows(values):
    return lax.all_gather(values, "fsdp", axis=0, tiled=True)


def reduce_weights(term_fn, shard_rows):
    return lax.psum_scatter(
        term_fn(jnp.int32(0), shard_rows * lax.axis_size("ctx")).astype(jnp.bfloat16),
        "ctx",
        scatter_dimension=0,
        tiled=True,
    ).astype(jnp.float32)


def split_heads(key_value, groups, heads_here):
    width = key_value.shape[-1]
    key_heads = to_heads(key_value[0].reshape(-1, width), groups, heads_here)
    value_heads = to_heads(key_value[1].reshape(-1, width), groups, heads_here)
    return (key_heads, value_heads)


def per_device(
    tokens,
    cotangent,
    attn_ids,
    mlp_ids,
    span_ids,
    attn_gain,
    attn_router,
    kv_weight,
    query_weight,
    output_weight,
    mlp_gain,
    mlp_router,
    gate_up_weight,
    down_weight,
):
    sharded = (
        kv_weight,
        query_weight,
        output_weight,
        gate_up_weight,
        down_weight,
        attn_router,
        mlp_router,
        attn_gain,
        mlp_gain,
    )
    (
        kv_full,
        query_full,
        output_full,
        gate_up_full,
        down_full,
        router_one,
        router_two,
        gain_one,
        gain_two,
    ) = (
        lax.all_gather(sharded[0], "ctx", axis=1, tiled=True),
        lax.all_gather(sharded[1], "ctx", axis=1, tiled=True),
        lax.all_gather(sharded[2], "ctx", axis=1, tiled=True),
        lax.all_gather(sharded[3], "ctx", axis=2, tiled=True),
        lax.all_gather(sharded[4], "ctx", axis=1, tiled=True),
        lax.all_gather(sharded[5], "ctx", axis=0, tiled=True),
        lax.all_gather(sharded[6], "ctx", axis=0, tiled=True),
        lax.all_gather(sharded[7], "ctx", axis=0, tiled=True),
        lax.all_gather(sharded[8], "ctx", axis=0, tiled=True),
    )
    tok_rows = tokens.shape[0]
    model_width = tokens.shape[1]
    groups = lax.axis_size("fsdp")
    seq_len = tok_rows * lax.axis_size("ctx")
    capacity = 3 * tok_rows // 4
    attn_experts = query_weight.shape[0]
    mlp_experts = down_weight.shape[0]
    heads_here = kv_weight.shape[2] // DH
    scale_factor = 1.0 / math.sqrt(DH)
    own_start = lax.axis_index("fsdp") * tok_rows
    all_pos = positions(span_ids, tok_rows)
    own_pos = lax.dynamic_slice_in_dim(all_pos, lax.axis_index("ctx") * tok_rows, tok_rows)
    slot_pos = jnp.repeat(own_pos, 2)
    cosine_row, sine_row = rotation(jnp.tile(own_pos, groups))
    cosine_slot, sine_slot = rotation(jnp.tile(slot_pos, groups))
    causal = all_pos[None, :] <= slot_pos[:, None]
    ids_attn, ids_mlp = (
        lax.all_gather(attn_ids, "fsdp", axis=0, tiled=True),
        lax.all_gather(mlp_ids, "fsdp", axis=0, tiled=True),
    )
    inputs = tokens.astype(jnp.float32)
    inverse_one = lax.rsqrt(jnp.mean(inputs * inputs, axis=-1, keepdims=True) + EPSILON)
    scaled_one = inputs * inverse_one
    normed_one = (scaled_one * gain_one.astype(jnp.float32)).astype(jnp.bfloat16)
    rows_one = gather_rows(normed_one)
    attn_gates, attn_hot = chosen_gates(rows_one, router_one, ids_attn, attn_experts)
    gates_one_own = lax.dynamic_slice_in_dim(attn_gates, own_start, tok_rows, 0)
    hot_one_own = lax.dynamic_slice_in_dim(attn_hot, own_start, tok_rows, 0)
    key_local = rope(
        jnp.dot(rows_one, kv_full[0], preferred_element_type=jnp.float32),
        cosine_row,
        sine_row,
        False,
    ).astype(jnp.bfloat16)
    value_local = jnp.dot(rows_one, kv_full[1], preferred_element_type=jnp.float32).astype(
        jnp.bfloat16
    )
    local_pair = jnp.stack([key_local, value_local]).reshape(2, groups, tok_rows, -1)
    key_value = lax.all_gather(local_pair, "ctx", axis=2, tiled=True)
    key_heads, value_heads = split_heads(key_value, groups, heads_here)
    slot_a, source_a, filled_a = dispatch_maps(ids_attn, attn_experts, capacity, groups)
    block_in_one = to_blocks(rows_one, source_a // 2, filled_a, attn_experts)
    query_blocks = jnp.einsum(
        "ecd,edh->ech", block_in_one, query_full, preferred_element_type=jnp.float32
    )
    query_rows = rope(from_blocks(query_blocks, slot_a), cosine_slot, sine_slot, False).astype(
        jnp.bfloat16
    )
    query_heads = to_heads(query_rows, groups, heads_here)

    def forward_head(operands):
        query_h, key_h, value_h = operands
        scores = jnp.dot(query_h, key_h.T, preferred_element_type=jnp.float32) * scale_factor
        scores = jnp.where(causal, scores, MASKED)
        row_max = jnp.max(scores, axis=-1, keepdims=True)
        log_total = row_max + jnp.log(jnp.sum(jnp.exp(scores - row_max), axis=-1, keepdims=True))
        weights = jnp.exp(scores - log_total).astype(jnp.bfloat16)
        return (jnp.dot(weights, value_h, preferred_element_type=jnp.float32), log_total[:, 0])

    head_out, head_lse = lax.map(forward_head, (query_heads, key_heads, value_heads))
    mixed = from_heads(head_out, groups, heads_here).astype(jnp.bfloat16)
    mixed_blocks = to_blocks(mixed, source_a, filled_a, attn_experts)
    branch_blocks = jnp.einsum(
        "ech,edh->ecd", mixed_blocks, output_full, preferred_element_type=jnp.float32
    )
    branch_rows = from_blocks(branch_blocks, slot_a).reshape(-1, 2, model_width)
    attn_full = tensor_total(owner_total(jnp.sum(attn_gates[:, :, None] * branch_rows, axis=1)))
    residual = inputs + attn_full
    inverse_two = lax.rsqrt(jnp.mean(residual * residual, axis=-1, keepdims=True) + EPSILON)
    scaled_two = residual * inverse_two
    normed_two = (scaled_two * gain_two.astype(jnp.float32)).astype(jnp.bfloat16)
    rows_two = gather_rows(normed_two)
    mlp_gates, mlp_hot = chosen_gates(rows_two, router_two, ids_mlp, mlp_experts)
    gates_two_own = lax.dynamic_slice_in_dim(mlp_gates, own_start, tok_rows, 0)
    hot_two_own = lax.dynamic_slice_in_dim(mlp_hot, own_start, tok_rows, 0)
    slot_m, source_m, filled_m = dispatch_maps(ids_mlp, mlp_experts, capacity, groups)
    block_in_two = to_blocks(rows_two, source_m // 2, filled_m, mlp_experts)
    gate_pre = jnp.einsum(
        "ecd,edf->ecf", block_in_two, gate_up_full[:, 0], preferred_element_type=jnp.float32
    )
    up_pre = jnp.einsum(
        "ecd,edf->ecf", block_in_two, gate_up_full[:, 1], preferred_element_type=jnp.float32
    )
    sigmoid_gate = jax.nn.sigmoid(gate_pre)
    silu_gate = gate_pre * sigmoid_gate
    hidden_b = (silu_gate * up_pre).astype(jnp.bfloat16)
    mlp_blocks = jnp.einsum("ecf,edf->ecd", hidden_b, down_full, preferred_element_type=jnp.float32)
    mlp_rows = from_blocks(mlp_blocks, slot_m).reshape(-1, 2, model_width)
    mlp_full = tensor_total(owner_total(jnp.sum(mlp_gates[:, :, None] * mlp_rows, axis=1)))
    layer_out = (residual + mlp_full).astype(jnp.bfloat16)
    (
        kv_full,
        query_full,
        output_full,
        gate_up_full,
        down_full,
        router_one,
        router_two,
        gain_one,
        gain_two,
    ) = (
        lax.all_gather(sharded[0], "ctx", axis=1, tiled=True),
        lax.all_gather(sharded[1], "ctx", axis=1, tiled=True),
        lax.all_gather(sharded[2], "ctx", axis=1, tiled=True),
        lax.all_gather(sharded[3], "ctx", axis=2, tiled=True),
        lax.all_gather(sharded[4], "ctx", axis=1, tiled=True),
        lax.all_gather(sharded[5], "ctx", axis=0, tiled=True),
        lax.all_gather(sharded[6], "ctx", axis=0, tiled=True),
        lax.all_gather(sharded[7], "ctx", axis=0, tiled=True),
        lax.all_gather(sharded[8], "ctx", axis=0, tiled=True),
    )
    upstream = cotangent.astype(jnp.float32)
    upstream_rows_b = gather_rows(cotangent)
    upstream_rows = upstream_rows_b.astype(jnp.float32)
    grad_mlp_rows = jnp.sum(upstream_rows[:, None, :] * mlp_rows, axis=-1)
    gate_block_m = (mlp_gates.reshape(-1)[source_m] * filled_m).reshape(mlp_experts, -1, 1)
    upstream_blocks = to_blocks(upstream_rows_b, source_m // 2, filled_m, mlp_experts)
    grad_expert_b = (gate_block_m * upstream_blocks.astype(jnp.float32)).astype(jnp.bfloat16)
    grad_hidden = jnp.einsum(
        "ecd,edf->ecf", grad_expert_b, down_full, preferred_element_type=jnp.float32
    )
    silu_slope = sigmoid_gate * (1.0 + gate_pre * (1.0 - sigmoid_gate))
    grad_gate_b = (grad_hidden * up_pre * silu_slope).astype(jnp.bfloat16)
    grad_up_b = (grad_hidden * silu_gate).astype(jnp.bfloat16)
    grad_in_two = jnp.einsum(
        "ecf,edf->ecd", grad_gate_b, gate_up_full[:, 0], preferred_element_type=jnp.float32
    )
    grad_in_two = grad_in_two + jnp.einsum(
        "ecf,edf->ecd", grad_up_b, gate_up_full[:, 1], preferred_element_type=jnp.float32
    )
    grad_two_part = jnp.sum(from_blocks(grad_in_two, slot_m).reshape(-1, 2, model_width), axis=1)
    grad_norm_two, grad_gates_m = tensor_total(owner_total((grad_two_part, grad_mlp_rows)))
    grad_logits_two = router_back(gates_two_own, grad_gates_m, hot_two_own)
    grad_normed_two = grad_norm_two + jnp.dot(
        grad_logits_two, router_two.astype(jnp.float32).T, precision=HIGH
    )
    grad_scaled_two = grad_normed_two * gain_two.astype(jnp.float32)
    grad_residual = upstream + inverse_two * (
        grad_scaled_two
        - scaled_two * jnp.mean(grad_scaled_two * scaled_two, axis=-1, keepdims=True)
    )
    grad_res_rows = lax.all_gather(
        grad_residual.astype(jnp.bfloat16), "fsdp", axis=0, tiled=True
    ).astype(grad_residual.dtype)
    grad_attn_rows = jnp.sum(grad_res_rows[:, None, :] * branch_rows, axis=-1)
    gate_block_a = (attn_gates.reshape(-1)[source_a] * filled_a).reshape(attn_experts, -1, 1)
    grad_branch_b = (
        gate_block_a * to_blocks(grad_res_rows, source_a // 2, filled_a, attn_experts)
    ).astype(jnp.bfloat16)
    grad_mixed_blocks = jnp.einsum(
        "ecd,edh->ech", grad_branch_b, output_full, preferred_element_type=jnp.float32
    )
    grad_mixed = from_blocks(grad_mixed_blocks, slot_a).astype(jnp.bfloat16)
    grad_mixed_heads = to_heads(grad_mixed, groups, heads_here)

    def backward_head(operands):
        query_h, key_h, value_h, grad_h, lse_h = operands
        scores = jnp.dot(query_h, key_h.T, preferred_element_type=jnp.float32) * scale_factor
        scores = jnp.where(causal, scores, MASKED)
        probs = jnp.exp(scores - lse_h[:, None])
        weights = probs.astype(jnp.bfloat16)
        grad_probs = jnp.dot(grad_h, value_h.T, preferred_element_type=jnp.float32)
        centre = jnp.sum(probs * grad_probs, axis=-1, keepdims=True)
        grad_scores = (probs * (grad_probs - centre)).astype(jnp.bfloat16)
        grad_query_h = (
            jnp.dot(grad_scores, key_h, preferred_element_type=jnp.float32) * scale_factor
        )
        grad_key_h = (
            jnp.dot(grad_scores.T, query_h, preferred_element_type=jnp.float32) * scale_factor
        )
        grad_value_h = jnp.dot(weights.T, grad_h, preferred_element_type=jnp.float32)
        return (grad_query_h, grad_key_h, grad_value_h)

    grad_query_heads, grad_key_heads, grad_value_heads = lax.map(
        backward_head, (query_heads, key_heads, value_heads, grad_mixed_heads, head_lse)
    )
    grad_kv_all = jnp.stack(
        [
            from_heads(grad_key_heads, groups, heads_here).reshape(groups, seq_len, -1),
            from_heads(grad_value_heads, groups, heads_here).reshape(groups, seq_len, -1),
        ]
    )
    grad_kv_own = (
        lax.psum_scatter(grad_kv_all.astype(jnp.bfloat16), "ctx", scatter_dimension=2, tiled=True)
        .astype(jnp.float32)
        .reshape(2, groups * tok_rows, -1)
    )
    grad_key_b = rope(grad_kv_own[0], cosine_row, sine_row, True).astype(jnp.bfloat16)
    grad_value_b = grad_kv_own[1].astype(jnp.bfloat16)
    grad_query_rows = rope(
        from_heads(grad_query_heads, groups, heads_here), cosine_slot, sine_slot, True
    ).astype(jnp.bfloat16)
    grad_query_blocks = to_blocks(grad_query_rows, source_a, filled_a, attn_experts)
    grad_in_one = jnp.einsum(
        "ech,edh->ecd", grad_query_blocks, query_full, preferred_element_type=jnp.float32
    )
    grad_one_part = jnp.sum(from_blocks(grad_in_one, slot_a).reshape(-1, 2, model_width), axis=1)
    grad_one_part = grad_one_part + jnp.einsum(
        "nh,dh->nd", grad_key_b, kv_full[0], preferred_element_type=jnp.float32
    )
    grad_one_part = grad_one_part + jnp.einsum(
        "nh,dh->nd", grad_value_b, kv_full[1], preferred_element_type=jnp.float32
    )
    grad_norm_one, grad_gates_a = tensor_total(owner_total((grad_one_part, grad_attn_rows)))
    grad_logits_one = router_back(gates_one_own, grad_gates_a, hot_one_own)
    grad_normed_one = grad_norm_one + jnp.dot(
        grad_logits_one, router_one.astype(jnp.float32).T, precision=HIGH
    )
    grad_scaled_one = grad_normed_one * gain_one.astype(jnp.float32)
    grad_input = grad_residual + inverse_one * (
        grad_scaled_one
        - scaled_one * jnp.mean(grad_scaled_one * scaled_one, axis=-1, keepdims=True)
    )
    grad_tokens = grad_input.astype(jnp.bfloat16)
    gain_one_column = jnp.sum(grad_normed_one * scaled_one, axis=0)
    gain_two_column = jnp.sum(grad_normed_two * scaled_two, axis=0)
    ctx_rows = model_width // lax.axis_size("ctx")

    def attention_terms(first_row, row_count):
        key_term = jnp.einsum("nd,nh->dh", rows_one, grad_key_b, preferred_element_type=jnp.float32)
        value_term = jnp.einsum(
            "nd,nh->dh", rows_one, grad_value_b, preferred_element_type=jnp.float32
        )
        query_term = jnp.einsum(
            "ecd,ech->deh", block_in_one, grad_query_blocks, preferred_element_type=jnp.float32
        )
        output_term = jnp.einsum(
            "ecd,ech->deh", grad_branch_b, mixed_blocks, preferred_element_type=jnp.float32
        )
        return jnp.concatenate(
            [key_term[:, None], value_term[:, None], query_term, output_term], axis=1
        )

    attention_shard = reduce_weights(attention_terms, ctx_rows)
    grad_kv_weight = attention_shard[:, 0:2].transpose(1, 0, 2)
    grad_query_weight = attention_shard[:, 2 : 2 + attn_experts].transpose(1, 0, 2)
    grad_output_weight = attention_shard[:, 2 + attn_experts :].transpose(1, 0, 2)

    def expert_terms(expert):

        def terms(first_row, row_count):
            cols_two = block_in_two[expert]
            gate_term = jnp.einsum(
                "cd,cf->df", cols_two, grad_gate_b[expert], preferred_element_type=jnp.float32
            )
            up_term = jnp.einsum(
                "cd,cf->df", cols_two, grad_up_b[expert], preferred_element_type=jnp.float32
            )
            down_cols = grad_expert_b[expert]
            down_term = jnp.einsum(
                "cd,cf->df", down_cols, hidden_b[expert], preferred_element_type=jnp.float32
            )
            return jnp.stack([gate_term, up_term, down_term], axis=1)

        return terms

    expert_shards = jnp.stack(
        [reduce_weights(expert_terms(expert), ctx_rows) for expert in range(mlp_experts)]
    )
    grad_gate_up = expert_shards[:, :, 0:2].transpose(0, 2, 1, 3)
    grad_down = expert_shards[:, :, 2]
    cols_one = normed_one.astype(jnp.float32)
    cols_two = normed_two.astype(jnp.float32)
    router_one_term = jnp.dot(cols_one.T, grad_logits_one, precision=HIGH)
    router_two_term = jnp.dot(cols_two.T, grad_logits_two, precision=HIGH)
    gain_one_term = gain_one_column[:, None]
    gain_two_term = gain_two_column[:, None]
    small_shard = lax.psum_scatter(
        jnp.concatenate([gain_one_term, gain_two_term, router_one_term, router_two_term], axis=1),
        ("fsdp", "ctx"),
        scatter_dimension=0,
        tiled=True,
    )
    grad_attn_gain = small_shard[:, 0]
    grad_mlp_gain = small_shard[:, 1]
    grad_attn_router = small_shard[:, 2 : 2 + attn_experts]
    grad_mlp_router = small_shard[:, 2 + attn_experts :]
    return (
        layer_out,
        grad_tokens,
        grad_attn_gain,
        grad_attn_router,
        grad_kv_weight,
        grad_query_weight,
        grad_output_weight,
        grad_mlp_gain,
        grad_mlp_router,
        grad_gate_up,
        grad_down,
    )


def solution(mesh):
    placed = (
        P(("fsdp", "ctx"), None),
        P(("fsdp", "ctx"), None),
        P(("fsdp", "ctx"), None),
        P(("fsdp", "ctx"), None),
        P(),
        P("ctx"),
        P("ctx", None),
        P(None, "ctx", ("fsdp", "tp")),
        P(None, "ctx", ("fsdp", "tp")),
        P(None, "ctx", ("fsdp", "tp")),
        P("ctx"),
        P("ctx", None),
        P(None, None, "ctx", ("fsdp", "tp")),
        P(None, "ctx", ("fsdp", "tp")),
    )
    return jax.shard_map(
        per_device,
        mesh=mesh,
        in_specs=placed,
        out_specs=(
            P(("fsdp", "ctx"), None),
            P(("fsdp", "ctx"), None),
            P(("fsdp", "ctx")),
            P(("fsdp", "ctx"), None),
            P(None, "ctx", ("fsdp", "tp")),
            P(None, "ctx", ("fsdp", "tp")),
            P(None, "ctx", ("fsdp", "tp")),
            P(("fsdp", "ctx")),
            P(("fsdp", "ctx"), None),
            P(None, None, "ctx", ("fsdp", "tp")),
            P(None, "ctx", ("fsdp", "tp")),
        ),
        check_vma=False,
    )
```

profile of v0, /device:TPU:0, one launch (start us, length us, event | category | flops | bytes accessed | tf_op | source)
XLA Modules:
  0.0 2642.5 jit_solution(3594698173338154874)
XLA Ops:
  29.0 29.3 %all-gather.19.cloned.1.call-done = bf16[2,2048,256]{2,1,0:T(8,128)(2,1)} async-done(((bf16[2,512,256]{2,1,0:T(8,128)(2,1)}), bf16[2,2048,256]{2,1,0:T(8,128)(2,1)}) %all-gather.19.cloned.1.call-update) | async-done | bytes 2097168 | tf_op jit(solution)/shard_map/all_gather | solution.py:192
  61.0 42.5 %all-gather.15.cloned.1.call-done = bf16[768,2048]{1,0:T(8,128)(2,1)} async-done(((bf16[192,2048]{1,0:T(8,128)(2,1)}), bf16[768,2048]{1,0:T(8,128)(2,1)}) %all-gather.15.cloned.1.call-update) | async-done | bytes 3145744 | tf_op jit(solution)/shard_map/all_gather | solution.py:135
  214.5 17.5 gather_fusion.9
  269.7 32.4 %while.30 = (s32[]{:T(128)}, bf16[8,384,128]{2,1,0:T(8,128)(2,1)}, f32[8,384]{1,0:T(8,128)}, bf16[8,384,128]{2,1,0:T(8,128)(2,1)}, bf16[8,768,128]{2,1,0:T(8,128...) while((s32[]{:T(128)}, bf16[8,384,128]{2,1,0:T(8,128)(2,1)}, ...), condition=%wide.region_12.13_spmd.clone.clone, body=%wide.region_9.12_spmd.clone.sunk.clone | while | flops 153353856 | bytes 4252769 | solution.py:261
  311.7 19.2 all-gather.23.cloned.1.call-done
  340.8 19.1 gather_fusion.3
  375.3 21.6 multiply_reduce_fusion.4
  397.0 42.6 %reduce-scatter.18.cloned.1.call-done = bf16[192,2048]{1,0:T(8,128)(2,1)} async-done(((bf16[768,2048]{1,0:T(8,128)(2,1)}), bf16[192,2048]{1,0:T(8,128)(2,1)}) %reduce-scatter.18.cloned.1.call-update) | async-done | bytes 786448 | tf_op jit(solution)/shard_map/reduce_scatter | solution.py:130
  508.3 20.8 gather_fusion.7
  529.1 25.8 all-gather.25.cloned.1.call-done
  591.4 356.7 %all-gather.27.cloned.1.call-done = bf16[4,2,2048,704]{2,3,0,1:T(8,128)(2,1)} async-done(((bf16[4,2,512,704]{2,3,0,1:T(8,128)(2,1)}), bf16[4,2,2048,704]{2,3,0,1:T(8,128)(2,1)}) %all-gather.27.cloned.1.call-update) | async-done | bytes 23068688 | tf_op jit(solution)/shard_map/all_gather | solution.py:195
  979.2 170.0 %all-gather.29.cloned.1.call-done = bf16[4,2048,704]{1,2,0:T(8,128)(2,1)} async-done(((bf16[4,512,704]{1,2,0:T(8,128)(2,1)}), bf16[4,2048,704]{1,2,0:T(8,128)(2,1)}) %all-gather.29.cloned.1.call-update) | async-done | bytes 11534352 | tf_op jit(solution)/shard_map/all_gather | solution.py:196
  1149.2 18.4 multiply_convert_fusion.3
  1182.6 18.2 fusion.56
  1200.9 18.9 gather_fusion.8
  1235.1 18.3 reduce_sum.232
  1274.3 19.1 gather_fusion.5
  1308.8 28.0 %multiply_reduce_fusion.2 = (bf16[768,2]{1,0:T(8,128)(2,1)}, bf16[768,2048]{1,0:T(8,128)(2,1)}) fusion(f32[768,2,2048]{2,1,0:T(2,128)} %reshape.658, f32[768,2048]{1,0:T(8,128)} %convert_element_type.295, f32[768,2]{1,0:T(8,128)S(1)} %copy-done.32), kind=kLoop, calls=%fused_computation.76 | loop fusion | flops 11008512 | bytes 22029312 | tf_op jit(solution)/shard_map/reduce_sum | solution.py:316
  1337.6 22.1 reduce-scatter.40.cloned.1.call-done
  1363.3 17.9 all-reduce.7.cloned.1.call-done
  1387.4 45.1 %all-gather.33.cloned.1.call-done = bf16[768,2048]{1,0:T(8,128)(2,1)} async-done(((bf16[192,2048]{1,0:T(8,128)(2,1)}), bf16[768,2048]{1,0:T(8,128)(2,1)}) %all-gather.33.cloned.1.call-update) | async-done | bytes 3145744 | tf_op jit(solution)/shard_map/all_gather | solution.py:343
  1437.9 21.0 gather_fusion.10
  1474.8 69.1 %while.31 = (s32[]{:T(128)}, f32[8,384,128]{2,1,0:T(8,128)}, bf16[8,768,128]{2,1,0:T(8,128)(2,1)}, bf16[8,768,128]{2,1,0:T(8,128)(2,1)}, bf16[8,384,128]{2,1,0:T...) while((s32[]{:T(128)}, f32[8,384,128]{2,1,0:T(8,128)}, ...), condition=%wide.region_39.40_spmd.clone.clone, body=%wide.region_37.39_spmd.clone.sunk.clone | while | flops 380583552 | bytes 10830969 | solution.py:375
  1578.6 18.9 gather_fusion.13
  1612.8 19.1 reduce_sum.237
  1666.7 44.0 %reduce-scatter.26.cloned.1.call-done = bf16[192,2048]{1,0:T(8,128)(2,1)} async-done(((bf16[768,2048]{1,0:T(8,128)(2,1)}), bf16[192,2048]{1,0:T(8,128)(2,1)}) %reduce-scatter.26.cloned.1.call-update) | async-done | bytes 786448 | tf_op jit(solution)/shard_map/reduce_scatter | solution.py:130
  1829.7 83.4 %reduce-scatter.38.cloned.1.call-done = bf16[512,3,704]{0,2,1:T(8,128)(2,1)} async-done(((bf16[2048,3,704]{0,2,1:T(8,128)(2,1)}), bf16[512,3,704]{0,2,1:T(8,128)(2,1)}) %reduce-scatter.38.cloned.1.call-update) | async-done | bytes 2162704 | tf_op jit(solution)/shard_map/reduce_scatter | solution.py:139
  1913.2 151.9 %reduce-scatter.36.cloned.1.call-done = bf16[512,3,704]{0,2,1:T(8,128)(2,1)} async-done(((bf16[2048,3,704]{0,2,1:T(8,128)(2,1)}), bf16[512,3,704]{0,2,1:T(8,128)(2,1)}) %reduce-scatter.36.cloned.1.call-update) | async-done | bytes 2162704 | tf_op jit(solution)/shard_map/reduce_scatter | solution.py:139
  2065.1 151.9 %reduce-scatter.34.cloned.1.call-done = bf16[512,3,704]{0,2,1:T(8,128)(2,1)} async-done(((bf16[2048,3,704]{0,2,1:T(8,128)(2,1)}), bf16[512,3,704]{0,2,1:T(8,128)(2,1)}) %reduce-scatter.34.cloned.1.call-update) | async-done | bytes 2162704 | tf_op jit(solution)/shard_map/reduce_scatter | solution.py:139
  2217.0 151.8 %reduce-scatter.32.cloned.1.call-done = bf16[512,3,704]{0,2,1:T(8,128)(2,1)} async-done(((bf16[2048,3,704]{0,2,1:T(8,128)(2,1)}), bf16[512,3,704]{0,2,1:T(8,128)(2,1)}) %reduce-scatter.32.cloned.1.call-update) | async-done | bytes 2162704 | tf_op jit(solution)/shard_map/reduce_scatter | solution.py:139
  2394.5 54.1 %reduce-scatter.28.cloned.1.call-done = f32[128,10]{0,1:T(8,128)} async-done(((f32[2048,10]{0,1:T(8,128)}), f32[128,10]{0,1:T(8,128)}) %reduce-scatter.28.cloned.1.call-update) | async-done | bytes 5136 | tf_op jit(solution)/shard_map/reduce_scatter | solution.py:469
  2451.2 174.0 %reduce-scatter.30.cloned.1.call-done = bf16[512,10,256]{0,2,1:T(8,128)(2,1)} async-done(((bf16[2048,10,256]{0,2,1:T(8,128)(2,1)}), bf16[512,10,256]{0,2,1:T(8,128)(2,1)}) %reduce-scatter.30.cloned.1.call-update) | async-done | bytes 2621456 | tf_op jit(solution)/shard_map/reduce_scatter | solution.py:139
  (611 shorter events, 785.1 us)
Async XLA Ops:
  7.2 51.1 %all-gather.19.cloned.1.call-start = ((), (), s32[]{:S(2)}) async-start(), calls=%async_computation.15 | async-start | bytes 2621440 | tf_op jit(solution)/shard_map/all_gather | solution.py:192
  7.9 95.5 %all-gather.15.cloned.1.call-start = ((), (), s32[]{:S(2)}) async-start(), calls=%async_computation.13 | async-start | bytes 3932160 | tf_op jit(solution)/shard_map/all_gather | solution.py:135
  26.4 217.6 %all-gather.17.cloned.1.call-start = ((), (), s32[]{:S(2)}) async-start(), calls=%async_computation.14 | async-start | bytes 5242880 | tf_op jit(solution)/shard_map/all_gather | solution.py:193
  27.2 232.0 %all-gather.21.cloned.1.call-start = ((), (), s32[]{:S(2)}) async-start(), calls=%async_computation.16 | async-start | bytes 3932160 | tf_op jit(solution)/shard_map/all_gather | solution.py:240
  29.0 82.9 %copy-start.33 = (f32[768,64]{0,1:T(8,128)}, f32[768,64]{0,1:T(8,128)S(1)}, u32[]{:S(2)}) copy-start(f32[768,64]{0,1:T(8,128)S(1)} %get-tuple-element.316) | copy-start | bytes 589828
  29.0 82.9 %copy-start.35 = (f32[768,64]{0,1:T(8,128)}, f32[768,64]{0,1:T(8,128)S(1)}, u32[]{:S(2)}) copy-start(f32[768,64]{0,1:T(8,128)S(1)} %get-tuple-element.317) | copy-start | bytes 589828
  120.1 210.8 %all-gather.23.cloned.1.call-start = ((), (), s32[]{:S(2)}) async-start(), calls=%async_computation.17 | async-start | bytes 5242880 | tf_op jit(solution)/shard_map/all_gather | solution.py:194
  120.7 318.9 %reduce-scatter.18.cloned.1.call-start = ((), (), s32[]{:S(2)}) async-start(), calls=%async_computation.18 | async-start | bytes 3932160 | tf_op jit(solution)/shard_map/reduce_scatter | solution.py:130
  170.9 170.0 %copy-start.44 = (s32[2048]{0:T(1024)}, s32[2048]{0:T(1024)S(1)}, u32[]{:S(2)}) copy-start(s32[2048]{0:T(1024)S(1)} %pad_clamp_fusion.5) | copy-start | bytes 24580
  234.2 96.7 %copy-start.41 = (bf16[4,576]{1,0:T(4,128)(2,1)}, bf16[4,576]{1,0:T(4,128)(2,1)S(1)}, u32[]{:S(2)}) copy-start(bf16[4,576]{1,0:T(4,128)(2,1)S(1)} %mul.579) | copy-start | bytes 13828
  396.9 64.2 %all-reduce.5.cloned.1.call-start = ((), (), s32[]{:S(2)}) async-start(), calls=%async_computation.19 | async-start | bytes 1572864 | tf_op jit(solution)/shard_map/psum | solution.py:124
  439.6 68.7 %all-gather.31.cloned.1.call-start = ((), (), s32[]{:S(2)}) async-start(), calls=%async_computation.24 | async-start | bytes 3932160 | tf_op jit(solution)/shard_map/all_gather | solution.py:135
  440.3 114.6 %all-gather.25.cloned.1.call-start = ((), (), s32[]{:S(2)}) async-start(), calls=%async_computation.20 | async-start | bytes 3932160 | tf_op jit(solution)/shard_map/all_gather | solution.py:135
  465.5 482.6 %all-gather.27.cloned.1.call-start = ((), (), s32[]{:S(2)}) async-start(), calls=%async_computation.21 | async-start | bytes 28835840 | tf_op jit(solution)/shard_map/all_gather | solution.py:195
  471.1 678.0 %all-gather.29.cloned.1.call-start = ((), (), s32[]{:S(2)}) async-start(), calls=%async_computation.22 | async-start | bytes 14417920 | tf_op jit(solution)/shard_map/all_gather | solution.py:196
  471.9 865.1 %reduce-scatter.22.cloned.1.call-start = ((), (), s32[]{:S(2)}) async-start(), calls=%async_computation.25 | async-start | bytes 3932160 | tf_op jit(solution)/shard_map/reduce_scatter | solution.py:130
  1253.4 106.2 %reduce-scatter.40.cloned.1.call-start = ((), (), s32[]{:S(2)}) async-start(), calls=%async_computation.36 | async-start | bytes 245760
  1308.8 72.5 %copy-start.5 = (bf16[192,2048]{1,0:T(8,128)(2,1)S(1)}, bf16[192,2048]{1,0:T(8,128)(2,1)}, u32[]{:S(2)}) copy-start(bf16[192,2048]{1,0:T(8,128)(2,1)} %param.18) | copy-start | bytes 2359300
  1308.8 72.4 %copy-start.7 = (bf16[192,2048]{1,0:T(8,128)(2,1)S(1)}, bf16[192,2048]{1,0:T(8,128)(2,1)}, u32[]{:S(2)}) copy-start(bf16[192,2048]{1,0:T(8,128)(2,1)} %all-reduce.5.cloned.1.call-done) | copy-start | bytes 2359300
  1336.9 44.3 %all-reduce.7.cloned.1.call-start = ((), (), s32[]{:S(2)}) async-start(), calls=%async_computation.26 | async-start | bytes 1572864 | tf_op jit(solution)/shard_map/psum | solution.py:124
  1337.5 95.0 %all-gather.33.cloned.1.call-start = ((), (), s32[]{:S(2)}) async-start(), calls=%async_computation.27 | async-start | bytes 3932160 | tf_op jit(solution)/shard_map/all_gather | solution.py:343
  1387.2 244.8 %reduce-scatter.24.cloned.1.call-start = ((), (), s32[]{:S(2)}) async-start(), calls=%async_computation.28 | async-start | bytes 3932160 | tf_op jit(solution)/shard_map/reduce_scatter | solution.py:385
  1556.7 110.0 %reduce-scatter.20.cloned.1.call-start = ((), (), s32[]{:S(2)}) async-start(), calls=%async_computation.23 | async-start | bytes 3932160 | tf_op jit(solution)/shard_map/reduce_scatter | solution.py:130
  1557.3 153.5 %reduce-scatter.26.cloned.1.call-start = ((), (), s32[]{:S(2)}) async-start(), calls=%async_computation.29 | async-start | bytes 3932160 | tf_op jit(solution)/shard_map/reduce_scatter | solution.py:130
  1644.7 156.0 %reduce-scatter.42.cloned.1.call-start = ((), (), s32[]{:S(2)}) async-start(), calls=%async_computation.37 | async-start | bytes 245760
  1658.6 157.4 %all-reduce.9.cloned.1.call-start = ((), (), s32[]{:S(2)}) async-start(), calls=%async_computation.38 | async-start | bytes 3145728 | tf_op jit(solution)/shard_map/psum | solution.py:124
  1710.8 202.4 %reduce-scatter.38.cloned.1.call-start = ((), (), s32[]{:S(2)}) async-start(), calls=%async_computation.35 | async-start | bytes 10813440 | tf_op jit(solution)/shard_map/reduce_scatter | solution.py:139
  1726.7 338.4 %reduce-scatter.36.cloned.1.call-start = ((), (), s32[]{:S(2)}) async-start(), calls=%async_computation.34 | async-start | bytes 10813440 | tf_op jit(solution)/shard_map/reduce_scatter | solution.py:139
  1744.0 473.0 %reduce-scatter.34.cloned.1.call-start = ((), (), s32[]{:S(2)}) async-start(), calls=%async_computation.33 | async-start | bytes 10813440 | tf_op jit(solution)/shard_map/reduce_scatter | solution.py:139
  1761.6 607.2 %reduce-scatter.32.cloned.1.call-start = ((), (), s32[]{:S(2)}) async-start(), calls=%async_computation.32 | async-start | bytes 10813440 | tf_op jit(solution)/shard_map/reduce_scatter | solution.py:139
  1779.1 669.5 %reduce-scatter.28.cloned.1.call-start = ((), (), s32[]{:S(2)}) async-start(), calls=%async_computation.30 | async-start | bytes 139264 | tf_op jit(solution)/shard_map/reduce_scatter | solution.py:469
  1820.6 804.6 %reduce-scatter.30.cloned.1.call-start = ((), (), s32[]{:S(2)}) async-start(), calls=%async_computation.31 | async-start | bytes 13107200 | tf_op jit(solution)/shard_map/reduce_scatter | solution.py:139
  (98 other events, 1387.8 us)
Sparse Core Ops, SparseCore 0:
  9.6 48.6 all-gather.18
  60.7 42.7 all-gather.14
  105.0 80.9 all-gather.16
  188.0 61.9 all-gather.20
  251.4 79.4 all-gather.22
  397.1 42.4 reduce-scatter.17
  441.9 19.1 all-reduce.4
  463.1 45.1 all-gather.30
  510.9 43.9 all-gather.24
  557.0 391.0 all-gather.26
  949.8 199.3 all-gather.28
  1253.6 42.1 reduce-scatter.21
  1337.0 22.6 reduce-scatter.39
  1362.0 19.1 all-reduce.6
  1387.3 45.1 all-gather.32
  1556.8 60.2 reduce-scatter.23
  1620.0 43.9 reduce-scatter.19
  1666.8 43.9 reduce-scatter.25
  1714.1 23.9 reduce-scatter.41
  1740.3 20.4 all-reduce.8
  1763.3 149.7 reduce-scatter.37
  1915.6 149.4 reduce-scatter.35
  2067.6 149.3 reduce-scatter.33
  2219.4 149.4 reduce-scatter.31
  2371.7 76.8 reduce-scatter.27
  2450.8 174.3 reduce-scatter.29
where the time goes:
time: 2660 us; the launch traced here: 2640 us
  waiting for transfers between devices  1610 us (61%)
  local copies, waits for them, and re-layouts  403 us (15%)
  matrix products  316 us (12%)
  other arithmetic  225 us (8%)
  blocking collectives  73.8 us (3%)
    reduce_scatter x5, waiting for transfers between devices, reduce_weights(): lax.psum_scatter(term_fn(jnp.int32(0), shard_rows * lax.axis_size('ctx'))...  713 us
    all_gather x1, waiting for transfers between devices, per_device(): lax.all_gather(sharded[3], 'ctx', axis=2, tiled=True)  357 us
    all_gather x1, waiting for transfers between devices, per_device(): lax.all_gather(sharded[4], 'ctx', axis=1, tiled=True)  170 us
    gather x7, local copies, waits for them, and re-layouts, from_blocks(): return blocks.reshape(-1, blocks.shape[-1])[flat_slot]  87.4 us
    reduce_scatter x4, waiting for transfers between devices, owner_total(): lax.psum_scatter(for_sending(values), 'fsdp', scatter_dimension=0, tiled=...  86.7 us
    all_gather x3, waiting for transfers between devices, gather_rows(): return lax.all_gather(values, 'fsdp', axis=0, tiled=True)  78.5 us
    gather x6, local copies, waits for them, and re-layouts, to_blocks(): picked = row_values[source] * filled[:, None].astype(row_values.dtype)  75.4 us
    reduce_scatter x1, waiting for transfers between devices, per_device(): lax.psum_scatter(jnp.concatenate([gain_one_term, gain_two_term, router_on...  54.1 us
  transfers between devices with their start and end apart: 26, of which 19 were waited for; matrix products, arithmetic and copies ran while one was open for 24% of the time, Pallas kernels for 0%

commit v1 on v0

v1 whole, which is shorter than its diff:
```python
import functools
import math

import jax
import jax.numpy as jnp
from jax import lax
from jax.experimental import pallas as pl
from jax.experimental.pallas import tpu as pltpu
from jax.sharding import PartitionSpec as P

DH = 128
EPSILON = 1e-06
ROPE_BASE = 10000.0
MASKED = -1e30
HIGH = lax.Precision.HIGHEST
MESH = pl.DeviceIdType.MESH
AXES = ("fsdp", "ctx", "tp")
F32 = jnp.float32
BF16 = jnp.bfloat16
VMEM_LIMIT = 60 * 1024 * 1024
NT = (((1,), (1,)), ((), ()))
NN = (((1,), (0,)), ((), ()))
TN = (((0,), (0,)), ((), ()))


def dot(a, b, dims=NN):
    return lax.dot_general(a, b, dims, preferred_element_type=F32)


class Layout:
    def __init__(self, experts):
        self.nf = lax.axis_size("fsdp")
        self.nc = lax.axis_size("ctx")
        self.nt = lax.axis_size("tp")
        self.experts = experts
        self.rep = self.nc // experts
        self.seqs = self.nf // self.nt
        self.f = lax.axis_index("fsdp")
        self.c = lax.axis_index("ctx")
        self.t = lax.axis_index("tp")
        self.home = self.t == self.f // self.seqs
        self.sizes = (self.nf, self.nc, self.nt, self.seqs)

    def flat(self, f, c, t):
        return (f * self.nc + c) * self.nt + t


def home_pairs(lay, move):
    pairs = []
    for f in range(lay.nf):
        t = f // lay.seqs
        for c in range(lay.nc):
            f2, c2 = move(f, c)
            pairs.append((lay.flat(f, c, t), lay.flat(f2, c2, t)))
    return pairs


def collect_permute(lay, block_of, blocks, stride):
    got, last = [], None
    for j in range(blocks):
        partial = block_of(j, last)
        zeros = jnp.zeros((lay.nf,) + partial.shape[1:], partial.dtype)
        full = lax.dynamic_update_slice_in_dim(zeros, partial, lay.t * lay.seqs, 0)
        last = lax.psum_scatter(full, "fsdp", scatter_dimension=0, tiled=True)[0]
        if j > 0:
            pairs = home_pairs(lay, lambda f, c: (f, (c - stride * j) % lay.nc))
            last = lax.ppermute(last, AXES, pairs)
        got.append(last)
    return jnp.stack(got)


class Haul:
    def __init__(self, array, piece=None, shape=None, both=False):
        self.array, self.piece, self.both = array, piece, both
        self.shape = array.shape if shape is None else shape

    def out_shapes(self, nc):
        dims = self.shape if self.piece is None else (nc,) + self.shape
        return [jax.ShapeDtypeStruct(dims, self.array.dtype)] * (2 if self.both else 1)

    def scratch(self, nc):
        return [pltpu.SemaphoreType.DMA((nc,))] * (4 if self.both else 2)

    def bind(self, place, src, outs, sems):
        load = Load()
        load.piece, load.both, load.place = self.piece, self.both, place
        load.src, load.outs, load.sems = src, outs, sems
        return load


class Load:
    def along_ctx(self, j):
        nc, c, nt, t = self.place
        return pltpu.make_async_remote_copy(
            src_ref=self.piece(self.src, lax.rem(c + j, nc)),
            dst_ref=self.outs[0].at[c],
            send_sem=self.sems[0].at[j],
            recv_sem=self.sems[1].at[j],
            device_id={"ctx": lax.rem(c + j, nc)},
            device_id_type=MESH,
        )

    def landed(self, j):
        nc, c, nt, t = self.place
        here = self.outs[0].at[lax.rem(c - j + nc, nc)]
        return pltpu.make_async_remote_copy(
            src_ref=here,
            dst_ref=here,
            send_sem=self.sems[0].at[j],
            recv_sem=self.sems[1].at[j],
            device_id={"ctx": lax.rem(c + j, nc)},
            device_id_type=MESH,
        )

    def to_core(self, j):
        nc, c, nt, t = self.place
        if self.piece is None:
            src, dst, at = self.src, self.outs[0], 0
        else:
            source = lax.rem(c - j + nc, nc)
            src = self.piece(self.src, c) if j == 0 else self.outs[0].at[source]
            dst, at = self.outs[1].at[source], 2
        return pltpu.make_async_remote_copy(
            src_ref=src,
            dst_ref=dst,
            send_sem=self.sems[at].at[j],
            recv_sem=self.sems[at + 1].at[j],
            device_id={"tp": lax.rem(t + 1, nt)},
            device_id_type=MESH,
        )

    def keep(self):
        nc, c, nt, t = self.place
        return pltpu.make_async_copy(
            self.piece(self.src, c), self.outs[0].at[c], self.sems[0].at[0]
        )

    def start(self):
        if self.piece is None:
            self.to_core(0).start()
            return
        for j in range(1, self.place[0]):
            self.along_ctx(j).start()
        self.keep().start()
        if self.both:
            self.to_core(0).start()

    def pass_on(self):
        if self.piece is None:
            return
        for j in range(1, self.place[0]):
            self.landed(j).wait_recv()
            if self.both:
                self.to_core(j).start()

    def finish(self):
        if self.piece is None:
            self.to_core(0).wait()
            return
        self.keep().wait()
        for j in range(self.place[0]):
            if j > 0:
                self.along_ctx(j).wait_send()
            if self.both:
                self.to_core(j).wait()


class Relay:
    both = True

    def __init__(self, array):
        self.array = array

    def out_shapes(self, nc):
        return [jax.ShapeDtypeStruct((nc,) + self.array.shape, self.array.dtype)] * 2

    def scratch(self, nc):
        return [pltpu.SemaphoreType.DMA((2, nc))] * 2 + [pltpu.SemaphoreType.DMA((nc,))] * 2

    def bind(self, place, src, outs, sems):
        load = RelayLoad()
        load.place, load.src, load.outs, load.sems = place, src, outs, sems
        return load


def relay_step(place, way, k, src, dst, send_sem, recv_sem):
    nc, c = place[:2]
    step = 1 - 2 * way
    copy = pltpu.make_async_remote_copy(
        src_ref=src,
        dst_ref=dst,
        send_sem=send_sem.at[way, k],
        recv_sem=recv_sem.at[way, k],
        device_id={"ctx": lax.rem(c + step + nc, nc)},
        device_id_type=MESH,
    )
    sent = jnp.logical_and(c - step * k >= 0, c - step * k < nc)
    sent = jnp.logical_and(sent, jnp.logical_and(c + step >= 0, c + step < nc))
    return copy, sent


def relayed(place, way, k):
    nc, c = place[:2]
    source = c - (1 - 2 * way) * k
    return lax.rem(source + nc, nc), jnp.logical_and(source >= 0, source < nc)


class RelayLoad:
    def copy(self, way, k):
        source = relayed(self.place, way, k)[0]
        src = self.src if k == 0 else self.outs[0].at[source]
        return relay_step(self.place, way, k, src, self.outs[0].at[source], *self.sems[:2])

    def arrival(self, way, k):
        source, there = relayed(self.place, way, k)
        here = self.outs[0].at[source]
        return pltpu.make_async_remote_copy(
            src_ref=here,
            dst_ref=here,
            send_sem=self.sems[0].at[way, k],
            recv_sem=self.sems[1].at[way, k - 1],
            device_id={"ctx": lax.rem(self.place[1] + 1, self.place[0])},
            device_id_type=MESH,
        ), there

    def to_core(self, source):
        nc, c, nt, t = self.place
        return pltpu.make_async_remote_copy(
            src_ref=self.outs[0].at[source],
            dst_ref=self.outs[1].at[source],
            send_sem=self.sems[2].at[source],
            recv_sem=self.sems[3].at[source],
            device_id={"tp": lax.rem(t + 1, nt)},
            device_id_type=MESH,
        )

    def own_to_core(self):
        nc, c, nt, t = self.place
        return pltpu.make_async_remote_copy(
            src_ref=self.src,
            dst_ref=self.outs[1].at[c],
            send_sem=self.sems[2].at[c],
            recv_sem=self.sems[3].at[c],
            device_id={"tp": lax.rem(t + 1, nt)},
            device_id_type=MESH,
        )

    def keep(self):
        nc, c = self.place[:2]
        return pltpu.make_async_copy(self.src, self.outs[0].at[c], self.sems[0].at[0, nc - 1])

    def start(self):
        for way in range(2):
            copy, sent = self.copy(way, 0)
            pl.when(sent)(copy.start)
        self.keep().start()
        self.own_to_core().start()

    def pass_on(self):
        nc = self.place[0]
        for k in range(1, nc):
            for way in range(2):
                arrival, there = self.arrival(way, k)
                source = relayed(self.place, way, k)[0]
                copy, sent = self.copy(way, k)

                @pl.when(there)
                def _():
                    arrival.wait_recv()
                    self.to_core(source).start()

                if k < nc - 1:
                    pl.when(sent)(copy.start)

    def finish(self):
        nc, c = self.place[:2]
        self.keep().wait()
        for k in range(nc - 1):
            for way in range(2):
                copy, sent = self.copy(way, k)
                pl.when(sent)(copy.wait_send)
        for source in range(nc):

            @pl.when(c != source)
            def _():
                self.to_core(source).wait()

        self.own_to_core().wait()


class Share:
    both = False

    def __init__(self, lay, array):
        self.lay_sizes, self.array = lay.sizes, array

    def out_shapes(self, nc):
        nt, seqs = self.lay_sizes[2:]
        n, rows, width = self.array.shape
        return [jax.ShapeDtypeStruct((seqs, n, rows, nt * width), self.array.dtype)]

    def scratch(self, nc):
        nf, _, nt, seqs = self.lay_sizes
        return [pltpu.SemaphoreType.DMA((nf,)), pltpu.SemaphoreType.DMA((seqs, nt))]

    def bind(self, place, src, outs, sems):
        load = SharedLoad()
        load.lay_sizes, load.src, load.out, load.sems = self.lay_sizes, src, outs[0], sems
        return load


class SharedLoad:
    def target(self, slot, core):
        width = self.src.shape[-1]
        return self.out.at[slot, :, :, pl.ds(pl.multiple_of(core * width, 128), width)]

    def to_chip(self, k):
        nf, _, nt, seqs = self.lay_sizes
        f, t = lax.axis_index("fsdp"), lax.axis_index("tp")
        own = lax.rem(f, seqs)
        return pltpu.make_async_remote_copy(
            src_ref=self.src,
            dst_ref=self.target(own, t),
            send_sem=self.sems[0].at[k],
            recv_sem=self.sems[1].at[own, t],
            device_id={"fsdp": lax.rem(f + k, nf), "tp": f // seqs},
            device_id_type=MESH,
        )

    def keep(self):
        f, t = lax.axis_index("fsdp"), lax.axis_index("tp")
        own = lax.rem(f, self.lay_sizes[3])
        return pltpu.make_async_copy(self.src, self.target(own, t), self.sems[0].at[0])

    def at_home(self):
        return lax.axis_index("tp") == lax.axis_index("fsdp") // self.lay_sizes[3]

    def start(self):
        for k in range(1, self.lay_sizes[0]):
            self.to_chip(k).start()
        pl.when(self.at_home())(lambda: self.keep().start())
        pl.when(jnp.logical_not(self.at_home()))(lambda: self.to_chip(0).start())

    def pass_on(self):
        pass

    def finish(self):
        nf, _, nt, seqs = self.lay_sizes
        f, t = lax.axis_index("fsdp"), lax.axis_index("tp")
        for i in range(seqs):
            for core in range(nt):
                mine = jnp.logical_and(f == t * seqs + i, t == core)

                @pl.when(jnp.logical_not(mine))
                def _():
                    pltpu.make_async_remote_copy(
                        src_ref=self.target(i, core),
                        dst_ref=self.target(i, core),
                        send_sem=self.sems[0].at[0],
                        recv_sem=self.sems[1].at[i, core],
                        device_id={"fsdp": lax.rem(f + 1, nf)},
                        device_id_type=MESH,
                    ).wait_recv()

        for k in range(1, nf):
            self.to_chip(k).wait_send()
        pl.when(self.at_home())(lambda: self.keep().wait())
        pl.when(jnp.logical_not(self.at_home()))(lambda: self.to_chip(0).wait_send())


class Hauls:
    def __init__(self, lay, hauls):
        self.nc, self.hauls = lay.nc, list(hauls)
        self.operands = [h.array for h in self.hauls]
        self.shapes = [shape for h in self.hauls for shape in h.out_shapes(lay.nc)]
        self.scratch = [sem for h in self.hauls for sem in h.scratch(lay.nc)]
        anywhere = pl.BlockSpec(memory_space=pl.ANY)
        self.in_specs = [anywhere] * len(self.operands)
        self.out_specs = [anywhere] * len(self.shapes)

    def split(self, refs, n_in, n_out):
        more_in, more_out, sems = len(self.operands), len(self.shapes), len(self.scratch)
        ins, refs = refs[:n_in], refs[n_in:]
        srcs, refs = refs[:more_in], refs[more_in:]
        outs, refs = refs[:n_out], refs[n_out:]
        dsts, refs = refs[:more_out], refs[more_out:]
        scratch = refs[: len(refs) - sems]
        refs = refs[len(refs) - sems :]
        c, t = lax.axis_index("ctx"), lax.axis_index("tp")
        place = (self.nc, c, lax.axis_size("tp"), t)
        loads = []
        for haul, src in zip(self.hauls, srcs):
            count, held = len(haul.out_shapes(self.nc)), len(haul.scratch(self.nc))
            loads.append(haul.bind(place, src, dsts[:count], refs[:held]))
            dsts, refs = dsts[count:], refs[held:]
        return ins, outs, scratch, loads


def start_all(loads):
    for load in loads:
        load.start()


def finish_all(loads):
    for load in loads:
        load.pass_on()
    for load in loads:
        load.finish()


def greet(nf, nc, nt, whole_plane=False):
    f, c, t = lax.axis_index("fsdp"), lax.axis_index("ctx"), lax.axis_index("tp")
    barrier = pltpu.get_barrier_semaphore()
    peers = [{"ctx": lax.rem(c + gap, nc)} for gap in range(1, nc)]
    for k in range(nf):
        for u in range(nt):
            if (k, u) != (0, 0) and (k == 0 or u == 0 or whole_plane):
                peers.append({"fsdp": lax.rem(f + k, nf), "tp": lax.rem(t + u, nt)})
    for peer in peers:
        pl.semaphore_signal(barrier, inc=1, device_id=peer, device_id_type=MESH)
    pl.semaphore_wait(barrier, len(peers))


def params(call_id):
    return pltpu.CompilerParams(
        collective_id=call_id, has_side_effects=True, vmem_limit_bytes=VMEM_LIMIT
    )


def opening_body(lay_sizes, experts, hauls, *refs):
    nf, nc, nt, seqs = lay_sizes
    (src, small, later), (out, smalls, mine, stage), sems, loads = hauls.split(refs, 3, 4)
    zsend, zrecv, psend, precv, ssend, srecv, lsend, lrecv, here = sems
    f, c, t = lax.axis_index("fsdp"), lax.axis_index("ctx"), lax.axis_index("tp")
    place = (nc, c, nt, t)
    own = lax.rem(f, seqs)
    home = t == f // seqs
    rows, width = stage.shape[1], mine.shape[2]
    greet(nf, nc, nt, True)

    def half(ref, core):
        return ref.at[pl.ds(pl.multiple_of(core * rows, 16), rows)]

    def relay(way, k):
        source = relayed(place, way, k)[0]
        from_ref = half(src, t) if k == 0 else stage.at[source]
        return relay_step(place, way, k, from_ref, stage.at[source], zsend, zrecv)

    def in_plane(source, k, first):
        return pltpu.make_async_remote_copy(
            src_ref=half(src, t) if first else stage.at[source],
            dst_ref=half(out.at[own, source], t),
            send_sem=psend.at[source, k],
            recv_sem=precv.at[own, source, t],
            device_id={"fsdp": lax.rem(f + k, nf), "tp": f // seqs},
            device_id_type=MESH,
        )

    def keep(source, first):
        from_ref = half(src, t) if first else stage.at[source]
        return pltpu.make_async_copy(from_ref, half(out.at[own, source], t), here.at[source])

    def share(source, first=False):
        for k in range(1, nf):
            in_plane(source, k, first).start()
        pl.when(home)(lambda: keep(source, first).start())
        pl.when(jnp.logical_not(home))(lambda: in_plane(source, 0, first).start())

    def small_along_ctx(j, source):
        return pltpu.make_async_remote_copy(
            src_ref=small,
            dst_ref=smalls.at[source],
            send_sem=ssend.at[j],
            recv_sem=srecv.at[j],
            device_id={"ctx": lax.rem(c + j, nc)},
            device_id_type=MESH,
        )

    def later_along_ctx(j):
        return pltpu.make_async_remote_copy(
            src_ref=later.at[j, :, pl.ds(pl.multiple_of(t * width, 128), width)],
            dst_ref=mine.at[j],
            send_sem=lsend.at[j],
            recv_sem=lrecv.at[j],
            device_id={"ctx": lax.rem(c + (nc // experts) * j, nc)},
            device_id_type=MESH,
        )

    def keep_later():
        src_ref = later.at[0, :, pl.ds(pl.multiple_of(t * width, 128), width)]
        return pltpu.make_async_copy(src_ref, mine.at[0], lsend.at[0])

    for way in range(2):
        copy, sent = relay(way, 0)
        pl.when(sent)(lambda: copy.start())
    for j in range(1, nc):
        small_along_ctx(j, c).start()
    keep_small = pltpu.make_async_copy(small, smalls.at[c], ssend.at[0])
    keep_small.start()
    share(c, True)
    keep_later().start()

    for k in range(1, nc):
        for way in range(2):
            source, there = relayed(place, way, k)

            @pl.when(there)
            def _():
                pltpu.make_async_remote_copy(
                    src_ref=stage.at[source],
                    dst_ref=stage.at[source],
                    send_sem=zsend.at[way, k],
                    recv_sem=zrecv.at[way, k - 1],
                    device_id={"ctx": lax.rem(c + 1, nc)},
                    device_id_type=MESH,
                ).wait_recv()
                if k < nc - 1:
                    copy, sent = relay(way, k)
                    pl.when(sent)(lambda: copy.start())
                share(source)

    start_all(loads)
    for j in range(1, experts):
        later_along_ctx(j).start()

    for i in range(seqs):
        for core in range(nt):
            mine_here = jnp.logical_and(f == t * seqs + i, t == core)

            @pl.when(jnp.logical_not(mine_here))
            def _():
                for source in range(nc):
                    landing = half(out.at[i, source], core)
                    pltpu.make_async_remote_copy(
                        src_ref=landing,
                        dst_ref=landing,
                        send_sem=psend.at[source, 0],
                        recv_sem=precv.at[i, source, core],
                        device_id={"fsdp": lax.rem(f + 1, nf)},
                        device_id_type=MESH,
                    ).wait_recv()

    for j in range(1, nc):
        small_along_ctx(j, lax.rem(c - j + nc, nc)).wait_recv()
        small_along_ctx(j, c).wait_send()
    keep_small.wait()
    keep_later().wait()
    for k in range(nc - 1):
        for way in range(2):
            copy, sent = relay(way, k)
            pl.when(sent)(lambda: copy.wait_send())
    for source in range(nc):
        for k in range(1, nf):
            in_plane(source, k, False).wait_send()
        pl.when(home)(lambda: keep(source, False).wait())
        pl.when(jnp.logical_not(home))(lambda: in_plane(source, 0, False).wait_send())
    for j in range(1, experts):
        later_along_ctx(j).wait()
    finish_all(loads)


def opening(lay, rows, small, later, call_id, hauls):
    count, width = rows.shape
    nf, nc, nt, seqs = lay.sizes
    hauls = Hauls(lay, hauls)
    experts = lay.experts
    dma = pltpu.SemaphoreType.DMA
    anywhere = pl.BlockSpec(memory_space=pl.ANY)
    shapes = [
        jax.ShapeDtypeStruct((seqs, nc, count, width), rows.dtype),
        jax.ShapeDtypeStruct((nc,) + small.shape, small.dtype),
        jax.ShapeDtypeStruct(later.shape[:2] + (later.shape[2] // nt,), later.dtype),
        jax.ShapeDtypeStruct((nc, count // nt, width), rows.dtype),
    ]
    return pl.pallas_call(
        functools.partial(opening_body, lay.sizes, experts, hauls),
        out_shape=shapes + hauls.shapes,
        in_specs=[anywhere] * 3 + hauls.in_specs,
        out_specs=[anywhere] * 4 + hauls.out_specs,
        scratch_shapes=[
            dma((2, nc)),
            dma((2, nc)),
            dma((nc, nf)),
            dma((seqs, nc, nt)),
            dma((nc,)),
            dma((nc,)),
            dma((experts,)),
            dma((experts,)),
            dma((nc,)),
        ]
        + hauls.scratch,
        compiler_params=params(call_id),
        name=f"opening{call_id}",
    )(rows, small, later, *hauls.operands)


def spread_body(lay_sizes, stride, blocks, hauls, *refs):
    nf, nc, nt, seqs = lay_sizes
    (src,), (out,), (zsend, zrecv, psend, precv, here), loads = hauls.split(refs, 1, 1)
    f, c, t = lax.axis_index("fsdp"), lax.axis_index("ctx"), lax.axis_index("tp")
    own = lax.rem(f, seqs)
    home = t == f // seqs
    greet(nf, nc, nt)

    def along_ctx(j):
        return pltpu.make_async_remote_copy(
            src_ref=src.at[j],
            dst_ref=out.at[own, j],
            send_sem=zsend.at[j],
            recv_sem=zrecv.at[j],
            device_id={"ctx": lax.rem(c + stride * j, nc)},
            device_id_type=MESH,
        )

    def in_plane(j, k):
        return pltpu.make_async_remote_copy(
            src_ref=src.at[0] if j == 0 else out.at[own, j],
            dst_ref=out.at[own, j],
            send_sem=psend.at[j, k],
            recv_sem=precv.at[own, j],
            device_id={"fsdp": lax.rem(f + k, nf)},
            device_id_type=MESH,
        )

    keep = pltpu.make_async_copy(src.at[0], out.at[own, 0], here)

    @pl.when(home)
    def _():
        for j in range(1, blocks):
            along_ctx(j).start()
        for k in range(1, nf):
            in_plane(0, k).start()
        keep.start()

    start_all(loads)

    @pl.when(home)
    def _():
        for j in range(1, blocks):
            along_ctx(j).wait_recv()
            for k in range(1, nf):
                in_plane(j, k).start()
        keep.wait()

    for i in range(seqs):

        @pl.when(jnp.logical_not(jnp.logical_and(home, own == i)))
        def _():
            for j in range(blocks):
                pltpu.make_async_remote_copy(
                    src_ref=out.at[i, j],
                    dst_ref=out.at[i, j],
                    send_sem=psend.at[j, 0],
                    recv_sem=precv.at[i, j],
                    device_id={"fsdp": lax.rem(f + 1, nf)},
                    device_id_type=MESH,
                ).wait_recv()

    @pl.when(home)
    def _():
        for j in range(1, blocks):
            along_ctx(j).wait_send()
        for j in range(blocks):
            for k in range(1, nf):
                in_plane(j, k).wait_send()

    finish_all(loads)


def spread(lay, rows, stride, call_id, hauls=()):
    blocks = rows.shape[0]
    hauls = Hauls(lay, hauls)
    dma = pltpu.SemaphoreType.DMA
    anywhere = pl.BlockSpec(memory_space=pl.ANY)
    return pl.pallas_call(
        functools.partial(spread_body, lay.sizes, stride, blocks, hauls),
        out_shape=[jax.ShapeDtypeStruct((lay.seqs,) + rows.shape, rows.dtype)] + hauls.shapes,
        in_specs=[anywhere] + hauls.in_specs,
        out_specs=[anywhere] + hauls.out_specs,
        scratch_shapes=[
            dma((blocks,)),
            dma((blocks,)),
            dma((blocks, lay.nf)),
            dma((lay.seqs, blocks)),
            dma,
        ]
        + hauls.scratch,
        compiler_params=params(call_id),
        name=f"spread{call_id}",
    )(rows, *hauls.operands)


def collect_body(lay_sizes, stride, blocks, by_plane, dims, sets, n_a, n_w, hauls, *refs):
    nf, nc, nt, seqs = lay_sizes
    ins, (out,), scratch, loads = hauls.split(refs, n_a + n_w, 1)
    lefts, rights = ins[:n_a], ins[n_a:]
    part, came, psend, precv, zsend, zrecv = scratch
    f, c, t = lax.axis_index("fsdp"), lax.axis_index("ctx"), lax.axis_index("tp")
    own = lax.rem(f, seqs)
    home = t == f // seqs
    greet(nf, nc, nt)
    start_all(loads)
    wide = part.shape[-1]
    rows = part.shape[-2] // blocks

    def to_chip(n, slot, s):
        chip = t * seqs + slot
        gap = lax.rem(f - chip + nf, nf) - 1
        return pltpu.make_async_remote_copy(
            src_ref=part.at[n, slot, s],
            dst_ref=came.at[n, gap, s],
            send_sem=psend.at[n, slot, s],
            recv_sem=precv.at[n, gap, s],
            device_id={"fsdp": chip},
            device_id_type=MESH,
        )

    def block(j):
        at = lax.rem(c - j + nc, nc) if by_plane else j
        return pl.ds(pl.multiple_of(at * rows, 16), rows)

    def to_owner(n, s, j):
        return pltpu.make_async_remote_copy(
            src_ref=part.at[n, own, s, block(j)],
            dst_ref=out.at[n, j, :, pl.ds(pl.multiple_of(s * wide, wide), wide)],
            send_sem=zsend.at[n, s, j],
            recv_sem=zrecv.at[n, s, j],
            device_id={"ctx": lax.rem(c - stride * j + nc, nc)},
            device_id_type=MESH,
        )

    for n, terms in enumerate(sets):

        @pl.loop(0, seqs * nc)
        def _(i):
            s = lax.rem(i, nc)
            slot = lax.rem(own + 1 + i // nc, seqs)
            acc = None
            for which, lead, first, size, weight, row in terms:
                right = rights[weight][s] if row is None else rights[weight][s, row]
                term = dot(lefts[which][lead, slot, :, first : first + size], right, dims)
                acc = term if acc is None else acc + term
            part[n, slot, s] = acc.astype(BF16)

            @pl.when(t * seqs + slot != f)
            def _():
                to_chip(n, slot, s).start()

    for n in range(len(sets)):

        @pl.when(home)
        def _():
            @pl.loop(0, nc)
            def _(s):
                for r in range(nf - 1):
                    pltpu.make_async_remote_copy(
                        src_ref=came.at[n, r, s],
                        dst_ref=came.at[n, r, s],
                        send_sem=psend.at[n, 0, s],
                        recv_sem=precv.at[n, r, s],
                        device_id={"fsdp": lax.rem(f + 1, nf)},
                        device_id_type=MESH,
                    ).wait_recv()
                for j in reversed(range(blocks)):
                    where = block(j)
                    summed = part[n, own, s, where].astype(F32)
                    for r in range(nf - 1):
                        summed = summed + came[n, r, s, where].astype(F32)
                    if j == 0:
                        out[n, 0, :, pl.ds(pl.multiple_of(s * wide, wide), wide)] = summed.astype(BF16)
                    else:
                        part[n, own, s, where] = summed.astype(BF16)
                        to_owner(n, s, j).start()

    @pl.when(home)
    def _():
        for n in range(len(sets)):
            for s in range(nc):
                for j in range(1, blocks):
                    to_owner(n, s, j).wait()

    @pl.when(jnp.logical_not(home))
    def _():
        out[...] = jnp.zeros_like(out)

    for slot in range(seqs):

        @pl.when(t * seqs + slot != f)
        def _():
            for n in range(len(sets)):
                for s in range(nc):
                    to_chip(n, slot, s).wait_send()

    finish_all(loads)


def collect(lay, lefts, rights, sets, stride, blocks, call_id, dims=NT, hauls=(), by_plane=False):
    seqs, count = lefts[0].shape[1:3]
    nc, wide = rights[0].shape[0], rights[0].shape[-2 if dims == NT else -1]
    rows, width = count // blocks, nc * wide
    held = len(sets) * (seqs + lay.nf) * count * width * 2
    held += sum(a.size for a in lefts) * 9 // 4 + sum(w.size for w in rights) * 2
    if held > VMEM_LIMIT:

        def block_of(terms, j, last):
            at = (lay.c - j) % nc if by_plane else j
            here = [lax.dynamic_slice_in_dim(a, at * rows, rows, 2) for a in lefts]
            if last is not None:
                here = lax.optimization_barrier((here, last))[0]
            partial = 0.0
            for which, lead, first, size, weight, row in terms:
                partial = partial + jnp.einsum(
                    "srh,pdh->srpd" if dims == NT else "srh,phd->srpd",
                    here[which][lead, :, :, first : first + size],
                    rights[weight] if row is None else rights[weight][:, row],
                    preferred_element_type=F32,
                )
            return partial.astype(BF16).reshape(seqs, rows, width)

        sums = [
            collect_permute(lay, functools.partial(block_of, terms), blocks, stride) for terms in sets
        ]
        return [jnp.stack(sums), *haul_alone(lay, hauls, call_id)]
    hauls = Hauls(lay, hauls)
    dma = pltpu.SemaphoreType.DMA
    in_vmem = pl.BlockSpec(memory_space=pltpu.VMEM)
    return pl.pallas_call(
        functools.partial(
            collect_body,
            lay.sizes,
            stride,
            blocks,
            by_plane,
            dims,
            sets,
            len(lefts),
            len(rights),
            hauls,
        ),
        out_shape=[jax.ShapeDtypeStruct((len(sets), blocks, rows, width), BF16)] + hauls.shapes,
        in_specs=[in_vmem] * (len(lefts) + len(rights)) + hauls.in_specs,
        out_specs=[in_vmem] + hauls.out_specs,
        scratch_shapes=[
            pltpu.VMEM((len(sets), seqs, nc, count, wide), BF16),
            pltpu.VMEM((len(sets), lay.nf - 1, nc, count, wide), BF16),
            dma((len(sets), seqs, nc)),
            dma((len(sets), lay.nf - 1, nc)),
            dma((len(sets), nc, blocks)),
            dma((len(sets), nc, blocks)),
        ]
        + hauls.scratch,
        compiler_params=params(call_id),
        name=f"collect{call_id}",
    )(*lefts, *rights, *hauls.operands)


def haul_alone_body(lay_sizes, hauls, *refs):
    nf, nc, nt, seqs = lay_sizes
    loads = hauls.split(refs, 0, 0)[3]
    greet(nf, nc, nt)
    start_all(loads)
    finish_all(loads)


def haul_alone(lay, hauls, call_id):
    if not hauls:
        return []
    hauls = Hauls(lay, hauls)
    return pl.pallas_call(
        functools.partial(haul_alone_body, lay.sizes, hauls),
        out_shape=hauls.shapes,
        in_specs=hauls.in_specs,
        out_specs=hauls.out_specs,
        scratch_shapes=hauls.scratch,
        compiler_params=params(call_id),
        name=f"haul{call_id}",
    )(*hauls.operands)


def finish_body(lay_sizes, hauls, *refs):
    nf, nc, nt, seqs = lay_sizes
    (terms, grad), (sums, grad_out), scratch, loads = hauls.split(refs, 2, 2)
    landed, middle, total, zsend, zrecv, psend, precv, tsend, trecv = scratch
    f, c, t = lax.axis_index("fsdp"), lax.axis_index("ctx"), lax.axis_index("tp")
    home = t == f // seqs
    barrier = pltpu.get_barrier_semaphore()
    others = [(k, u) for k in range(nf) for u in range(nt) if (k, u) != (0, 0)]
    for j in range(1, nc):
        pl.semaphore_signal(
            barrier, inc=1, device_id={"ctx": lax.rem(c + j, nc)}, device_id_type=MESH
        )
    for k, u in others:
        pl.semaphore_signal(
            barrier,
            inc=1,
            device_id={"fsdp": lax.rem(f + k, nf), "tp": lax.rem(t + u, nt)},
            device_id_type=MESH,
        )
    pl.semaphore_wait(barrier, nc - 1 + len(others))

    def along_ctx(j):
        return pltpu.make_async_remote_copy(
            src_ref=terms.at[lax.rem(c + j, nc)],
            dst_ref=middle.at[j],
            send_sem=zsend.at[j],
            recv_sem=zrecv.at[j],
            device_id={"ctx": lax.rem(c + j, nc)},
            device_id_type=MESH,
        )

    def in_plane(k, u):
        chip = lax.rem(f + k, nf)
        return pltpu.make_async_remote_copy(
            src_ref=total.at[chip],
            dst_ref=landed.at[f],
            send_sem=psend.at[k, u],
            recv_sem=precv.at[f],
            device_id={"fsdp": chip, "tp": lax.rem(t + u, nt)},
            device_id_type=MESH,
        )

    def to_core(u):
        return pltpu.make_async_remote_copy(
            src_ref=grad,
            dst_ref=grad_out,
            send_sem=tsend.at[u],
            recv_sem=trecv.at[0],
            device_id={"tp": lax.rem(t + u, nt)},
            device_id_type=MESH,
        )

    @pl.when(home)
    def _():
        for j in range(1, nc):
            along_ctx(j).start()
        for u in range(1, nt):
            to_core(u).start()

    start_all(loads)

    @pl.when(home)
    def _():
        grad_out[...] = grad[...]
        summed = terms[c]
        for j in range(1, nc):
            along_ctx(j).wait_recv()
            summed = summed + middle[j]
        total[...] = summed
        for k, u in others:
            in_plane(k, u).start()
        landed[f] = total[f]

    for chip in range(nf):

        @pl.when(jnp.logical_not(jnp.logical_and(home, f == chip)))
        def _():
            pltpu.make_async_remote_copy(
                src_ref=landed.at[chip],
                dst_ref=landed.at[chip],
                send_sem=psend.at[0, 0],
                recv_sem=precv.at[chip],
                device_id={"fsdp": lax.rem(f + 1, nf)},
                device_id_type=MESH,
            ).wait_recv()

    sums[...] = jnp.sum(landed[...], axis=0)

    @pl.when(home)
    def _():
        for j in range(1, nc):
            along_ctx(j).wait_send()
        for k, u in others:
            in_plane(k, u).wait_send()
        for u in range(1, nt):
            to_core(u).wait_send()

    @pl.when(jnp.logical_not(home))
    def _():
        to_core(1).wait_recv()

    finish_all(loads)


def finish(lay, terms, grad, call_id, hauls=()):
    lines, width = terms.shape
    part = width // (lay.nf * lay.nc)
    terms = terms.reshape(lines, lay.nf, lay.nc, part).transpose(2, 1, 0, 3)
    hauls = Hauls(lay, hauls)
    dma = pltpu.SemaphoreType.DMA
    in_vmem = pl.BlockSpec(memory_space=pltpu.VMEM)
    return pl.pallas_call(
        functools.partial(finish_body, lay.sizes, hauls),
        out_shape=[
            jax.ShapeDtypeStruct((lines, part), F32),
            jax.ShapeDtypeStruct(grad.shape, grad.dtype),
        ]
        + hauls.shapes,
        in_specs=[in_vmem] * 2 + hauls.in_specs,
        out_specs=[in_vmem] * 2 + hauls.out_specs,
        scratch_shapes=[
            pltpu.VMEM((lay.nf, lines, part), F32),
            pltpu.VMEM((lay.nc, lay.nf, lines, part), F32),
            pltpu.VMEM((lay.nf, lines, part), F32),
            dma((lay.nc,)),
            dma((lay.nc,)),
            dma((lay.nf, lay.nt)),
            dma((lay.nf,)),
            dma((lay.nt,)),
            dma((1,)),
        ]
        + hauls.scratch,
        compiler_params=params(call_id),
        name=f"finish{call_id}",
    )(terms, grad, *hauls.operands)


def turn(values, cosine, sine):
    return values * cosine + pltpu.roll(values, DH // 2, axis=1) * sine


def chunk_dot(a_ref, weights, row=None, dims=NN):
    planes, wide = weights.shape[0], weights.shape[-2 if dims == NN else -1]
    acc = None
    for s in range(planes):
        weight = weights[s] if row is None else weights[s, row]
        term = dot(a_ref[:, s * wide : (s + 1) * wide], weight, dims)
        acc = term if acc is None else acc + term
    return acc


def pick_columns(ids, expert, planes, cap):
    count = ids.shape[0]
    rows = count // lax.axis_size("ctx")
    member = jnp.where(jnp.logical_or(ids[:, 0:1] == expert, ids[:, 1:2] == expert), 1.0, 0.0)
    before = lax.broadcasted_iota(jnp.int32, (rows, rows), 1)
    before = (before < lax.broadcasted_iota(jnp.int32, (rows, rows), 0)).astype(BF16)
    places = []
    for plane in range(count // rows):
        here = member[plane * rows : (plane + 1) * rows]
        rank = dot(before, jnp.broadcast_to(here, (rows, DH)).astype(BF16))[:, 0:1]
        first = -1.0
        for n, chosen in enumerate(planes):
            first = jnp.where(chosen == plane, float(n * cap), first)
        places.append(jnp.where(jnp.logical_and(here > 0.5, first >= 0.0), rank + first, -1.0))
    place = jnp.concatenate(places, axis=0)
    columns = lax.broadcasted_iota(jnp.int32, (count, len(planes) * cap), 1).astype(F32)
    return jnp.where(place == columns, 1.0, 0.0)


def attend_body(lay_sizes, rep, hauls, *refs):
    nf, nc, nt, seqs = lay_sizes
    ins, outs, scratch, loads = hauls.split(refs, 10, 8)
    x_ref, ids_ref, small_ref, q0, q1, kv0, kv1, cos_ref, sin_ref, pos_ref = ins
    normed_ref, q_ref, k_ref, v_ref, mixed_ref, put_ref, qpos_ref, other_ref = outs
    c = lax.axis_index("ctx")
    expert = c // rep

    @pl.when(pl.program_id(0) == 0)
    def _():
        greet(nf, nc, nt, True)
        start_all(loads)

    wide = small_ref.shape[-1]
    total = 0.0
    for s in range(nc):
        x = x_ref[0, :, s * wide : (s + 1) * wide].astype(F32)
        total = total + jnp.sum(x * x, axis=-1, keepdims=True)
    inverse = lax.rsqrt(total * (1.0 / (nc * wide)) + EPSILON)
    for s in range(nc):
        columns = slice(s * wide, (s + 1) * wide)
        gain = small_ref[s, 0:1].astype(F32)
        normed_ref[0, :, columns] = (x_ref[0, :, columns].astype(F32) * inverse * gain).astype(BF16)
    normed = normed_ref.at[0]

    cap = qpos_ref.shape[-1] * rep // nc
    planes = [lax.rem(c - rep * j + nc, nc) for j in range(nc // rep)]
    ids = ids_ref[0].astype(F32)
    pick = pick_columns(ids[:, 0:2], expert.astype(F32), planes, cap)
    put_ref[0] = pick.astype(BF16)
    qpos_ref[0] = jnp.sum(pick * pos_ref[...], axis=0, keepdims=True)
    seen = pos_ref[...] <= qpos_ref[0]
    pick_m = pick_columns(ids[:, 2:4], expert.astype(F32), planes, cap).astype(BF16)
    other = jnp.where(ids[:, 2:3] == expert.astype(F32), ids[:, 3:4], ids[:, 2:3])
    other = dot(pick_m, jnp.broadcast_to(other, (other.shape[0], DH)).astype(BF16), TN)
    other_ref[0] = other[:, 0:1]

    cosine, sine = cos_ref[...], sin_ref[...]
    half = q0.shape[-1]
    for side, (query, key_value) in enumerate(((q0, kv0), (q1, kv1))):
        v_ref[0, :, side * half : (side + 1) * half] = chunk_dot(normed, key_value, 1).astype(BF16)
        keys = chunk_dot(normed, key_value, 0)
        queries = chunk_dot(normed, query)
        for h in range(half // DH):
            cols = slice(side * half + h * DH, side * half + (h + 1) * DH)
            here = slice(h * DH, (h + 1) * DH)
            k_ref[0, :, cols] = turn(keys[:, here], cosine, sine).astype(BF16)
            turned = turn(queries[:, here], cosine, sine).astype(BF16)
            q_ref[0, :, cols] = dot(put_ref[0], turned, TN).astype(BF16)
    for h in range(2 * half // DH):
        cols = slice(h * DH, (h + 1) * DH)
        scores = dot(k_ref[0, :, cols], q_ref[0, :, cols], NT) * (1.0 / math.sqrt(DH))
        scores = jnp.where(seen, scores, MASKED)
        powers = jnp.exp(scores - jnp.max(scores, axis=0, keepdims=True))
        probs = (powers / jnp.sum(powers, axis=0, keepdims=True)).astype(BF16)
        mixed_ref[0, :, cols] = dot(probs, v_ref[0, :, cols], TN).astype(BF16)

    @pl.when(pl.program_id(0) == seqs - 1)
    def _():
        finish_all(loads)


def attend(lay, x, small, weights, cosine, sine, pos, cap, call_id, hauls):
    seqs, count = x.shape[:2]
    width = lay.nc * small.shape[-1]
    heads = 2 * weights[0].shape[-1]
    picked = lay.experts * cap
    hauls = Hauls(lay, hauls)
    per_seq = lambda i: (i, 0, 0)
    once = pl.Buffered(1)
    weight_specs = [
        pl.BlockSpec(w.shape, lambda i, n=w.ndim: (0,) * n, pipeline_mode=once) for w in weights
    ]
    results = [
        ((count, width), BF16),
        ((picked, heads), BF16),
        ((count, heads), BF16),
        ((count, heads), BF16),
        ((picked, heads), BF16),
        ((count, picked), BF16),
        ((1, picked), F32),
        ((picked, 1), F32),
    ]
    return pl.pallas_call(
        functools.partial(attend_body, lay.sizes, lay.rep, hauls),
        grid=(seqs,),
        in_specs=[
            pl.BlockSpec((1, count, width), per_seq),
            pl.BlockSpec((1, count, DH), lambda i: (i, 0, width // DH)),
            pl.BlockSpec(small.shape, lambda i: (0, 0, 0)),
            *weight_specs,
            pl.BlockSpec((count, DH), lambda i: (0, 0)),
            pl.BlockSpec((count, DH), lambda i: (0, 0)),
            pl.BlockSpec((count, 1), lambda i: (0, 0)),
        ]
        + hauls.in_specs,
        out_specs=[pl.BlockSpec((1,) + dims, per_seq) for dims, _ in results] + hauls.out_specs,
        out_shape=[jax.ShapeDtypeStruct((seqs,) + dims, kind) for dims, kind in results]
        + hauls.shapes,
        scratch_shapes=hauls.scratch,
        compiler_params=params(call_id),
        name="attend",
    )(x, x, small, *weights, cosine, sine, pos, *hauls.operands)


def experts_body(rep, experts, n_ref, g_ref, small_ref, other_ref, *refs):
    weights, (ge_ref, hidden_ref, gate_ref, up_ref) = refs[:6], refs[6:]
    c = lax.axis_index("ctx")
    lanes = lax.broadcasted_iota(jnp.int32, (1, small_ref.shape[0]), 1) - (2 + experts)
    logits = dot(n_ref[0], small_ref[...], NT)
    mine = jnp.sum(jnp.where(lanes == c // rep, logits, 0.0), axis=-1, keepdims=True)
    theirs = jnp.where(lanes.astype(F32) == other_ref[0], logits, 0.0)
    theirs = jnp.sum(theirs, axis=-1, keepdims=True)
    ge_ref[0] = (jax.nn.sigmoid(mine - theirs) * g_ref[0].astype(F32)).astype(BF16)
    for side in range(2):
        gate_weight, up_weight, down_weight = weights[side::2]
        gate_pre = chunk_dot(n_ref.at[0], gate_weight, None, NT)
        up_pre = chunk_dot(n_ref.at[0], up_weight, None, NT)
        grad_hidden = chunk_dot(ge_ref.at[0], down_weight, None, NT)
        sigmoid_gate = jax.nn.sigmoid(gate_pre)
        silu_gate = gate_pre * sigmoid_gate
        hidden_ref[side, 0] = (silu_gate * up_pre).astype(BF16)
        silu_slope = sigmoid_gate + silu_gate * (1.0 - sigmoid_gate)
        gate_ref[side, 0] = (grad_hidden * up_pre * silu_slope).astype(BF16)
        up_ref[side, 0] = (grad_hidden * silu_gate).astype(BF16)


def experts_apply(lay, n2, g, small, other, *weights):
    seqs, count, width = n2.shape
    ff = weights[0].shape[-2]
    per_seq = lambda i: (i, 0, 0)
    once = pl.Buffered(1)
    wide = pl.BlockSpec((2, 1, count, ff), lambda i: (0, i, 0, 0))
    return pl.pallas_call(
        functools.partial(experts_body, lay.rep, lay.experts),
        grid=(seqs,),
        in_specs=[
            pl.BlockSpec((1, count, width), per_seq),
            pl.BlockSpec((1, count, width), per_seq),
            pl.BlockSpec(small.shape, lambda i: (0, 0)),
            pl.BlockSpec((1, count, 1), per_seq),
        ]
        + [pl.BlockSpec(w.shape, lambda i: (0, 0, 0), pipeline_mode=once) for w in weights],
        out_specs=[pl.BlockSpec((1, count, width), per_seq), wide, wide, wide],
        out_shape=[jax.ShapeDtypeStruct(n2.shape, BF16)]
        + [jax.ShapeDtypeStruct((2, seqs, count, ff), BF16)] * 3,
        compiler_params=pltpu.CompilerParams(vmem_limit_bytes=VMEM_LIMIT),
        name="experts",
    )(n2, g, small, other, *weights)


def core_exchange(refs, nt):
    away, came, send_sem, recv_sem = refs

    def copy(s):
        return pltpu.make_async_remote_copy(
            src_ref=away.at[s],
            dst_ref=came.at[s],
            send_sem=send_sem.at[s],
            recv_sem=recv_sem.at[s],
            device_id={"tp": lax.rem(lax.axis_index("tp") + 1, nt)},
            device_id_type=MESH,
        )

    return copy


def greet_core(nt):
    barrier = pltpu.get_barrier_semaphore()
    other = lax.rem(lax.axis_index("tp") + 1, nt)
    pl.semaphore_signal(barrier, inc=1, device_id={"tp": other}, device_id_type=MESH)
    pl.semaphore_wait(barrier, 1)


def mlp_grads_body(nc, nt, n_ref, ge_ref, hidden_ref, gate_ref, up_ref, *refs):
    outs, (away, came) = refs[:5], refs[5:7]
    copy = core_exchange(refs[5:], nt)
    wide = away.shape[-1]
    half = outs[1].shape[1]
    pairs = ((gate_ref, n_ref), (up_ref, n_ref), (hidden_ref, ge_ref))
    greet_core(nt)

    @pl.loop(0, nc)
    def _(s):
        columns = pl.ds(pl.multiple_of(s * wide, wide), wide)
        for i, (left, right) in enumerate(pairs):
            away[s, i] = dot(left[1], right[:, columns], TN).astype(BF16)
        copy(s).start()

    @pl.loop(0, nc)
    def _(s):
        columns = pl.ds(pl.multiple_of(s * wide, wide), wide)
        copy(s).wait_recv()
        for i, (left, right) in enumerate(pairs):
            own = dot(left[0], right[:, columns], TN)
            grad = (own + came[s, i].astype(F32)).astype(BF16)
            if i == 0:
                outs[0][s] = grad
            else:
                outs[2 * i - 1][s] = grad[:half]
                outs[2 * i][s] = grad[half:]

    @pl.loop(0, nc)
    def _(s):
        copy(s).wait_send()


def mlp_grads(lay, n2, ge, hidden, gate, up, call_id):
    width, ff, nc = n2.shape[1], hidden.shape[-1], lay.nc
    piece = (3, ff, width // nc)
    in_vmem = pl.BlockSpec(memory_space=pltpu.VMEM)
    whole = jax.ShapeDtypeStruct((nc, ff, width // nc), BF16)
    half = jax.ShapeDtypeStruct((nc, ff // 2, width // nc), BF16)
    return pl.pallas_call(
        functools.partial(mlp_grads_body, nc, lay.nt),
        in_specs=[in_vmem] * 5,
        out_specs=[in_vmem] * 5,
        out_shape=[whole] + [half] * 4,
        scratch_shapes=[
            pltpu.VMEM((nc,) + piece, BF16),
            pltpu.VMEM((nc,) + piece, BF16),
            pltpu.SemaphoreType.DMA((nc,)),
            pltpu.SemaphoreType.DMA((nc,)),
        ],
        compiler_params=params(call_id),
        name="mlp_grads",
    )(n2, ge, hidden, gate, up)


def attn_grads_body(lay_sizes, hauls, *refs):
    nf, nc, nt, seqs = lay_sizes
    (x_ref, d_ref, g_ref, mixed_ref), outs, scratch, loads = hauls.split(refs, 4, 4)
    kept, away, came = scratch[:3]
    copy = core_exchange(scratch[1:], nt)
    wide, half = away.shape[-2:]
    greet(nf, nc, nt)
    start_all(loads)

    @pl.loop(0, nc)
    def _(s):
        columns = pl.ds(pl.multiple_of(s * wide, wide), wide)
        first = dot(x_ref[:, columns], d_ref[...], TN)
        last = dot(g_ref[:, columns], mixed_ref[...], TN)
        for i in range(4):
            part, at = (first, i) if i < 3 else (last, 0)
            step = 3 if i < 3 else 1
            kept[s, i] = part[:, at * half : (at + 1) * half]
            away[s, i] = part[:, (step + at) * half : (step + at + 1) * half].astype(BF16)
        copy(s).start()

    @pl.loop(0, nc)
    def _(s):
        copy(s).wait_recv()
        for i in range(4):
            outs[i][s] = (kept[s, i] + came[s, i].astype(F32)).astype(BF16)

    @pl.loop(0, nc)
    def _(s):
        copy(s).wait_send()

    finish_all(loads)


def attn_grads(lay, x, grads, g, mixed, call_id, hauls):
    width, heads, nc = x.shape[1], mixed.shape[-1], lay.nc
    piece = (width // nc, heads // 2)
    hauls = Hauls(lay, hauls)
    in_vmem = pl.BlockSpec(memory_space=pltpu.VMEM)
    return pl.pallas_call(
        functools.partial(attn_grads_body, lay.sizes, hauls),
        in_specs=[in_vmem] * 4 + hauls.in_specs,
        out_specs=[in_vmem] * 4 + hauls.out_specs,
        out_shape=[jax.ShapeDtypeStruct((nc,) + piece, BF16)] * 4 + hauls.shapes,
        scratch_shapes=[
            pltpu.VMEM((nc, 4) + piece, F32),
            pltpu.VMEM((nc, 4) + piece, BF16),
            pltpu.VMEM((nc, 4) + piece, BF16),
            pltpu.SemaphoreType.DMA((nc,)),
            pltpu.SemaphoreType.DMA((nc,)),
        ]
        + hauls.scratch,
        compiler_params=params(call_id),
        name="attn_grads",
    )(x, grads, g, mixed, *hauls.operands)


def attend_back_body(lay_sizes, hauls, *refs):
    nf, nc, nt, seqs = lay_sizes
    ins, (out_ref,), scratch, loads = hauls.split(refs, 11, 1)
    q_ref, k_ref, v_ref, g_ref, wo0, wo1, qpos_ref, kpos_ref, cosine, sine, put = ins

    @pl.when(pl.program_id(0) == 0)
    def _():
        greet(nf, nc, nt)
        start_all(loads)

    scale = 1.0 / math.sqrt(DH)
    seen = kpos_ref[...] <= qpos_ref[0]
    half = wo0.shape[-1]
    for side, weight in enumerate((wo0, wo1)):
        grad_mixed = chunk_dot(g_ref.at[0], weight).astype(BF16)
        for h in range(half // DH):
            cols = slice(side * half + h * DH, side * half + (h + 1) * DH)
            q, k, v = q_ref[0, :, cols], k_ref[0, :, cols], v_ref[0, :, cols]
            g = grad_mixed[:, h * DH : (h + 1) * DH]
            scores = jnp.where(seen, dot(k, q, NT) * scale, MASKED)
            powers = jnp.exp(scores - jnp.max(scores, axis=0, keepdims=True))
            probs = powers / jnp.sum(powers, axis=0, keepdims=True)
            grad_probs = dot(v, g, NT)
            centre = jnp.sum(probs * grad_probs, axis=0, keepdims=True)
            grad_scores = (probs * (grad_probs - centre)).astype(BF16)

            def at(part):
                first = (3 * side + part) * half + h * DH
                return slice(first, first + DH)

            out_ref[0, :, at(2)] = dot(probs.astype(BF16), g).astype(BF16)
            dk = dot(grad_scores, q) * scale
            out_ref[0, :, at(1)] = turn(dk, cosine[...], -sine[...]).astype(BF16)
            dq = dot(grad_scores, k, TN) * scale
            high = dq.astype(BF16)
            low = (dq - high.astype(F32)).astype(BF16)
            dq = dot(put[0], high) + dot(put[0], low)
            out_ref[0, :, at(0)] = turn(dq, cosine[...], -sine[...]).astype(BF16)

    @pl.when(pl.program_id(0) == seqs - 1)
    def _():
        finish_all(loads)


def attend_back(lay, q, k, v, g, weights, qpos, kpos, cosine, sine, put, call_id, hauls):
    seqs, count, heads = q.shape
    width = g.shape[-1]
    length = k.shape[1]
    hauls = Hauls(lay, hauls)
    per_seq = lambda s: (s, 0, 0)
    once = lambda s: (0, 0)
    return pl.pallas_call(
        functools.partial(attend_back_body, lay.sizes, hauls),
        grid=(seqs,),
        in_specs=[
            pl.BlockSpec((1, count, heads), per_seq),
            pl.BlockSpec((1, length, heads), per_seq),
            pl.BlockSpec((1, length, heads), per_seq),
            pl.BlockSpec((1, count, width), per_seq),
            pl.BlockSpec(weights[0].shape, lambda s: (0, 0, 0)),
            pl.BlockSpec(weights[1].shape, lambda s: (0, 0, 0)),
            pl.BlockSpec((1, 1, count), per_seq),
            pl.BlockSpec((length, 1), once),
            pl.BlockSpec((length, DH), once),
            pl.BlockSpec((length, DH), once),
            pl.BlockSpec((1, length, count), per_seq),
        ]
        + hauls.in_specs,
        out_specs=[pl.BlockSpec((1, length, 3 * heads), per_seq)] + hauls.out_specs,
        out_shape=[jax.ShapeDtypeStruct((seqs, length, 3 * heads), BF16)] + hauls.shapes,
        scratch_shapes=hauls.scratch,
        compiler_params=params(call_id),
        name="attend_back",
    )(q, k, v, g, *weights, qpos, kpos, cosine, sine, put, *hauls.operands)


def unpack_body(gate, up_a, up_b, down_a, down_b, gate_up, down):
    half = up_a.shape[1]

    def total(ref):
        return jnp.sum(ref[...].astype(F32), axis=0)

    gate_up[0, 0] = total(gate)
    gate_up[0, 1, 0:half] = total(up_a)
    gate_up[0, 1, half:] = total(up_b)
    down[0, 0:half] = total(down_a)
    down[0, half:] = total(down_b)


def unpack(lay, *parts):
    ff, wide = parts[0].shape[1:]
    experts, rep = lay.experts, lay.rep
    return pl.pallas_call(
        unpack_body,
        grid=(experts,),
        in_specs=[pl.BlockSpec((rep,) + p.shape[1:], lambda e: (e, 0, 0)) for p in parts],
        out_specs=[
            pl.BlockSpec((1, 2, ff, wide), lambda e: (e, 0, 0, 0)),
            pl.BlockSpec((1, ff, wide), lambda e: (e, 0, 0)),
        ],
        out_shape=[
            jax.ShapeDtypeStruct((experts, 2, ff, wide), F32),
            jax.ShapeDtypeStruct((experts, ff, wide), F32),
        ],
        compiler_params=pltpu.CompilerParams(vmem_limit_bytes=VMEM_LIMIT),
        name="unpack",
    )(*parts)


def ranks_of(member):
    count = member.shape[-1]
    before = (jnp.arange(count)[:, None] < jnp.arange(count)[None, :]).astype(BF16)
    return jnp.einsum("...m,mn->...n", member.astype(BF16), before, preferred_element_type=F32)


def pick_maps(ids, expert, cap):
    member = jnp.any(ids == expert[..., None, None], axis=-1)
    rank = ranks_of(member).astype(jnp.int32)
    place = jnp.arange(cap, dtype=jnp.int32)[:, None]
    return jnp.logical_and(member[..., None, :], rank[..., None, :] == place)


def choose_maps(pick, ids, expert):
    chosen = ids.T[:, None, :] == expert[None, :, None]
    maps = jnp.logical_and(pick[None], chosen[:, :, None, :])
    slots, experts, cap, rows = maps.shape
    return maps.transpose(0, 3, 1, 2).reshape(slots, rows, experts * cap).astype(BF16)


def chosen_gates(normed, router, expert_ids, experts):
    logits = jnp.dot(normed, router, preferred_element_type=F32)
    onehot = (expert_ids[:, :, None] == jnp.arange(experts, dtype=jnp.int32)).astype(F32)
    picked = jnp.sum(onehot * logits[:, None, :], axis=-1)
    return jax.nn.softmax(picked, axis=-1), onehot


def router_back(gates, grad_gates, onehot):
    inner = gates * (grad_gates - jnp.sum(gates * grad_gates, axis=-1, keepdims=True))
    return jnp.sum(onehot * inner[:, :, None], axis=1)


def per_device(
    tokens,
    cotangent,
    attn_ids,
    mlp_ids,
    span_ids,
    attn_gain,
    attn_router,
    kv_weight,
    query_weight,
    output_weight,
    mlp_gain,
    mlp_router,
    gate_up_weight,
    down_weight,
):
    experts = query_weight.shape[0]
    lay = Layout(experts)
    nf, nc, rep, seqs = lay.nf, lay.nc, lay.rep, lay.seqs
    rows, width = tokens.shape
    cap = 3 * rows // 4
    expert = lay.c // rep

    def to_planes(array, index_of, both=False):
        index = index_of(0)
        shape = array.shape[len(index) :]
        return Haul(array, lambda ref, d: ref.at[index_of(d)] if index else ref, shape, both)

    expert_of = (expert + jnp.arange(experts)) % experts
    pick_own_m = pick_maps(jnp.broadcast_to(mlp_ids, (experts, rows, 2)), expert_of, cap)

    def dispatch(pick, values):
        return jnp.einsum(
            "jrn,nd->jrd", pick.astype(BF16), values, preferred_element_type=F32
        ).astype(BF16)

    ids = jnp.concatenate([attn_ids, mlp_ids], axis=1).astype(BF16)
    payload = jnp.concatenate([tokens, jnp.pad(ids, ((0, 0), (0, 124)))], axis=1)
    small = jnp.concatenate([attn_gain[None], mlp_gain[None], attn_router.T, mlp_router.T])
    small = jnp.pad(small, ((0, -small.shape[0] % 16), (0, 0)))
    g_own = dispatch(pick_own_m, cotangent)
    by_plane = lambda *more: lambda d: (d // rep,) + more
    x_all, small_all, g_mine, _, q_own, q_sib, kv_own, kv_sib = opening(
        lay,
        payload,
        small,
        g_own,
        1,
        [to_planes(query_weight, by_plane(), True), Relay(kv_weight)],
    )
    smalls = small_all.transpose(1, 0, 2).reshape(-1, width)
    gain_one, gain_two = smalls[0:1].astype(F32), smalls[1:2].astype(F32)
    router_one = smalls[2 : 2 + experts].T
    router_two = smalls[2 + experts : 2 + 2 * experts].T

    gate_up_turned = gate_up_weight.swapaxes(-1, -2)
    down_turned = down_weight.swapaxes(-1, -2)

    pick_own_a = pick_maps(jnp.broadcast_to(attn_ids, (experts, rows, 2)), expert_of, cap)
    choose_a = choose_maps(pick_own_a, attn_ids, expert_of)
    choose_m = choose_maps(pick_own_m, mlp_ids, expert_of)

    def by_slot(choose, values):
        flat = values.reshape(-1, values.shape[-1])
        return jnp.einsum("knr,rd->knd", choose, flat, preferred_element_type=F32)

    half_len = rows // 2
    offsets = jnp.arange(rows, dtype=jnp.int32)
    pos = jnp.where(
        offsets[None, :] < half_len,
        span_ids[:, 0:1] * half_len + offsets[None, :],
        span_ids[:, 1:2] * half_len + offsets[None, :] - half_len,
    )
    pos = pos.astype(F32).reshape(-1, 1)
    freqs = ROPE_BASE ** (-jnp.arange(DH // 2, dtype=F32) / (DH // 2))

    cosine, sine = jnp.cos(pos * freqs), jnp.sin(pos * freqs)
    cosine = jnp.concatenate([cosine, cosine], axis=-1)
    sine = jnp.concatenate([-sine, sine], axis=-1)

    inputs = tokens.astype(F32)
    inverse_one = lax.rsqrt(jnp.mean(inputs * inputs, axis=-1, keepdims=True) + EPSILON)
    scaled_one = inputs * inverse_one
    normed_one = (scaled_one * gain_one).astype(BF16)
    attn_gates, attn_hot = chosen_gates(normed_one, router_one, attn_ids, experts)

    normed_all, q, k, v, mixed, put, pos_q, other, o_own, o_sib, gate_own, gate_sib, g_blocks = attend(
        lay,
        x_all.reshape(seqs, nc * rows, -1),
        small_all,
        [q_own, q_sib, kv_own, kv_sib],
        cosine,
        sine,
        pos,
        cap,
        9,
        [
            to_planes(output_weight, by_plane(), True),
            to_planes(gate_up_turned, by_plane(0), True),
            Share(lay, g_mine),
        ],
    )
    g_blocks = g_blocks.reshape(seqs, experts * cap, width)
    heads = q.shape[-1]
    half = heads // 2
    branch_rows, up_own, up_sib = collect(
        lay,
        [mixed[None]],
        [o_own, o_sib],
        [((0, 0, 0, half, 0, None), (0, 0, half, half, 1, None))],
        rep,
        experts,
        2,
        hauls=[to_planes(gate_up_turned, by_plane(1), True)],
    )
    branch = by_slot(choose_a, branch_rows[0])
    residual = inputs + jnp.sum(attn_gates.T[:, :, None] * branch, axis=0)
    inverse_two = lax.rsqrt(jnp.mean(residual * residual, axis=-1, keepdims=True) + EPSILON)
    scaled_two = residual * inverse_two
    normed_two = (scaled_two * gain_two).astype(BF16)
    mlp_gates, mlp_hot = chosen_gates(normed_two, router_two, mlp_ids, experts)

    n2, down_own, down_sib = spread(
        lay,
        dispatch(pick_own_m, normed_two),
        rep,
        3,
        [to_planes(down_turned, by_plane(), True)],
    )
    n2 = n2.reshape(seqs, experts * cap, width)
    grad_expert, hidden, grad_gate, grad_up = experts_apply(
        lay,
        n2,
        g_blocks,
        smalls,
        other,
        gate_own,
        gate_sib,
        up_own,
        up_sib,
        down_own,
        down_sib,
    )
    ff = hidden.shape[-1]
    gate_grads, up_a, up_b, down_a, down_b = mlp_grads(
        lay,
        n2.reshape(-1, width),
        grad_expert.reshape(-1, width),
        *(a.reshape(2, -1, ff) for a in (hidden, grad_gate, grad_up)),
        4,
    )
    by_piece = lambda d: (d,)
    back_rows, gate_back = collect(
        lay,
        [hidden, grad_gate, grad_up],
        [gate_own, up_own, down_own, gate_sib, up_sib, down_sib],
        [
            tuple((0, side, 0, ff, 3 * side + 2, None) for side in range(2)),
            tuple((1 + i, side, 0, ff, 3 * side + i, None) for side in range(2) for i in range(2)),
        ],
        rep,
        experts,
        5,
        NN,
        [to_planes(gate_grads, by_piece)],
    )
    expert_rows, grad_rows = back_rows[0], back_rows[1]
    expert_out = by_slot(choose_m, expert_rows)
    layer_out = residual + jnp.sum(mlp_gates.T[:, :, None] * expert_out, axis=0)
    layer_out = layer_out.astype(BF16)
    upstream = cotangent.astype(F32)
    grad_choice_m = jnp.sum(upstream[None] * expert_out, axis=-1).T
    grad_logits_two = router_back(mlp_gates, grad_choice_m, mlp_hot)
    grad_normed_two = jnp.sum(by_slot(choose_m, grad_rows), axis=0) + jnp.dot(
        grad_logits_two, router_two.astype(F32).T, precision=HIGH
    )
    grad_scaled_two = grad_normed_two * gain_two
    grad_residual = upstream + inverse_two * (
        grad_scaled_two
        - scaled_two * jnp.mean(grad_scaled_two * scaled_two, axis=-1, keepdims=True)
    )

    gate_rows_a = jnp.zeros((experts, rows), F32)
    for slot in range(2):
        gate_rows_a = gate_rows_a + jnp.where(
            attn_ids[None, :, slot] == expert_of[:, None], attn_gates[None, :, slot], 0.0
        )
    grad_branch_own = jnp.einsum(
        "jrn,jnd->jrd",
        pick_own_a.astype(BF16),
        (gate_rows_a[:, :, None] * grad_residual[None]).astype(BF16),
        preferred_element_type=F32,
    ).astype(BF16)
    gb, up_a = spread(lay, grad_branch_own, rep, 6, [to_planes(up_a, by_piece)])
    gb = gb.reshape(seqs, experts * cap, width)
    dqkv, up_b = attend_back(
        lay,
        q,
        k,
        v,
        gb,
        [o_own, o_sib],
        pos_q,
        pos,
        cosine,
        sine,
        put,
        11,
        [to_planes(up_b, by_piece)],
    )
    q_grads, k_grads, v_grads, o_grads, down_a = attn_grads(
        lay,
        normed_all.reshape(-1, width),
        dqkv.reshape(-1, 3 * heads),
        gb.reshape(-1, width),
        mixed.reshape(-1, heads),
        10,
        [to_planes(down_a, by_piece)],
    )
    grad_one_rows, down_b, o_back = collect(
        lay,
        [dqkv[None]],
        [q_own, kv_own, q_sib, kv_sib],
        [
            tuple(
                (0, 0, (3 * s + i) * half, half, 2 * s + (i > 0), None if i == 0 else i - 1)
                for i in range(3)
                for s in range(2)
            )
        ],
        1,
        nc,
        7,
        hauls=[to_planes(down_b, by_piece), to_planes(o_grads, by_piece)],
        by_plane=True,
    )

    grad_choice_a = jnp.sum(grad_residual[None] * branch, axis=-1).T
    grad_logits_one = router_back(attn_gates, grad_choice_a, attn_hot)
    grad_normed_one = jnp.sum(grad_one_rows[0].astype(F32), axis=0) + jnp.dot(
        grad_logits_one, router_one.astype(F32).T, precision=HIGH
    )
    grad_scaled_one = grad_normed_one * gain_one
    grad_tokens = grad_residual + inverse_one * (
        grad_scaled_one
        - scaled_one * jnp.mean(grad_scaled_one * scaled_one, axis=-1, keepdims=True)
    )
    grad_tokens = grad_tokens.astype(BF16)
    terms = jnp.concatenate(
        [
            jnp.sum(grad_normed_one * scaled_one, axis=0)[None],
            jnp.sum(grad_normed_two * scaled_two, axis=0)[None],
            jnp.dot(grad_logits_one.T, normed_one.astype(F32), precision=HIGH),
            jnp.dot(grad_logits_two.T, normed_two.astype(F32), precision=HIGH),
        ]
    )
    terms = jnp.pad(terms, ((0, -terms.shape[0] % 8), (0, 0)))
    terms, both_out, q_back, k_back, v_back = finish(
        lay,
        terms,
        jnp.stack([layer_out, grad_tokens]),
        8,
        [to_planes(grads, by_piece) for grads in (q_grads, k_grads, v_grads)],
    )
    layer_out, grad_tokens = both_out[0], both_out[1]

    def by_expert(came):
        out = came.astype(F32)
        if rep > 1:
            out = jnp.sum(out.reshape((experts, rep) + out.shape[1:]), axis=1)
        return out

    grad_query_weight, grad_output_weight = by_expert(q_back), by_expert(o_back)
    grad_kv_weight = jnp.stack([jnp.sum(g.astype(F32), axis=0) for g in (k_back, v_back)])
    grad_gate_up, grad_down = unpack(lay, gate_back, up_a, up_b, down_a, down_b)
    grad_gate_up, grad_down = grad_gate_up.swapaxes(-1, -2), grad_down.swapaxes(-1, -2)
    return (
        layer_out,
        grad_tokens,
        terms[0],
        terms[2 : 2 + experts].T,
        grad_kv_weight,
        grad_query_weight,
        grad_output_weight,
        terms[1],
        terms[2 + experts : 2 + 2 * experts].T,
        grad_gate_up,
        grad_down,
    )


def solution(mesh):
    placed = (
        P(("fsdp", "ctx"), None),
        P(("fsdp", "ctx"), None),
        P(("fsdp", "ctx"), None),
        P(("fsdp", "ctx"), None),
        P(),
        P("ctx"),
        P("ctx", None),
        P(None, "ctx", ("fsdp", "tp")),
        P(None, "ctx", ("fsdp", "tp")),
        P(None, "ctx", ("fsdp", "tp")),
        P("ctx"),
        P("ctx", None),
        P(None, None, "ctx", ("fsdp", "tp")),
        P(None, "ctx", ("fsdp", "tp")),
    )
    return jax.shard_map(
        per_device,
        mesh=mesh,
        in_specs=placed,
        out_specs=(
            P(("fsdp", "ctx"), None),
            P(("fsdp", "ctx"), None),
            P(("fsdp", "ctx")),
            P(("fsdp", "ctx"), None),
            P(None, "ctx", ("fsdp", "tp")),
            P(None, "ctx", ("fsdp", "tp")),
            P(None, "ctx", ("fsdp", "tp")),
            P(("fsdp", "ctx")),
            P(("fsdp", "ctx"), None),
            P(None, None, "ctx", ("fsdp", "tp")),
            P(None, "ctx", ("fsdp", "tp")),
        ),
        check_vma=False,
    )
```

time: 2660 us -> 1030 us (0.39)
  waiting for transfers between devices: 1610 us -> 0 us
  Pallas kernels: 0 us -> 967 us
  local copies, waits for them, and re-layouts: 403 us -> 13 us
  matrix products: 316 us -> 21.6 us
  other arithmetic: 225 us -> 19.8 us
  blocking collectives: 73.8 us -> 0 us
    pallas_call x0 -> x13, Pallas kernels: none -> 967 us  [the longest x3 363 us: collect(): pl.pallas_call(functools.partial(collect_body, lay.sizes, stride, blocks,...]
    reduce_scatter x11 -> x0, waiting for transfers between devices: 854 us -> none  [the longest x5 713 us: reduce_weights(): lax.psum_scatter(term_fn(jnp.int32(0), shard_rows * lax.axis_size('ctx'))...]
    all_gather x10 -> x0, waiting for transfers between devices: 699 us -> none  [the longest x1 357 us: per_device(): lax.all_gather(sharded[3], 'ctx', axis=2, tiled=True)]
    dot_general x92 -> x14, matrix products: 316 us -> 21.6 us  [the longest x3 9.52 us: by_slot(): return jnp.einsum('knr,rd->knd', choose, flat, preferred_element_type=F32)]
    gather x15 -> x0, local copies, waits for them, and re-layouts: 193 us -> none  [the longest x7 87.4 us: from_blocks(): return blocks.reshape(-1, blocks.shape[-1])[flat_slot]]
    reduce_sum x15 -> x5, other arithmetic: 105 us -> 6.56 us  [the longest x1 2.84 us: per_device(): jnp.sum(grad_one_rows[0].astype(F32), axis=0)]
    all_gather x6 -> x0, blocking collectives: 68.9 us -> none  [the longest x1 14.8 us: per_device(): lax.all_gather(sharded[5], 'ctx', axis=0, tiled=True)]
    reshape x7 -> x3, local copies, waits for them, and re-layouts: 68.3 us -> 1.43 us  [the longest x2 0.8 us: finish(): terms = terms.reshape(lines, lay.nf, lay.nc, part).transpose(2, 1, 0, 3)]
  transfers between devices with their start and end apart: 26 -> 0, of which waited for: 19 -> 0; matrix products, arithmetic and copies ran while one was open for 24% -> 0% of each run, Pallas kernels for 0% -> 0%
where the time goes in v1:
time: 1030 us; the launch traced here: 1020 us
  Pallas kernels  967 us (94%)
  matrix products  21.6 us (2%)
  other arithmetic  19.8 us (2%)
  local copies, waits for them, and re-layouts  13 us (1%)
    pallas_call x3, Pallas kernels, collect(): pl.pallas_call(functools.partial(collect_body, lay.sizes, stride, blocks,...  363 us
    pallas_call x2, Pallas kernels, spread(): pl.pallas_call(functools.partial(spread_body, lay.sizes, stride, blocks,...  163 us
    pallas_call x1, Pallas kernels, opening(): pl.pallas_call(functools.partial(opening_body, lay.sizes, experts, hauls)...  113 us
    pallas_call x1, Pallas kernels, attend(): pl.pallas_call(functools.partial(attend_body, lay.sizes, lay.rep, hauls),...  93.5 us
    pallas_call x1, Pallas kernels, finish(): pl.pallas_call(functools.partial(finish_body, lay.sizes, hauls), out_shap...  72.8 us
    pallas_call x1, Pallas kernels, attend_back(): pl.pallas_call(functools.partial(attend_back_body, lay.sizes, hauls), gri...  45.9 us
    pallas_call x1, Pallas kernels, attn_grads(): pl.pallas_call(functools.partial(attn_grads_body, lay.sizes, hauls), in_s...  37.1 us
    pallas_call x1, Pallas kernels, experts_apply(): pl.pallas_call(functools.partial(experts_body, lay.rep, lay.experts), gri...  35.5 us

profile of v1, /device:TPU:0, one launch (start us, length us, event | category | flops | bytes accessed | tf_op | source)
XLA Modules:
  0.0 1023.2 jit_solution(17309364560086088299)
XLA Ops:
  1.6 3.4 convolution_convert_fusion.1.refs_2_
  6.9 112.8 %opening1.1 = (bf16[2,4,192,2176]{3,2,1,0:T(8,128)(2,1)}, bf16[4,16,512]{2,1,0:T(8,128)(2,1)}, bf16[4,144,1024]{2,1,0:T(8,128)(2,1)}, bf16[4,96,2176]{2,1,0:T(8,...) custom-call(bf16[192,2176]{1,0:T(8,128)(2,1)} %fusion.17.refs_0_, ...), custom_call_target="tpu_custom_call" | custom-call | tf_op jit(solution)/shard_map/opening1/pallas_call | solution.py:575
  119.9 1.5 fusion.39
  121.4 1.2 pad_maximum_fusion.2
  123.6 93.5 %attend.1 = (bf16[2,768,2048]{2,1,0:T(8,128)(2,1)}, bf16[2,576,512]{2,1,0:T(8,128)(2,1)}, bf16[2,768,512]{2,1,0:T(8,128)(2,1)}, bf16[2,768,512]{2,1,0:T(8,128)(2...) custom-call(bf16[2,768,2176]{2,1,0:T(8,128)(2,1)} %bitcast.118, ...), custom_call_target="tpu_custom_call" | custom-call | tf_op jit(solution)/shard_map/attend/pallas_call | solution.py:1133
  217.1 112.7 %collect2.1 = (bf16[1,4,144,2048]{3,2,1,0:T(8,128)(2,1)}, bf16[4,704,512]{2,1,0:T(8,128)(2,1)}, bf16[4,704,512]{2,1,0:T(8,128)(2,1)}) custom-call(bf16[1,2,576,512]{3,2,1,0:T(8,128)(2,1)} %bitcast.132, bf16[4,512,256]{2,1,0:T(8,128)(2,1)} %get-tuple-element.78.refs_1_.refs_4_, bf16[4,512,256]{2,1,0:T(8,128)(2,1)} %get-tuple-element.79.refs_2_.refs_5_, ...), custom_call_target="tpu_custom_call" | custom-call | tf_op jit(solution)/shard_map/collect2/pallas_call | solution.py:827
  331.3 5.0 multiply_reduce_fusion.3
  336.9 2.2 convolution_convert_fusion.refs_0_
  339.1 88.8 %spread3.1 = (bf16[2,4,144,2048]{3,2,1,0:T(8,128)(2,1)}, bf16[4,704,512]{2,1,0:T(8,128)(2,1)}, bf16[4,704,512]{2,1,0:T(8,128)(2,1)}) custom-call(bf16[4,144,2048]{2,1,0:T(8,128)(2,1)} %convolution_convert_fusion.refs_0_, bf16[4,704,512]{2,1,0:T(8,128)(2,1)} %bitcast.136), custom_call_target="tpu_custom_call" | custom-call | tf_op jit(solution)/shard_map/spread3/pallas_call | solution.py:675
  428.5 35.5 %experts.1 = (bf16[2,576,2048]{2,1,0:T(8,128)(2,1)}, bf16[2,2,576,704]{3,2,1,0:T(8,128)(2,1)}, bf16[2,2,576,704]{3,2,1,0:T(8,128)(2,1)}, bf16[2,2,576,704]{3,2,1,0:T(8,128)(2,1)}) custom-call(bf16[2,576,2048]{2,1,0:T(8,128)(2,1)} %bitcast.126, bf16[2,576,2048]{2,1,0:T(8,128)(2,1)} %bitcast.135, bf16[16,2048]{1,0:T(8,128)(2,1)} %bitcast.149, ...), custom_call_target="tpu_custom_call" | custom-call | tf_op jit(solution)/shard_map/experts/pallas_call | solution.py:1183
  464.0 34.8 %mlp_grads.1 = (bf16[4,704,512]{2,1,0:T(8,128)(2,1)}, bf16[4,352,512]{2,1,0:T(8,128)(2,1)}, bf16[4,352,512]{2,1,0:T(8,128)(2,1)}, bf16[4,352,512]{2,1,0:T(8,128)(2,1)}, bf16[4,352,512]{2,1,0:T(8,128)(2,1)}) custom-call(bf16[1152,2048]{1,0:T(8,128)(2,1)} %bitcast.127, bf16[1152,2048]{1,0:T(8,128)(2,1)} %bitcast.134, bf16[2,1152,704]{2,1,0:T(8,128)(2,1)} %bitcast.128, ...), custom_call_target="tpu_custom_call" | custom-call | tf_op jit(solution)/shard_map/mlp_grads/pallas_call | solution.py:1263
  498.9 148.1 %collect5.1 = (bf16[2,4,144,2048]{3,2,1,0:T(8,128)(2,1)}, bf16[4,704,512]{2,1,0:T(8,128)(2,1)}) custom-call(bf16[2,2,576,704]{3,2,1,0:T(8,128)(2,1)} %get-tuple-element.90.refs_0_, bf16[2,2,576,704]{3,2,1,0:T(8,128)(2,1)} %get-tuple-element.91.refs_1_, bf16[2,2,576,704]{3,2,1,0:T(8,128)(2,1)} %get-tuple-element.92.refs_2_, ...), custom_call_target="tpu_custom_call" | custom-call | tf_op jit(solution)/shard_map/collect5/pallas_call | solution.py:827
  647.0 4.3 fusion.56
  651.3 2.6 convolution_reduce_fusion
  654.5 1.4 copy-done.8
  656.0 1.9 multiply_reduce_fusion
  658.8 1.5 multiply_reduce_fusion.4
  660.9 2.3 fusion.3.refs_0_
  663.2 74.0 %spread6.1 = (bf16[2,4,144,2048]{3,2,1,0:T(8,128)(2,1)}, bf16[4,352,512]{2,1,0:T(8,128)(2,1)}) custom-call(bf16[4,144,2048]{2,1,0:T(8,128)(2,1)} %fusion.3.refs_0_, bf16[4,352,512]{2,1,0:T(8,128)(2,1)} %get-tuple-element.96.refs_1_), custom_call_target="tpu_custom_call" | custom-call | tf_op jit(solution)/shard_map/spread6/pallas_call | solution.py:675
  737.2 45.9 %attend_back.1 = (bf16[2,768,1536]{2,1,0:T(8,128)(2,1)}, bf16[4,352,512]{2,1,0:T(8,128)(2,1)}) custom-call(bf16[2,576,512]{2,1,0:T(8,128)(2,1)} %get-tuple-element.74.refs_0_, bf16[2,768,512]{2,1,0:T(8,128)(2,1)} %get-tuple-element.75.refs_1_, bf16[2,768,512]{2,1,0:T(8,128)(2,1)} %get-tuple-element.76.refs_2_, bf16[2,576,2048]{2,1,0:T(8,128)(2,1)} %bitcast.124, ...), custom_call_target="tpu_custom_call" | custom-call | tf_op jit(solution)/shard_map/attend_back/pallas_call | solution.py:1387
  783.1 37.1 %attn_grads.1 = (bf16[4,512,256]{2,1,0:T(8,128)(2,1)}, bf16[4,512,256]{2,1,0:T(8,128)(2,1)}, bf16[4,512,256]{2,1,0:T(8,128)(2,1)}, bf16[4,512,256]{2,1,0:T(8,128)(2,1)}, bf16[4,352,512]{2,1,0:T(8,128)(2,1)}) custom-call(bf16[1536,2048]{1,0:T(8,128)(2,1)} %bitcast.131, bf16[1536,1536]{1,0:T(8,128)(2,1)} %bitcast.122, bf16[1152,2048]{1,0:T(8,128)(2,1)} %bitcast.125, ...), custom_call_target="tpu_custom_call" | custom-call | tf_op jit(solution)/shard_map/attn_grads/pallas_call | solution.py:1318
  820.2 101.7 %collect7.1 = (bf16[1,4,192,2048]{3,2,1,0:T(8,128)(2,1)}, bf16[4,352,512]{2,1,0:T(8,128)(2,1)}, bf16[4,512,256]{2,1,0:T(8,128)(2,1)}) custom-call(bf16[1,2,768,1536]{3,2,1,0:T(8,128)(2,1)} %bitcast.123, bf16[4,512,256]{2,1,0:T(8,128)(2,1)} %get-tuple-element.69.refs_3_.refs_1_, bf16[4,2,512,256]{3,2,1,0:T(8,128)(2,1)} %get-tuple-element.71.refs_5_.refs_2_, ...), custom_call_target="tpu_custom_call" | custom-call | tf_op jit(solution)/shard_map/collect7/pallas_call | solution.py:827
  921.9 9.5 unpack.1
  931.3 2.8 convert_reduce_fusion
  935.3 1.4 fusion.11
  937.8 1.3 pad_maximum_fusion.refs_1_
  941.0 72.8 %finish8.1 = (f32[16,128]{1,0:T(8,128)}, bf16[2,192,2048]{2,1,0:T(8,128)(2,1)}, bf16[4,512,256]{2,1,0:T(8,128)(2,1)}, bf16[4,512,256]{2,1,0:T(8,128)(2,1)}, bf16[4,512,256]{2,1,0:T(8,128)(2,1)}) custom-call(f32[4,4,16,128]{3,2,1,0:T(8,128)} %bitcast.143, bf16[2,192,2048]{2,1,0:T(8,128)(2,1)} %pad_maximum_fusion.refs_1_, ...), custom_call_target="tpu_custom_call" | custom-call | tf_op jit(solution)/shard_map/finish8/pallas_call | solution.py:991
  1013.8 1.5 convert_reduce_fusion.2
  1015.5 1.0 pad_maximum_fusion.1
  1016.8 1.5 convert_element_type.145
  1018.9 1.3 slice_bitcast_fusion
  1021.3 1.5 convert_element_type.146
  (110 shorter events, 14.8 us)
Async XLA Ops:
  1.6 3.4 copy-start.15
  1.6 3.4 copy-start.16
  1.6 3.6 copy-start
  5.0 1.2 copy-start.20
  5.0 1.2 copy-start.21
  5.0 1.2 copy-start.17
  5.0 1.2 copy-start.18
  6.9 112.9 %copy-start.22 = (s32[4,2]{0,1:T(2,128)S(1)}, s32[4,2]{0,1:T(2,128)}, u32[]{:S(2)}) copy-start(s32[4,2]{0,1:T(2,128)} %param.18) | copy-start | bytes 100
  217.1 112.7 %copy-start.14 = (bf16[4,16,512]{2,1,0:T(8,128)(2,1)S(1)}, bf16[4,16,512]{2,1,0:T(8,128)(2,1)}, u32[]{:S(2)}) copy-start(bf16[4,16,512]{2,1,0:T(8,128)(2,1)} %get-tuple-element.68.refs_2_) | copy-start | bytes 196612
  336.9 317.1 %copy-start.3 = (bf16[192,2048]{1,0:T(8,128)(2,1)}, bf16[192,2048]{1,0:T(8,128)(2,1)S(1)}, u32[]{:S(2)}) copy-start(bf16[192,2048]{1,0:T(8,128)(2,1)S(1)} %multiply_convert_fusion.4) | copy-start | bytes 2359300
  651.3 3.0 copy-start.5
  654.3 1.7 copy-start.8
  656.0 1.9 copy-start.9
  658.8 1.6 copy-start.6
  931.3 2.9 copy-start.2
  934.2 1.1 copy-start.1
  936.7 1.1 copy-start.7
  937.8 1.8 copy-start.4
  1013.8 1.5 copy-start.13
  1015.3 1.4 copy-start.12
  1016.8 2.1 copy-start.10
  1018.9 1.3 copy-start.19
  1018.9 2.4 copy-start.11

commit v2 on v1

--- a/solution.py
+++ b/solution.py
@@ -55,6 +55,10 @@
     return pairs
 
 
+def ctx_shift(lay, array, shift):
+    return lax.ppermute(array, "ctx", [(c, (c + shift) % lay.nc) for c in range(lay.nc)])
+
+
 def collect_permute(lay, block_of, blocks, stride):
     got, last = [], None
     for j in range(blocks):
@@ -86,6 +90,20 @@
         load.piece, load.both, load.place = self.piece, self.both, place
         load.src, load.outs, load.sems = src, outs, sems
         return load
+
+
+def farthest_first(at, size):
+    order = []
+    for gap in range(size - 1, 0, -1):
+        order += [(gap, at + gap < size), (size - gap, at - gap >= 0)]
+    return order
+
+
+def nearest_first(at, size):
+    order = []
+    for gap in range(1, size):
+        order += [(gap, at - gap >= 0), (size - gap, at + gap < size)]
+    return order
 
 
 class Load:
@@ -139,8 +157,8 @@
         if self.piece is None:
             self.to_core(0).start()
             return
-        for j in range(1, self.place[0]):
-            self.along_ctx(j).start()
+        for j, there in farthest_first(self.place[1], self.place[0]):
+            pl.when(there)(lambda j=j: self.along_ctx(j).start())
         self.keep().start()
         if self.both:
             self.to_core(0).start()
@@ -148,10 +166,13 @@
     def pass_on(self):
         if self.piece is None:
             return
-        for j in range(1, self.place[0]):
-            self.landed(j).wait_recv()
-            if self.both:
-                self.to_core(j).start()
+        for j, there in nearest_first(self.place[1], self.place[0]):
+
+            @pl.when(there)
+            def _():
+                self.landed(j).wait_recv()
+                if self.both:
+                    self.to_core(j).start()
 
     def finish(self):
         if self.piece is None:
@@ -498,6 +519,7 @@
     keep_small = pltpu.make_async_copy(small, smalls.at[c], ssend.at[0])
     keep_small.start()
     share(c, True)
+    loads[0].start()
     keep_later().start()
 
     for k in range(1, nc):
@@ -519,7 +541,7 @@
                     pl.when(sent)(lambda: copy.start())
                 share(source)
 
-    start_all(loads)
+    start_all(loads[1:])
     for j in range(1, experts):
         later_along_ctx(j).start()
 
@@ -626,8 +648,8 @@
 
     @pl.when(home)
     def _():
-        for j in range(1, blocks):
-            along_ctx(j).start()
+        for j, there in farthest_first(c // stride, blocks):
+            pl.when(there)(lambda j=j: along_ctx(j).start())
         for k in range(1, nf):
             in_plane(0, k).start()
         keep.start()
@@ -636,10 +658,14 @@
 
     @pl.when(home)
     def _():
-        for j in range(1, blocks):
-            along_ctx(j).wait_recv()
-            for k in range(1, nf):
-                in_plane(j, k).start()
+        for j, there in nearest_first(c // stride, blocks):
+
+            @pl.when(there)
+            def _():
+                along_ctx(j).wait_recv()
+                for k in range(1, nf):
+                    in_plane(j, k).start()
+
         keep.wait()
 
     for i in range(seqs):
@@ -692,7 +718,7 @@
 
 def collect_body(lay_sizes, stride, blocks, by_plane, dims, sets, n_a, n_w, hauls, *refs):
     nf, nc, nt, seqs = lay_sizes
-    ins, (out,), scratch, loads = hauls.split(refs, n_a + n_w, 1)
+    ins, outs, scratch, loads = hauls.split(refs, n_a + n_w, len(sets))
     lefts, rights = ins[:n_a], ins[n_a:]
     part, came, psend, precv, zsend, zrecv = scratch
     f, c, t = lax.axis_index("fsdp"), lax.axis_index("ctx"), lax.axis_index("tp")
@@ -722,7 +748,7 @@
     def to_owner(n, s, j):
         return pltpu.make_async_remote_copy(
             src_ref=part.at[n, own, s, block(j)],
-            dst_ref=out.at[n, j, :, pl.ds(pl.multiple_of(s * wide, wide), wide)],
+            dst_ref=outs[n].at[j, :, pl.ds(pl.multiple_of(s * wide, wide), wide)],
             send_sem=zsend.at[n, s, j],
             recv_sem=zrecv.at[n, s, j],
             device_id={"ctx": lax.rem(c - stride * j + nc, nc)},
@@ -767,7 +793,7 @@
                     for r in range(nf - 1):
                         summed = summed + came[n, r, s, where].astype(F32)
                     if j == 0:
-                        out[n, 0, :, pl.ds(pl.multiple_of(s * wide, wide), wide)] = summed.astype(BF16)
+                        outs[n][0, :, pl.ds(pl.multiple_of(s * wide, wide), wide)] = summed.astype(BF16)
                     else:
                         part[n, own, s, where] = summed.astype(BF16)
                         to_owner(n, s, j).start()
@@ -781,7 +807,8 @@
 
     @pl.when(jnp.logical_not(home))
     def _():
-        out[...] = jnp.zeros_like(out)
+        for out in outs:
+            out[...] = jnp.zeros_like(out)
 
     for slot in range(seqs):
 
@@ -820,7 +847,7 @@
         sums = [
             collect_permute(lay, functools.partial(block_of, terms), blocks, stride) for terms in sets
         ]
-        return [jnp.stack(sums), *haul_alone(lay, hauls, call_id)]
+        return [*sums, *haul_alone(lay, hauls, call_id)]
     hauls = Hauls(lay, hauls)
     dma = pltpu.SemaphoreType.DMA
     in_vmem = pl.BlockSpec(memory_space=pltpu.VMEM)
@@ -837,9 +864,9 @@
             len(rights),
             hauls,
         ),
-        out_shape=[jax.ShapeDtypeStruct((len(sets), blocks, rows, width), BF16)] + hauls.shapes,
+        out_shape=[jax.ShapeDtypeStruct((blocks, rows, width), BF16)] * len(sets) + hauls.shapes,
         in_specs=[in_vmem] * (len(lefts) + len(rights)) + hauls.in_specs,
-        out_specs=[in_vmem] + hauls.out_specs,
+        out_specs=[in_vmem] * len(sets) + hauls.out_specs,
         scratch_shapes=[
             pltpu.VMEM((len(sets), seqs, nc, count, wide), BF16),
             pltpu.VMEM((len(sets), lay.nf - 1, nc, count, wide), BF16),
@@ -982,9 +1009,7 @@
 
 
 def finish(lay, terms, grad, call_id, hauls=()):
-    lines, width = terms.shape
-    part = width // (lay.nf * lay.nc)
-    terms = terms.reshape(lines, lay.nf, lay.nc, part).transpose(2, 1, 0, 3)
+    lines, part = terms.shape[2:]
     hauls = Hauls(lay, hauls)
     dma = pltpu.SemaphoreType.DMA
     in_vmem = pl.BlockSpec(memory_space=pltpu.VMEM)
@@ -1155,8 +1180,8 @@
 def experts_body(rep, experts, n_ref, g_ref, small_ref, other_ref, *refs):
     weights, (ge_ref, hidden_ref, gate_ref, up_ref) = refs[:6], refs[6:]
     c = lax.axis_index("ctx")
-    lanes = lax.broadcasted_iota(jnp.int32, (1, small_ref.shape[0]), 1) - (2 + experts)
-    logits = dot(n_ref[0], small_ref[...], NT)
+    lanes = lax.broadcasted_iota(jnp.int32, (1, small_ref.shape[1]), 1) - (2 + experts)
+    logits = chunk_dot(n_ref.at[0], small_ref, None, NT)
     mine = jnp.sum(jnp.where(lanes == c // rep, logits, 0.0), axis=-1, keepdims=True)
     theirs = jnp.where(lanes.astype(F32) == other_ref[0], logits, 0.0)
     theirs = jnp.sum(theirs, axis=-1, keepdims=True)
@@ -1186,7 +1211,7 @@
         in_specs=[
             pl.BlockSpec((1, count, width), per_seq),
             pl.BlockSpec((1, count, width), per_seq),
-            pl.BlockSpec(small.shape, lambda i: (0, 0)),
+            pl.BlockSpec(small.shape, lambda i: (0, 0, 0)),
             pl.BlockSpec((1, count, 1), per_seq),
         ]
         + [pl.BlockSpec(w.shape, lambda i: (0, 0, 0), pipeline_mode=once) for w in weights],
@@ -1278,7 +1303,7 @@
 
 def attn_grads_body(lay_sizes, hauls, *refs):
     nf, nc, nt, seqs = lay_sizes
-    (x_ref, d_ref, g_ref, mixed_ref), outs, scratch, loads = hauls.split(refs, 4, 4)
+    (x_ref, d_ref, g_ref, mixed_ref), outs, scratch, loads = hauls.split(refs, 4, 2 + lay_sizes[1])
     kept, away, came = scratch[:3]
     copy = core_exchange(scratch[1:], nt)
     wide, half = away.shape[-2:]
@@ -1300,8 +1325,13 @@
     @pl.loop(0, nc)
     def _(s):
         copy(s).wait_recv()
-        for i in range(4):
-            outs[i][s] = (kept[s, i] + came[s, i].astype(F32)).astype(BF16)
+        outs[0][s] = (kept[s, 0] + came[s, 0].astype(F32)).astype(BF16)
+        outs[1][s] = (kept[s, 3] + came[s, 3].astype(F32)).astype(BF16)
+
+    for s, piece in enumerate(outs[2:]):
+        d = lax.rem(lax.axis_index("ctx") + s, nc)
+        for i in range(2):
+            piece[i] = (kept[d, 1 + i] + came[d, 1 + i].astype(F32)).astype(BF16)
 
     @pl.loop(0, nc)
     def _(s):
@@ -1318,8 +1348,10 @@
     return pl.pallas_call(
         functools.partial(attn_grads_body, lay.sizes, hauls),
         in_specs=[in_vmem] * 4 + hauls.in_specs,
-        out_specs=[in_vmem] * 4 + hauls.out_specs,
-        out_shape=[jax.ShapeDtypeStruct((nc,) + piece, BF16)] * 4 + hauls.shapes,
+        out_specs=[in_vmem] * (2 + nc) + hauls.out_specs,
+        out_shape=[jax.ShapeDtypeStruct((nc,) + piece, BF16)] * 2
+        + [jax.ShapeDtypeStruct((2,) + piece, BF16)] * nc
+        + hauls.shapes,
         scratch_shapes=[
             pltpu.VMEM((nc, 4) + piece, F32),
             pltpu.VMEM((nc, 4) + piece, BF16),
@@ -1442,6 +1474,161 @@
     )(*parts)
 
 
+def row_of(small_ref, line):
+    planes = [small_ref[s, line : line + 1] for s in range(small_ref.shape[0])]
+    return jnp.concatenate(planes, axis=1).astype(F32)
+
+
+def choices(ids, expert, experts, cap):
+    rows = ids.shape[0]
+    before = lax.broadcasted_iota(jnp.int32, (rows, rows), 1)
+    before = (before < lax.broadcasted_iota(jnp.int32, (rows, rows), 0)).astype(BF16)
+    lanes = lax.broadcasted_iota(jnp.int32, (rows, DH), 1).astype(F32)
+    member = jnp.where(jnp.logical_or(ids[:, 0:1] == lanes, ids[:, 1:2] == lanes), 1.0, 0.0)
+    ranks = dot(before, member.astype(BF16))
+    columns = lax.broadcasted_iota(jnp.int32, (rows, experts * cap), 1).astype(F32)
+    maps = []
+    for slot in range(2):
+        chosen = ids[:, slot : slot + 1]
+        rank = jnp.sum(jnp.where(lanes == chosen, ranks, 0.0), axis=-1, keepdims=True)
+        ahead = chosen - expert.astype(F32)
+        ahead = jnp.where(ahead < 0.0, ahead + experts, ahead)
+        maps.append(jnp.where(columns == ahead * cap + rank, 1.0, 0.0).astype(BF16))
+    return maps
+
+
+def slot_gates(normed, small_ref, ids, first):
+    planes, lines, wide = small_ref.shape
+    logits = 0.0
+    for s in range(planes):
+        logits = logits + dot(normed[:, s * wide : (s + 1) * wide], small_ref[s], NT)
+    lanes = lax.broadcasted_iota(jnp.int32, logits.shape, 1).astype(F32)
+    picked = [
+        jnp.sum(jnp.where(lanes == ids[:, k : k + 1] + first, logits, 0.0), axis=-1, keepdims=True)
+        for k in range(2)
+    ]
+    return jax.nn.sigmoid(picked[0] - picked[1]), jax.nn.sigmoid(picked[1] - picked[0])
+
+
+def norm_of(values, gain):
+    inverse = lax.rsqrt(jnp.mean(values * values, axis=-1, keepdims=True) + EPSILON)
+    scaled = values * inverse
+    return inverse, scaled, (scaled * gain).astype(BF16)
+
+
+def norm_back(grad, gain, inverse, scaled):
+    turned = grad * gain
+    return inverse * (turned - scaled * jnp.mean(turned * scaled, axis=-1, keepdims=True))
+
+
+def logits_back(gates, choice, ids, first):
+    mean = gates[0] * choice[0] + gates[1] * choice[1]
+    lanes = lax.broadcasted_iota(jnp.int32, (ids.shape[0], DH), 1).astype(F32)
+    out = 0.0
+    for k in range(2):
+        inner = gates[k] * (choice[k] - mean)
+        out = out + jnp.where(lanes == ids[:, k : k + 1] + first, inner, 0.0)
+    return out
+
+
+def exact_tn(left, right):
+    total = 0.0
+    for _ in range(3):
+        part = left.astype(BF16)
+        total = total + dot(part, right, TN)
+        left = left - part.astype(F32)
+    return total
+
+
+def owner_forward_body(rep, experts, x_ref, ids_ref, small_ref, rows_ref, residual_ref, out_ref):
+    expert = lax.axis_index("ctx") // rep
+    cap = rows_ref.shape[0] // experts
+    ids = ids_ref[...]
+    x = x_ref[...].astype(F32)
+    normed_one = norm_of(x, row_of(small_ref, 0))[2]
+    gates = slot_gates(normed_one, small_ref, ids[:, 0:2], 2)
+    maps = choices(ids[:, 0:2], expert, experts, cap)
+    residual = x + (gates[0] * dot(maps[0], rows_ref[...]) + gates[1] * dot(maps[1], rows_ref[...]))
+    residual_ref[...] = residual
+    normed_two = norm_of(residual, row_of(small_ref, 1))[2]
+    maps = choices(ids[:, 2:4], expert, experts, cap)
+    out_ref[...] = dot(maps[0] + maps[1], normed_two, TN).astype(BF16)
+
+
+def owner_middle_body(rep, experts, *refs):
+    x_ref, ids_ref, small_ref, up_ref, residual_ref, branch_ref, expert_ref, grad_ref = refs[:8]
+    layer_ref, grad_res_ref, out_ref, logits_ref, terms_ref = refs[8:]
+    expert = lax.axis_index("ctx") // rep
+    cap = branch_ref.shape[0] // experts
+    ids = ids_ref[...]
+    upstream, residual = up_ref[...].astype(F32), residual_ref[...]
+    gain_two = row_of(small_ref, 1)
+    inverse_two, scaled_two, normed_two = norm_of(residual, gain_two)
+    gates = slot_gates(normed_two, small_ref, ids[:, 2:4], 2 + experts)
+    maps = choices(ids[:, 2:4], expert, experts, cap)
+    choice, total = [], 0.0
+    for k in range(2):
+        expert_out = dot(maps[k], expert_ref[...])
+        choice.append(jnp.sum(upstream * expert_out, axis=-1, keepdims=True))
+        total = total + gates[k] * expert_out
+    layer_ref[...] = (residual + total).astype(BF16)
+    logits_two = logits_back(gates, choice, ids[:, 2:4], 2 + experts)
+    grad = dot(maps[0] + maps[1], grad_ref[...])
+    for e in range(experts):
+        line = 2 + experts + e
+        grad = grad + logits_two[:, line : line + 1] * row_of(small_ref, line)
+    grad_res = upstream + norm_back(grad, gain_two, inverse_two, scaled_two)
+    grad_res_ref[...] = grad_res
+    gain_grad = jnp.sum(grad * scaled_two, axis=0, keepdims=True)
+    normed_one = norm_of(x_ref[...].astype(F32), row_of(small_ref, 0))[2]
+    gates = slot_gates(normed_one, small_ref, ids[:, 0:2], 2)
+    maps = choices(ids[:, 0:2], expert, experts, cap)
+    choice, out = [], 0.0
+    for k in range(2):
+        branch = dot(maps[k], branch_ref[...])
+        choice.append(jnp.sum(grad_res * branch, axis=-1, keepdims=True))
+        out = out + dot(maps[k], (gates[k] * grad_res).astype(BF16), TN)
+    out_ref[...] = out.astype(BF16)
+    logits_one = logits_back(gates, choice, ids[:, 0:2], 2)
+    logits_ref[...] = logits_one
+    lines = terms_ref.shape[0]
+    terms = exact_tn(logits_one, normed_one) + exact_tn(logits_two, normed_two)
+    place = lax.broadcasted_iota(jnp.int32, terms_ref.shape, 0)
+    terms_ref[...] = jnp.where(place == 1, gain_grad, terms[:lines])
+
+
+def owner_back_body(experts, x_ref, small_ref, rows_ref, logits_ref, grad_res_ref, layer_ref, terms_ref, both_ref, out_ref):
+    gain = row_of(small_ref, 0)
+    inverse, scaled, _ = norm_of(x_ref[...].astype(F32), gain)
+    grad = 0.0
+    for j in range(rows_ref.shape[0]):
+        grad = grad + rows_ref[j].astype(F32)
+    for e in range(experts):
+        grad = grad + logits_ref[:, 2 + e : 3 + e] * row_of(small_ref, 2 + e)
+    both_ref[0] = layer_ref[...]
+    both_ref[1] = (grad_res_ref[...] + norm_back(grad, gain, inverse, scaled)).astype(BF16)
+    gain_grad = jnp.sum(grad * scaled, axis=0, keepdims=True)
+    place = lax.broadcasted_iota(jnp.int32, terms_ref.shape, 0)
+    terms = jnp.where(place == 0, gain_grad, terms_ref[...])
+    planes, chips, _, part = out_ref.shape
+    for plane in range(planes):
+        for chip in range(chips):
+            first = (chip * planes + plane) * part
+            out_ref[plane, chip] = terms[:, first : first + part]
+
+
+def own_kernel(body, name, results, *operands):
+    in_vmem = pl.BlockSpec(memory_space=pltpu.VMEM)
+    return pl.pallas_call(
+        body,
+        in_specs=[in_vmem] * len(operands),
+        out_specs=[in_vmem] * len(results),
+        out_shape=[jax.ShapeDtypeStruct(dims, kind) for dims, kind in results],
+        compiler_params=pltpu.CompilerParams(vmem_limit_bytes=VMEM_LIMIT),
+        name=name,
+    )(*operands)
+
+
 def ranks_of(member):
     count = member.shape[-1]
     before = (jnp.arange(count)[:, None] < jnp.arange(count)[None, :]).astype(BF16)
@@ -1453,25 +1640,6 @@
     rank = ranks_of(member).astype(jnp.int32)
     place = jnp.arange(cap, dtype=jnp.int32)[:, None]
     return jnp.logical_and(member[..., None, :], rank[..., None, :] == place)
-
-
-def choose_maps(pick, ids, expert):
-    chosen = ids.T[:, None, :] == expert[None, :, None]
-    maps = jnp.logical_and(pick[None], chosen[:, :, None, :])
-    slots, experts, cap, rows = maps.shape
-    return maps.transpose(0, 3, 1, 2).reshape(slots, rows, experts * cap).astype(BF16)
-
-
-def chosen_gates(normed, router, expert_ids, experts):
-    logits = jnp.dot(normed, router, preferred_element_type=F32)
-    onehot = (expert_ids[:, :, None] == jnp.arange(experts, dtype=jnp.int32)).astype(F32)
-    picked = jnp.sum(onehot * logits[:, None, :], axis=-1)
-    return jax.nn.softmax(picked, axis=-1), onehot
-
-
-def router_back(gates, grad_gates, onehot):
-    inner = gates * (grad_gates - jnp.sum(gates * grad_gates, axis=-1, keepdims=True))
-    return jnp.sum(onehot * inner[:, :, None], axis=1)
 
 
 def per_device(
@@ -1524,21 +1692,10 @@
         1,
         [to_planes(query_weight, by_plane(), True), Relay(kv_weight)],
     )
-    smalls = small_all.transpose(1, 0, 2).reshape(-1, width)
-    gain_one, gain_two = smalls[0:1].astype(F32), smalls[1:2].astype(F32)
-    router_one = smalls[2 : 2 + experts].T
-    router_two = smalls[2 + experts : 2 + 2 * experts].T
-
     gate_up_turned = gate_up_weight.swapaxes(-1, -2)
     down_turned = down_weight.swapaxes(-1, -2)
 
-    pick_own_a = pick_maps(jnp.broadcast_to(attn_ids, (experts, rows, 2)), expert_of, cap)
-    choose_a = choose_maps(pick_own_a, attn_ids, expert_of)
-    choose_m = choose_maps(pick_own_m, mlp_ids, expert_of)
-
-    def by_slot(choose, values):
-        flat = values.reshape(-1, values.shape[-1])
-        return jnp.einsum("knr,rd->knd", choose, flat, preferred_element_type=F32)
+    own_ids = ids.astype(F32)
 
     half_len = rows // 2
     offsets = jnp.arange(rows, dtype=jnp.int32)
@@ -1553,12 +1710,6 @@
     cosine, sine = jnp.cos(pos * freqs), jnp.sin(pos * freqs)
     cosine = jnp.concatenate([cosine, cosine], axis=-1)
     sine = jnp.concatenate([-sine, sine], axis=-1)
-
-    inputs = tokens.astype(F32)
-    inverse_one = lax.rsqrt(jnp.mean(inputs * inputs, axis=-1, keepdims=True) + EPSILON)
-    scaled_one = inputs * inverse_one
-    normed_one = (scaled_one * gain_one).astype(BF16)
-    attn_gates, attn_hot = chosen_gates(normed_one, router_one, attn_ids, experts)
 
     normed_all, q, k, v, mixed, put, pos_q, other, o_own, o_sib, gate_own, gate_sib, g_blocks = attend(
         lay,
@@ -1589,16 +1740,20 @@
         2,
         hauls=[to_planes(gate_up_turned, by_plane(1), True)],
     )
-    branch = by_slot(choose_a, branch_rows[0])
-    residual = inputs + jnp.sum(attn_gates.T[:, :, None] * branch, axis=0)
-    inverse_two = lax.rsqrt(jnp.mean(residual * residual, axis=-1, keepdims=True) + EPSILON)
-    scaled_two = residual * inverse_two
-    normed_two = (scaled_two * gain_two).astype(BF16)
-    mlp_gates, mlp_hot = chosen_gates(normed_two, router_two, mlp_ids, experts)
+    branch_rows = branch_rows.reshape(-1, width)
+    residual, n2_own = own_kernel(
+        functools.partial(owner_forward_body, rep, experts),
+        "owner_forward",
+        [((rows, width), F32), ((experts * cap, width), BF16)],
+        tokens,
+        own_ids,
+        small_all,
+        branch_rows,
+    )
 
     n2, down_own, down_sib = spread(
         lay,
-        dispatch(pick_own_m, normed_two),
+        n2_own.reshape(experts, cap, width),
         rep,
         3,
         [to_planes(down_turned, by_plane(), True)],
@@ -1608,7 +1763,7 @@
         lay,
         n2,
         g_blocks,
-        smalls,
+        small_all,
         other,
         gate_own,
         gate_sib,
@@ -1626,7 +1781,7 @@
         4,
     )
     by_piece = lambda d: (d,)
-    back_rows, gate_back = collect(
+    expert_rows, grad_rows, gate_back = collect(
         lay,
         [hidden, grad_gate, grad_up],
         [gate_own, up_own, down_own, gate_sib, up_sib, down_sib],
@@ -1640,34 +1795,28 @@
         NN,
         [to_planes(gate_grads, by_piece)],
     )
-    expert_rows, grad_rows = back_rows[0], back_rows[1]
-    expert_out = by_slot(choose_m, expert_rows)
-    layer_out = residual + jnp.sum(mlp_gates.T[:, :, None] * expert_out, axis=0)
-    layer_out = layer_out.astype(BF16)
-    upstream = cotangent.astype(F32)
-    grad_choice_m = jnp.sum(upstream[None] * expert_out, axis=-1).T
-    grad_logits_two = router_back(mlp_gates, grad_choice_m, mlp_hot)
-    grad_normed_two = jnp.sum(by_slot(choose_m, grad_rows), axis=0) + jnp.dot(
-        grad_logits_two, router_two.astype(F32).T, precision=HIGH
+    lines = -(-(2 + 2 * experts) // 16) * 16
+    layer_out, grad_residual, gb_own, logits_one, terms = own_kernel(
+        functools.partial(owner_middle_body, rep, experts),
+        "owner_middle",
+        [
+            ((rows, width), BF16),
+            ((rows, width), F32),
+            ((experts * cap, width), BF16),
+            ((rows, DH), F32),
+            ((lines, width), F32),
+        ],
+        tokens,
+        own_ids,
+        small_all,
+        cotangent,
+        residual,
+        branch_rows,
+        expert_rows.reshape(-1, width),
+        grad_rows.reshape(-1, width),
     )
-    grad_scaled_two = grad_normed_two * gain_two
-    grad_residual = upstream + inverse_two * (
-        grad_scaled_two
-        - scaled_two * jnp.mean(grad_scaled_two * scaled_two, axis=-1, keepdims=True)
-    )
-
-    gate_rows_a = jnp.zeros((experts, rows), F32)
-    for slot in range(2):
-        gate_rows_a = gate_rows_a + jnp.where(
-            attn_ids[None, :, slot] == expert_of[:, None], attn_gates[None, :, slot], 0.0
-        )
-    grad_branch_own = jnp.einsum(
-        "jrn,jnd->jrd",
-        pick_own_a.astype(BF16),
-        (gate_rows_a[:, :, None] * grad_residual[None]).astype(BF16),
-        preferred_element_type=F32,
-    ).astype(BF16)
-    gb, up_a = spread(lay, grad_branch_own, rep, 6, [to_planes(up_a, by_piece)])
+
+    gb, up_a = spread(lay, gb_own.reshape(experts, cap, width), rep, 6, [to_planes(up_a, by_piece)])
     gb = gb.reshape(seqs, experts * cap, width)
     dqkv, up_b = attend_back(
         lay,
@@ -1684,7 +1833,7 @@
         11,
         [to_planes(up_b, by_piece)],
     )
-    q_grads, k_grads, v_grads, o_grads, down_a = attn_grads(
+    q_grads, o_grads, *kv_pieces, down_a = attn_grads(
         lay,
         normed_all.reshape(-1, width),
         dqkv.reshape(-1, 3 * heads),
@@ -1693,7 +1842,8 @@
         10,
         [to_planes(down_a, by_piece)],
     )
-    grad_one_rows, down_b, o_back = collect(
+    kv_back = [kv_pieces[0]] + [ctx_shift(lay, kv_pieces[s], s) for s in range(1, nc)]
+    grad_one_rows, down_b, o_back, q_back = collect(
         lay,
         [dqkv[None]],
         [q_own, kv_own, q_sib, kv_sib],
@@ -1707,37 +1857,23 @@
         1,
         nc,
         7,
-        hauls=[to_planes(down_b, by_piece), to_planes(o_grads, by_piece)],
+        hauls=[to_planes(grads, by_piece) for grads in (down_b, o_grads, q_grads)],
         by_plane=True,
     )
 
-    grad_choice_a = jnp.sum(grad_residual[None] * branch, axis=-1).T
-    grad_logits_one = router_back(attn_gates, grad_choice_a, attn_hot)
-    grad_normed_one = jnp.sum(grad_one_rows[0].astype(F32), axis=0) + jnp.dot(
-        grad_logits_one, router_one.astype(F32).T, precision=HIGH
+    both, terms = own_kernel(
+        functools.partial(owner_back_body, experts),
+        "owner_back",
+        [((2, rows, width), BF16), ((nc, nf, lines, width // (nf * nc)), F32)],
+        tokens,
+        small_all,
+        grad_one_rows,
+        logits_one,
+        grad_residual,
+        layer_out,
+        terms,
     )
-    grad_scaled_one = grad_normed_one * gain_one
-    grad_tokens = grad_residual + inverse_one * (
-        grad_scaled_one
-        - scaled_one * jnp.mean(grad_scaled_one * scaled_one, axis=-1, keepdims=True)
-    )
-    grad_tokens = grad_tokens.astype(BF16)
-    terms = jnp.concatenate(
-        [
-            jnp.sum(grad_normed_one * scaled_one, axis=0)[None],
-            jnp.sum(grad_normed_two * scaled_two, axis=0)[None],
-            jnp.dot(grad_logits_one.T, normed_one.astype(F32), precision=HIGH),
-            jnp.dot(grad_logits_two.T, normed_two.astype(F32), precision=HIGH),
-        ]
-    )
-    terms = jnp.pad(terms, ((0, -terms.shape[0] % 8), (0, 0)))
-    terms, both_out, q_back, k_back, v_back = finish(
-        lay,
-        terms,
-        jnp.stack([layer_out, grad_tokens]),
-        8,
-        [to_planes(grads, by_piece) for grads in (q_grads, k_grads, v_grads)],
-    )
+    terms, both_out = finish(lay, terms, both, 8)
     layer_out, grad_tokens = both_out[0], both_out[1]
 
     def by_expert(came):
@@ -1747,7 +1883,7 @@
         return out
 
     grad_query_weight, grad_output_weight = by_expert(q_back), by_expert(o_back)
-    grad_kv_weight = jnp.stack([jnp.sum(g.astype(F32), axis=0) for g in (k_back, v_back)])
+    grad_kv_weight = functools.reduce(jnp.add, [piece.astype(F32) for piece in kv_back])
     grad_gate_up, grad_down = unpack(lay, gate_back, up_a, up_b, down_a, down_b)
     grad_gate_up, grad_down = grad_gate_up.swapaxes(-1, -2), grad_down.swapaxes(-1, -2)
     return (

time: 1030 us -> 1050 us (1.019)
  Pallas kernels: 967 us -> 1000 us
  starting transfers between devices: 0 us -> 21 us
  matrix products: 21.6 us -> 2.33 us
    pallas_call x3, Pallas kernels: 363 us -> 417 us  [collect(): pl.pallas_call(functools.partial(collect_body, lay.sizes, stride, blocks,...]
    pallas_call x1, Pallas kernels: 72.8 us -> 23 us  [finish(): pl.pallas_call(functools.partial(finish_body, lay.sizes, hauls), out_shap...]
    pallas_call x0 -> x3, Pallas kernels: none -> 24.6 us  [own_kernel(): pl.pallas_call(body, in_specs=[in_vmem] * len(operands), out_specs=[in_vm...]
    ppermute x0 -> x3, starting transfers between devices: none -> 21 us  [ctx_shift(): lax.ppermute(array, 'ctx', [(c, (c + shift) % lay.nc) for c in range(lay....]
    dot_general x10 -> x0, matrix products: 15.7 us -> none  [the longest x3 9.52 us: by_slot(): return jnp.einsum('knr,rd->knd', choose, flat, preferred_element_type=F32)]
  transfers between devices with their start and end apart: 0 -> 3, of which waited for: 0 -> 0; matrix products, arithmetic and copies ran while one was open for 0% -> 1% of each run, Pallas kernels for 0% -> 17%
where the time goes in v2:
time: 1050 us
  Pallas kernels  1000 us (95%)
  starting transfers between devices  21 us (2%)
  other arithmetic  13.2 us (1%)
    pallas_call x3, Pallas kernels, collect(): pl.pallas_call(functools.partial(collect_body, lay.sizes, stride, blocks,...  417 us
    pallas_call x2, Pallas kernels, spread(): pl.pallas_call(functools.partial(spread_body, lay.sizes, stride, blocks,...  162 us
    pallas_call x1, Pallas kernels, opening(): pl.pallas_call(functools.partial(opening_body, lay.sizes, experts, hauls)...  115 us
    pallas_call x1, Pallas kernels, attend(): pl.pallas_call(functools.partial(attend_body, lay.sizes, lay.rep, hauls),...  87.8 us
    pallas_call x1, Pallas kernels, attend_back(): pl.pallas_call(functools.partial(attend_back_body, lay.sizes, hauls), gri...  52 us
    pallas_call x1, Pallas kernels, attn_grads(): pl.pallas_call(functools.partial(attn_grads_body, lay.sizes, hauls), in_s...  41.8 us
    pallas_call x1, Pallas kernels, experts_apply(): pl.pallas_call(functools.partial(experts_body, lay.rep, lay.experts), gri...  35.5 us
    pallas_call x1, Pallas kernels, mlp_grads(): pl.pallas_call(functools.partial(mlp_grads_body, nc, lay.nt), in_specs=[i...  34.8 us
  transfers between devices with their start and end apart: 3, of which 0 were waited for; matrix products, arithmetic and copies ran while one was open for 1% of the time, Pallas kernels for 17%

profile of v2, /device:TPU:0, one launch (start us, length us, event | category | flops | bytes accessed | tf_op | source)
XLA Modules:
  0.0 1049.0 jit_solution(18065782457113009379)
XLA Ops:
  0.7 0.8 multiply_bitcast_fusion.1
  1.6 1.0 convert_element_type.64.refs_9_.refs_7_
  3.3 0.8 compare_reduce_fusion
  4.1 0.7 convert.6
  7.1 2.1 fusion.1.refs_0_
  9.2 1.4 fusion.7
  10.7 2.2 convolution_convert_fusion.refs_2_
  12.9 1.1 pad_maximum_fusion
  14.7 115.5 %opening1.1 = (bf16[2,4,192,2176]{3,2,1,0:T(8,128)(2,1)}, bf16[4,16,512]{2,1,0:T(8,128)(2,1)}, bf16[4,144,1024]{2,1,0:T(8,128)(2,1)}, bf16[4,96,2176]{2,1,0:T(8,...) custom-call(bf16[192,2176]{1,0:T(8,128)(2,1)} %fusion.1.refs_0_, ...), custom_call_target="tpu_custom_call" | custom-call | tf_op jit(solution)/shard_map/opening1/pallas_call | solution.py:597
  130.2 87.8 %attend.1 = (bf16[2,768,2048]{2,1,0:T(8,128)(2,1)}, bf16[2,576,512]{2,1,0:T(8,128)(2,1)}, bf16[2,768,512]{2,1,0:T(8,128)(2,1)}, bf16[2,768,512]{2,1,0:T(8,128)(2...) custom-call(bf16[2,768,2176]{2,1,0:T(8,128)(2,1)} %bitcast.46, ...), custom_call_target="tpu_custom_call" | custom-call | tf_op jit(solution)/shard_map/attend/pallas_call | solution.py:1158
  218.0 113.3 %collect2.1 = (bf16[4,144,2048]{2,1,0:T(8,128)(2,1)}, bf16[4,704,512]{2,1,0:T(8,128)(2,1)}, bf16[4,704,512]{2,1,0:T(8,128)(2,1)}) custom-call(bf16[1,2,576,512]{3,2,1,0:T(8,128)(2,1)} %bitcast.62, bf16[4,512,256]{2,1,0:T(8,128)(2,1)} %get-tuple-element.88.refs_1_.refs_4_, bf16[4,512,256]{2,1,0:T(8,128)(2,1)} %get-tuple-element.89.refs_2_.refs_5_, ...), custom_call_target="tpu_custom_call" | custom-call | tf_op jit(solution)/shard_map/collect2/pallas_call | solution.py:854
  331.2 6.6 owner_forward.1
  337.8 88.8 %spread3.1 = (bf16[2,4,144,2048]{3,2,1,0:T(8,128)(2,1)}, bf16[4,704,512]{2,1,0:T(8,128)(2,1)}, bf16[4,704,512]{2,1,0:T(8,128)(2,1)}) custom-call(bf16[4,144,2048]{2,1,0:T(8,128)(2,1)} %bitcast.69, bf16[4,704,512]{2,1,0:T(8,128)(2,1)} %bitcast.66), custom_call_target="tpu_custom_call" | custom-call | tf_op jit(solution)/shard_map/spread3/pallas_call | solution.py:701
  426.6 35.5 %experts.1 = (bf16[2,576,2048]{2,1,0:T(8,128)(2,1)}, bf16[2,2,576,704]{3,2,1,0:T(8,128)(2,1)}, bf16[2,2,576,704]{3,2,1,0:T(8,128)(2,1)}, bf16[2,2,576,704]{3,2,1,0:T(8,128)(2,1)}) custom-call(bf16[2,576,2048]{2,1,0:T(8,128)(2,1)} %bitcast.54, bf16[2,576,2048]{2,1,0:T(8,128)(2,1)} %bitcast.65, bf16[4,16,512]{2,1,0:T(8,128)(2,1)} %get-tuple-element.77.refs_2_.small_ref, ...), custom_call_target="tpu_custom_call" | custom-call | tf_op jit(solution)/shard_map/experts/pallas_call | solution.py:1208
  462.2 34.8 %mlp_grads.1 = (bf16[4,704,512]{2,1,0:T(8,128)(2,1)}, bf16[4,352,512]{2,1,0:T(8,128)(2,1)}, bf16[4,352,512]{2,1,0:T(8,128)(2,1)}, bf16[4,352,512]{2,1,0:T(8,128)(2,1)}, bf16[4,352,512]{2,1,0:T(8,128)(2,1)}) custom-call(bf16[1152,2048]{1,0:T(8,128)(2,1)} %bitcast.55, bf16[1152,2048]{1,0:T(8,128)(2,1)} %bitcast.64, bf16[2,1152,704]{2,1,0:T(8,128)(2,1)} %bitcast.56, ...), custom_call_target="tpu_custom_call" | custom-call | tf_op jit(solution)/shard_map/mlp_grads/pallas_call | solution.py:1288
  497.0 160.7 %collect5.1 = (bf16[4,144,2048]{2,1,0:T(8,128)(2,1)}, bf16[4,144,2048]{2,1,0:T(8,128)(2,1)}, bf16[4,704,512]{2,1,0:T(8,128)(2,1)}) custom-call(bf16[2,2,576,704]{3,2,1,0:T(8,128)(2,1)} %get-tuple-element.102.refs_0_, bf16[2,2,576,704]{3,2,1,0:T(8,128)(2,1)} %get-tuple-element.103.refs_1_, bf16[2,2,576,704]{3,2,1,0:T(8,128)(2,1)} %get-tuple-element.104.refs_2_, ...), custom_call_target="tpu_custom_call" | custom-call | tf_op jit(solution)/shard_map/collect5/pallas_call | solution.py:854
  657.7 12.3 %owner_middle.1 = (bf16[192,2048]{1,0:T(8,128)(2,1)}, f32[192,2048]{1,0:T(8,128)}, bf16[576,2048]{1,0:T(8,128)(2,1)}, f32[192,128]{1,0:T(8,128)}, f32[16,2048]{1,0:T(8,128)}) custom-call(bf16[192,2048]{1,0:T(8,128)(2,1)} %x_ref.3, f32[192,4]{1,0:T(8,128)} %convert_element_type.57.ids_ref.refs_1_, bf16[4,16,512]{2,1,0:T(8,128)(2,1)} %get-tuple-element.77.refs_2_.small_ref, ...), custom_call_target="tpu_custom_call" | custom-call | tf_op jit(solution)/shard_map/owner_middle/pallas_call | solution.py:1622
  670.0 73.6 %spread6.1 = (bf16[2,4,144,2048]{3,2,1,0:T(8,128)(2,1)}, bf16[4,352,512]{2,1,0:T(8,128)(2,1)}) custom-call(bf16[4,144,2048]{2,1,0:T(8,128)(2,1)} %bitcast.70, bf16[4,352,512]{2,1,0:T(8,128)(2,1)} %get-tuple-element.110.refs_1_), custom_call_target="tpu_custom_call" | custom-call | tf_op jit(solution)/shard_map/spread6/pallas_call | solution.py:701
  743.6 52.0 %attend_back.1 = (bf16[2,768,1536]{2,1,0:T(8,128)(2,1)}, bf16[4,352,512]{2,1,0:T(8,128)(2,1)}) custom-call(bf16[2,576,512]{2,1,0:T(8,128)(2,1)} %get-tuple-element.84.refs_0_, bf16[2,768,512]{2,1,0:T(8,128)(2,1)} %get-tuple-element.85.refs_1_, bf16[2,768,512]{2,1,0:T(8,128)(2,1)} %get-tuple-element.86.refs_2_, bf16[2,576,2048]{2,1,0:T(8,128)(2,1)} %bitcast.52, ...), custom_call_target="tpu_custom_call" | custom-call | tf_op jit(solution)/shard_map/attend_back/pallas_call | solution.py:1419
  795.7 41.8 %attn_grads.1 = (bf16[4,512,256]{2,1,0:T(8,128)(2,1)}, bf16[4,512,256]{2,1,0:T(8,128)(2,1)}, bf16[2,512,256]{2,1,0:T(8,128)(2,1)}, bf16[2,512,256]{2,1,0:T(8,128...) custom-call(bf16[1536,2048]{1,0:T(8,128)(2,1)} %bitcast.61, ...), custom_call_target="tpu_custom_call" | custom-call | tf_op jit(solution)/shard_map/attn_grads/pallas_call | solution.py:1348
  837.4 18.5 %collective-permute-start = (bf16[2,512,256]{2,1,0:T(8,128)(2,1)}, bf16[2,512,256]{2,1,0:T(8,128)(2,1)S(1)}, u32[]{:S(2)}, u32[]{:S(2)}) collective-permute-start(bf16[2,512,256]{2,1,0:T(8,128)(2,1)} %get-tuple-element.131), channel_id=1, source_target_pairs={{0,2},{2,4},{4,6},{6,0},{1,3},{3,5},{5,7},{7,1},{8,10},{10,12},{12... | collective-permute-start | bytes 1572872 | tf_op jit(solution)/shard_map/ppermute | solution.py:59
  856.0 2.4 collective-permute-start.2
  858.4 143.5 %collect7.1 = (bf16[4,192,2048]{2,1,0:T(8,128)(2,1)}, bf16[4,352,512]{2,1,0:T(8,128)(2,1)}, bf16[4,512,256]{2,1,0:T(8,128)(2,1)}, bf16[4,512,256]{2,1,0:T(8,128)(2,1)}) custom-call(bf16[1,2,768,1536]{3,2,1,0:T(8,128)(2,1)} %bitcast.51, bf16[4,512,256]{2,1,0:T(8,128)(2,1)} %get-tuple-element.79.refs_3_.refs_1_, ...), custom_call_target="tpu_custom_call" | custom-call | tf_op jit(solution)/shard_map/collect7/pallas_call | solution.py:854
  1001.9 5.8 owner_back.1
  1007.7 23.0 %finish8.1 = (f32[16,128]{1,0:T(8,128)}, bf16[2,192,2048]{2,1,0:T(8,128)(2,1)}) custom-call(f32[4,4,16,128]{3,2,1,0:T(8,128)} %get-tuple-element.126.refs_0_, bf16[2,192,2048]{2,1,0:T(8,128)(2,1)} %get-tuple-element.127.refs_1_), custom_call_target="tpu_custom_call" | custom-call | tf_op jit(solution)/shard_map/finish8/pallas_call | solution.py:1016
  1030.7 1.3 slice_bitcast_fusion.2
  1032.1 1.3 slice_bitcast_fusion.4
  1033.3 1.5 convert_element_type.62
  1034.8 1.5 convert_element_type.63
  1036.3 9.6 unpack.1
  1045.9 1.3 slice_bitcast_fusion
  1047.2 1.2 convert_add_fusion
  (31 shorter events, 3.9 us)
Async XLA Ops:
  0.6 10.0 copy-start
  10.7 3.4 copy-start.5
  10.7 3.4 copy-start.6
  837.4 209.8 %collective-permute-start = (bf16[2,512,256]{2,1,0:T(8,128)(2,1)}, bf16[2,512,256]{2,1,0:T(8,128)(2,1)S(1)}, u32[]{:S(2)}, u32[]{:S(2)}) collective-permute-start(bf16[2,512,256]{2,1,0:T(8,128)(2,1)} %get-tuple-element.131), channel_id=1, source_target_pairs={{0,2},{2,4},{4,6},{6,0},{1,3},{3,5},{5,7},{7,1},{8,10},{10,12},{12... | collective-permute-start | bytes 1572872 | tf_op jit(solution)/shard_map/ppermute | solution.py:59
  856.0 191.2 %collective-permute-start.1 = (bf16[2,512,256]{2,1,0:T(8,128)(2,1)}, bf16[2,512,256]{2,1,0:T(8,128)(2,1)S(1)}, u32[]{:S(2)}, u32[]{:S(2)}) collective-permute-start(bf16[2,512,256]{2,1,0:T(8,128)(2,1)} %get-tuple-element.132), channel_id=1, source_target_pairs={{0,4},{2,6},{4,0},{6,2},{1,5},{3,7},{5,1},{7,3},{8,12},{10,14},{12... | collective-permute-start | bytes 1572872 | tf_op jit(solution)/shard_map/ppermute | solution.py:59
  856.0 191.2 %collective-permute-start.2 = (bf16[2,512,256]{2,1,0:T(8,128)(2,1)}, bf16[2,512,256]{2,1,0:T(8,128)(2,1)S(1)}, u32[]{:S(2)}, u32[]{:S(2)}) collective-permute-start(bf16[2,512,256]{2,1,0:T(8,128)(2,1)} %get-tuple-element.133), channel_id=1, source_target_pairs={{0,6},{2,0},{4,2},{6,4},{1,7},{3,1},{5,3},{7,5},{8,14},{10,8},{12,... | collective-permute-start | bytes 1572872 | tf_op jit(solution)/shard_map/ppermute | solution.py:59
  1007.7 25.6 %copy-start.3 = (bf16[4,512,256]{2,1,0:T(8,128)(2,1)S(1)}, bf16[4,512,256]{2,1,0:T(8,128)(2,1)}, u32[]{:S(2)}) copy-start(bf16[4,512,256]{2,1,0:T(8,128)(2,1)} %get-tuple-element.134) | copy-start | bytes 3145732
  1007.7 27.1 %copy-start.2 = (bf16[4,512,256]{2,1,0:T(8,128)(2,1)S(1)}, bf16[4,512,256]{2,1,0:T(8,128)(2,1)}, u32[]{:S(2)}) copy-start(bf16[4,512,256]{2,1,0:T(8,128)(2,1)} %get-tuple-element.135) | copy-start | bytes 3145732
  1036.3 9.6 copy-start.1
  1045.9 1.3 copy-start.4

commit v3 on v2

--- a/solution.py
+++ b/solution.py
@@ -55,10 +55,6 @@
     return pairs
 
 
-def ctx_shift(lay, array, shift):
-    return lax.ppermute(array, "ctx", [(c, (c + shift) % lay.nc) for c in range(lay.nc)])
-
-
 def collect_permute(lay, block_of, blocks, stride):
     got, last = [], None
     for j in range(blocks):
@@ -92,18 +88,23 @@
         return load
 
 
-def farthest_first(at, size):
+def by_gap(at, size, gaps):
     order = []
-    for gap in range(size - 1, 0, -1):
-        order += [(gap, at + gap < size), (size - gap, at - gap >= 0)]
-    return order
-
-
-def nearest_first(at, size):
-    order = []
-    for gap in range(1, size):
+    for gap in dict.fromkeys(gap for gap in gaps if gap > 0):
         order += [(gap, at - gap >= 0), (size - gap, at + gap < size)]
     return order
+
+
+def start_order(size):
+    return [size - 1, *range(1, size - 1)]
+
+
+def wait_order(size):
+    return [1, size - 1, *range(2, size - 1)] if size > 1 else []
+
+
+def ahead_by_gap(at, size):
+    return [(size - j, there) for j, there in by_gap(at, size, start_order(size))]
 
 
 class Load:
@@ -157,7 +158,7 @@
         if self.piece is None:
             self.to_core(0).start()
             return
-        for j, there in farthest_first(self.place[1], self.place[0]):
+        for j, there in ahead_by_gap(self.place[1], self.place[0]):
             pl.when(there)(lambda j=j: self.along_ctx(j).start())
         self.keep().start()
         if self.both:
@@ -166,7 +167,7 @@
     def pass_on(self):
         if self.piece is None:
             return
-        for j, there in nearest_first(self.place[1], self.place[0]):
+        for j, there in by_gap(self.place[1], self.place[0], wait_order(self.place[0])):
 
             @pl.when(there)
             def _():
@@ -648,17 +649,19 @@
 
     @pl.when(home)
     def _():
-        for j, there in farthest_first(c // stride, blocks):
+        for j, there in ahead_by_gap(c // stride, blocks):
             pl.when(there)(lambda j=j: along_ctx(j).start())
         for k in range(1, nf):
             in_plane(0, k).start()
         keep.start()
 
-    start_all(loads)
+    @pl.when(jnp.logical_not(home))
+    def _():
+        start_all(loads)
 
     @pl.when(home)
     def _():
-        for j, there in nearest_first(c // stride, blocks):
+        for j, there in by_gap(c // stride, blocks, wait_order(blocks)):
 
             @pl.when(there)
             def _():
@@ -666,6 +669,7 @@
                 for k in range(1, nf):
                     in_plane(j, k).start()
 
+        start_all(loads)
         keep.wait()
 
     for i in range(seqs):
@@ -796,7 +800,8 @@
                         outs[n][0, :, pl.ds(pl.multiple_of(s * wide, wide), wide)] = summed.astype(BF16)
                     else:
                         part[n, own, s, where] = summed.astype(BF16)
-                        to_owner(n, s, j).start()
+                for j, there in by_gap(c // stride, blocks, start_order(blocks)):
+                    pl.when(there)(lambda j=j: to_owner(n, s, j).start())
 
     @pl.when(home)
     def _():
@@ -1303,7 +1308,7 @@
 
 def attn_grads_body(lay_sizes, hauls, *refs):
     nf, nc, nt, seqs = lay_sizes
-    (x_ref, d_ref, g_ref, mixed_ref), outs, scratch, loads = hauls.split(refs, 4, 2 + lay_sizes[1])
+    (x_ref, d_ref, g_ref, mixed_ref), outs, scratch, loads = hauls.split(refs, 4, 4)
     kept, away, came = scratch[:3]
     copy = core_exchange(scratch[1:], nt)
     wide, half = away.shape[-2:]
@@ -1325,13 +1330,8 @@
     @pl.loop(0, nc)
     def _(s):
         copy(s).wait_recv()
-        outs[0][s] = (kept[s, 0] + came[s, 0].astype(F32)).astype(BF16)
-        outs[1][s] = (kept[s, 3] + came[s, 3].astype(F32)).astype(BF16)
-
-    for s, piece in enumerate(outs[2:]):
-        d = lax.rem(lax.axis_index("ctx") + s, nc)
-        for i in range(2):
-            piece[i] = (kept[d, 1 + i] + came[d, 1 + i].astype(F32)).astype(BF16)
+        for i in range(4):
+            outs[i][s] = (kept[s, i] + came[s, i].astype(F32)).astype(BF16)
 
     @pl.loop(0, nc)
     def _(s):
@@ -1348,10 +1348,8 @@
     return pl.pallas_call(
         functools.partial(attn_grads_body, lay.sizes, hauls),
         in_specs=[in_vmem] * 4 + hauls.in_specs,
-        out_specs=[in_vmem] * (2 + nc) + hauls.out_specs,
-        out_shape=[jax.ShapeDtypeStruct((nc,) + piece, BF16)] * 2
-        + [jax.ShapeDtypeStruct((2,) + piece, BF16)] * nc
-        + hauls.shapes,
+        out_specs=[in_vmem] * 4 + hauls.out_specs,
+        out_shape=[jax.ShapeDtypeStruct((nc,) + piece, BF16)] * 4 + hauls.shapes,
         scratch_shapes=[
             pltpu.VMEM((nc, 4) + piece, F32),
             pltpu.VMEM((nc, 4) + piece, BF16),
@@ -1833,7 +1831,7 @@
         11,
         [to_planes(up_b, by_piece)],
     )
-    q_grads, o_grads, *kv_pieces, down_a = attn_grads(
+    q_grads, k_grads, v_grads, o_grads, down_a = attn_grads(
         lay,
         normed_all.reshape(-1, width),
         dqkv.reshape(-1, 3 * heads),
@@ -1842,7 +1840,6 @@
         10,
         [to_planes(down_a, by_piece)],
     )
-    kv_back = [kv_pieces[0]] + [ctx_shift(lay, kv_pieces[s], s) for s in range(1, nc)]
     grad_one_rows, down_b, o_back, q_back = collect(
         lay,
         [dqkv[None]],
@@ -1873,7 +1870,9 @@
         layer_out,
         terms,
     )
-    terms, both_out = finish(lay, terms, both, 8)
+    terms, both_out, k_back, v_back = finish(
+        lay, terms, both, 8, [to_planes(grads, by_piece) for grads in (k_grads, v_grads)]
+    )
     layer_out, grad_tokens = both_out[0], both_out[1]
 
     def by_expert(came):
@@ -1883,7 +1882,7 @@
         return out
 
     grad_query_weight, grad_output_weight = by_expert(q_back), by_expert(o_back)
-    grad_kv_weight = functools.reduce(jnp.add, [piece.astype(F32) for piece in kv_back])
+    grad_kv_weight = jnp.stack([jnp.sum(g.astype(F32), axis=0) for g in (k_back, v_back)])
     grad_gate_up, grad_down = unpack(lay, gate_back, up_a, up_b, down_a, down_b)
     grad_gate_up, grad_down = grad_gate_up.swapaxes(-1, -2), grad_down.swapaxes(-1, -2)
     return (

time: 1050 us -> 1000 us (0.952)
  Pallas kernels: 1000 us -> 974 us
  starting transfers between devices: 21 us -> 0 us
    pallas_call x3, Pallas kernels: 417 us -> 346 us  [collect(): pl.pallas_call(functools.partial(collect_body, lay.sizes, stride, blocks,...]
    pallas_call x1, Pallas kernels: 23 us -> 51.2 us  [finish(): pl.pallas_call(functools.partial(finish_body, lay.sizes, hauls), out_shap...]
    ppermute x3 -> x0, starting transfers between devices: 21 us -> none  [ctx_shift(): lax.ppermute(array, 'ctx', [(c, (c + shift) % lay.nc) for c in range(lay....]
    pallas_call x1, Pallas kernels: 87.8 us -> 102 us  [attend(): pl.pallas_call(functools.partial(attend_body, lay.sizes, lay.rep, hauls),...]
  transfers between devices with their start and end apart: 3 -> 0, of which waited for: 0 -> 0; matrix products, arithmetic and copies ran while one was open for 1% -> 0% of each run, Pallas kernels for 17% -> 0%
where the time goes in v3:
time: 1000 us; the launch traced here: 998 us
  Pallas kernels  974 us (97%)
  other arithmetic  14.1 us (1%)
    pallas_call x3, Pallas kernels, collect(): pl.pallas_call(functools.partial(collect_body, lay.sizes, stride, blocks,...  346 us
    pallas_call x2, Pallas kernels, spread(): pl.pallas_call(functools.partial(spread_body, lay.sizes, stride, blocks,...  161 us
    pallas_call x1, Pallas kernels, opening(): pl.pallas_call(functools.partial(opening_body, lay.sizes, experts, hauls)...  115 us
    pallas_call x1, Pallas kernels, attend(): pl.pallas_call(functools.partial(attend_body, lay.sizes, lay.rep, hauls),...  102 us
    pallas_call x1, Pallas kernels, attend_back(): pl.pallas_call(functools.partial(attend_back_body, lay.sizes, hauls), gri...  51.9 us
    pallas_call x1, Pallas kernels, finish(): pl.pallas_call(functools.partial(finish_body, lay.sizes, hauls), out_shap...  51.2 us
    pallas_call x1, Pallas kernels, attn_grads(): pl.pallas_call(functools.partial(attn_grads_body, lay.sizes, hauls), in_s...  42.7 us
    pallas_call x1, Pallas kernels, experts_apply(): pl.pallas_call(functools.partial(experts_body, lay.rep, lay.experts), gri...  35.5 us

profile of v3, /device:TPU:0, one launch (start us, length us, event | category | flops | bytes accessed | tf_op | source)
XLA Modules:
  0.0 998.4 jit_solution(7164643823953506952)
XLA Ops:
  0.7 0.8 compare_reduce_fusion
  1.4 0.7 convert.6
  2.1 0.7 convert.7
  2.8 0.8 multiply_bitcast_fusion.1
  3.6 0.7 broadcast_in_dim.18
  4.3 0.7 broadcast_in_dim.19
  5.3 1.3 fusion.14.refs_1_
  7.4 1.0 convert_element_type.56.refs_9_.refs_7_
  8.4 2.2 fusion.1.refs_0_
  10.6 1.4 fusion.7
  12.0 1.2 pad_maximum_fusion.1
  13.2 2.2 convolution_convert_fusion.refs_2_
  15.4 115.5 %opening1.1 = (bf16[2,4,192,2176]{3,2,1,0:T(8,128)(2,1)}, bf16[4,16,512]{2,1,0:T(8,128)(2,1)}, bf16[4,144,1024]{2,1,0:T(8,128)(2,1)}, bf16[4,96,2176]{2,1,0:T(8,...) custom-call(bf16[192,2176]{1,0:T(8,128)(2,1)} %fusion.1.refs_0_, ...), custom_call_target="tpu_custom_call" | custom-call | tf_op jit(solution)/shard_map/opening1/pallas_call | solution.py:598
  130.9 102.0 %attend.1 = (bf16[2,768,2048]{2,1,0:T(8,128)(2,1)}, bf16[2,576,512]{2,1,0:T(8,128)(2,1)}, bf16[2,768,512]{2,1,0:T(8,128)(2,1)}, bf16[2,768,512]{2,1,0:T(8,128)(2...) custom-call(bf16[2,768,2176]{2,1,0:T(8,128)(2,1)} %bitcast.48, ...), custom_call_target="tpu_custom_call" | custom-call | tf_op jit(solution)/shard_map/attend/pallas_call | solution.py:1163
  232.9 99.4 %collect2.1 = (bf16[4,144,2048]{2,1,0:T(8,128)(2,1)}, bf16[4,704,512]{2,1,0:T(8,128)(2,1)}, bf16[4,704,512]{2,1,0:T(8,128)(2,1)}) custom-call(bf16[1,2,576,512]{3,2,1,0:T(8,128)(2,1)} %bitcast.64, bf16[4,512,256]{2,1,0:T(8,128)(2,1)} %get-tuple-element.88.refs_1_.refs_4_, bf16[4,512,256]{2,1,0:T(8,128)(2,1)} %get-tuple-element.89.refs_2_.refs_5_, ...), custom_call_target="tpu_custom_call" | custom-call | tf_op jit(solution)/shard_map/collect2/pallas_call | solution.py:859
  332.4 6.6 owner_forward.1
  338.9 93.9 %spread3.1 = (bf16[2,4,144,2048]{3,2,1,0:T(8,128)(2,1)}, bf16[4,704,512]{2,1,0:T(8,128)(2,1)}, bf16[4,704,512]{2,1,0:T(8,128)(2,1)}) custom-call(bf16[4,144,2048]{2,1,0:T(8,128)(2,1)} %bitcast.71, bf16[4,704,512]{2,1,0:T(8,128)(2,1)} %bitcast.68), custom_call_target="tpu_custom_call" | custom-call | tf_op jit(solution)/shard_map/spread3/pallas_call | solution.py:705
  432.9 35.5 %experts.1 = (bf16[2,576,2048]{2,1,0:T(8,128)(2,1)}, bf16[2,2,576,704]{3,2,1,0:T(8,128)(2,1)}, bf16[2,2,576,704]{3,2,1,0:T(8,128)(2,1)}, bf16[2,2,576,704]{3,2,1,0:T(8,128)(2,1)}) custom-call(bf16[2,576,2048]{2,1,0:T(8,128)(2,1)} %bitcast.56, bf16[2,576,2048]{2,1,0:T(8,128)(2,1)} %bitcast.67, bf16[4,16,512]{2,1,0:T(8,128)(2,1)} %get-tuple-element.77.refs_2_.small_ref, ...), custom_call_target="tpu_custom_call" | custom-call | tf_op jit(solution)/shard_map/experts/pallas_call | solution.py:1213
  468.3 34.8 %mlp_grads.1 = (bf16[4,704,512]{2,1,0:T(8,128)(2,1)}, bf16[4,352,512]{2,1,0:T(8,128)(2,1)}, bf16[4,352,512]{2,1,0:T(8,128)(2,1)}, bf16[4,352,512]{2,1,0:T(8,128)(2,1)}, bf16[4,352,512]{2,1,0:T(8,128)(2,1)}) custom-call(bf16[1152,2048]{1,0:T(8,128)(2,1)} %bitcast.57, bf16[1152,2048]{1,0:T(8,128)(2,1)} %bitcast.66, bf16[2,1152,704]{2,1,0:T(8,128)(2,1)} %bitcast.58, ...), custom_call_target="tpu_custom_call" | custom-call | tf_op jit(solution)/shard_map/mlp_grads/pallas_call | solution.py:1293
  503.2 127.1 %collect5.1 = (bf16[4,144,2048]{2,1,0:T(8,128)(2,1)}, bf16[4,144,2048]{2,1,0:T(8,128)(2,1)}, bf16[4,704,512]{2,1,0:T(8,128)(2,1)}) custom-call(bf16[2,2,576,704]{3,2,1,0:T(8,128)(2,1)} %get-tuple-element.102.refs_0_, bf16[2,2,576,704]{3,2,1,0:T(8,128)(2,1)} %get-tuple-element.103.refs_1_, bf16[2,2,576,704]{3,2,1,0:T(8,128)(2,1)} %get-tuple-element.104.refs_2_, ...), custom_call_target="tpu_custom_call" | custom-call | tf_op jit(solution)/shard_map/collect5/pallas_call | solution.py:859
  630.3 12.3 %owner_middle.1 = (bf16[192,2048]{1,0:T(8,128)(2,1)}, f32[192,2048]{1,0:T(8,128)}, bf16[576,2048]{1,0:T(8,128)(2,1)}, f32[192,128]{1,0:T(8,128)}, f32[16,2048]{1,0:T(8,128)}) custom-call(bf16[192,2048]{1,0:T(8,128)(2,1)} %x_ref.3, f32[192,4]{1,0:T(8,128)} %convert_element_type.51.ids_ref.refs_1_, bf16[4,16,512]{2,1,0:T(8,128)(2,1)} %get-tuple-element.77.refs_2_.small_ref, ...), custom_call_target="tpu_custom_call" | custom-call | tf_op jit(solution)/shard_map/owner_middle/pallas_call | solution.py:1620
  642.6 66.9 %spread6.1 = (bf16[2,4,144,2048]{3,2,1,0:T(8,128)(2,1)}, bf16[4,352,512]{2,1,0:T(8,128)(2,1)}) custom-call(bf16[4,144,2048]{2,1,0:T(8,128)(2,1)} %bitcast.72, bf16[4,352,512]{2,1,0:T(8,128)(2,1)} %get-tuple-element.110.refs_1_), custom_call_target="tpu_custom_call" | custom-call | tf_op jit(solution)/shard_map/spread6/pallas_call | solution.py:705
  709.5 51.9 %attend_back.1 = (bf16[2,768,1536]{2,1,0:T(8,128)(2,1)}, bf16[4,352,512]{2,1,0:T(8,128)(2,1)}) custom-call(bf16[2,576,512]{2,1,0:T(8,128)(2,1)} %get-tuple-element.84.refs_0_, bf16[2,768,512]{2,1,0:T(8,128)(2,1)} %get-tuple-element.85.refs_1_, bf16[2,768,512]{2,1,0:T(8,128)(2,1)} %get-tuple-element.86.refs_2_, bf16[2,576,2048]{2,1,0:T(8,128)(2,1)} %bitcast.54, ...), custom_call_target="tpu_custom_call" | custom-call | tf_op jit(solution)/shard_map/attend_back/pallas_call | solution.py:1417
  761.4 42.7 %attn_grads.1 = (bf16[4,512,256]{2,1,0:T(8,128)(2,1)}, bf16[4,512,256]{2,1,0:T(8,128)(2,1)}, bf16[4,512,256]{2,1,0:T(8,128)(2,1)}, bf16[4,512,256]{2,1,0:T(8,128)(2,1)}, bf16[4,352,512]{2,1,0:T(8,128)(2,1)}) custom-call(bf16[1536,2048]{1,0:T(8,128)(2,1)} %bitcast.63, bf16[1536,1536]{1,0:T(8,128)(2,1)} %bitcast.52, bf16[1152,2048]{1,0:T(8,128)(2,1)} %bitcast.55, ...), custom_call_target="tpu_custom_call" | custom-call | tf_op jit(solution)/shard_map/attn_grads/pallas_call | solution.py:1348
  804.1 119.1 %collect7.1 = (bf16[4,192,2048]{2,1,0:T(8,128)(2,1)}, bf16[4,352,512]{2,1,0:T(8,128)(2,1)}, bf16[4,512,256]{2,1,0:T(8,128)(2,1)}, bf16[4,512,256]{2,1,0:T(8,128)(2,1)}) custom-call(bf16[1,2,768,1536]{3,2,1,0:T(8,128)(2,1)} %bitcast.53, bf16[4,512,256]{2,1,0:T(8,128)(2,1)} %get-tuple-element.79.refs_3_.refs_1_, ...), custom_call_target="tpu_custom_call" | custom-call | tf_op jit(solution)/shard_map/collect7/pallas_call | solution.py:859
  923.1 5.8 owner_back.1
  928.9 51.2 %finish8.1 = (f32[16,128]{1,0:T(8,128)}, bf16[2,192,2048]{2,1,0:T(8,128)(2,1)}, bf16[4,512,256]{2,1,0:T(8,128)(2,1)}, bf16[4,512,256]{2,1,0:T(8,128)(2,1)}) custom-call(f32[4,4,16,128]{3,2,1,0:T(8,128)} %get-tuple-element.126.refs_0_, bf16[2,192,2048]{2,1,0:T(8,128)(2,1)} %get-tuple-element.127.refs_1_, bf16[4,512,256]{2,1,0:T(8,128)(2,1)} %get-tuple-element.128.refs_2_, ...), custom_call_target="tpu_custom_call" | custom-call | tf_op jit(solution)/shard_map/finish8/pallas_call | solution.py:1021
  980.2 2.8 slice_bitcast_fusion
  984.4 1.0 pad_maximum_fusion
  985.5 1.5 convert_element_type.54
  987.0 1.5 convert_element_type.55
  988.5 9.4 unpack.1
  (25 shorter events, 2.5 us)
Async XLA Ops:
  8.4 4.8 copy-start
  980.1 2.9 copy-start.5
  980.1 4.0 copy-start.4
  980.2 4.1 copy-start.3
  984.1 1.4 copy-start.2
  984.4 2.6 copy-start.1

commit v4 on v3

--- a/solution.py
+++ b/solution.py
@@ -767,8 +767,13 @@
             slot = lax.rem(own + 1 + i // nc, seqs)
             acc = None
             for which, lead, first, size, weight, row in terms:
-                right = rights[weight][s] if row is None else rights[weight][s, row]
-                term = dot(lefts[which][lead, slot, :, first : first + size], right, dims)
+                left = lefts[which][lead, slot, :, first : first + size]
+                if isinstance(weight, tuple):
+                    halves = [dot(left, rights[half][s], dims) for half in weight]
+                    term = jnp.concatenate(halves, axis=1)
+                else:
+                    right = rights[weight][s] if row is None else rights[weight][s, row]
+                    term = dot(left, right, dims)
                 acc = term if acc is None else acc + term
             part[n, slot, s] = acc.astype(BF16)
 
@@ -841,10 +846,14 @@
                 here = lax.optimization_barrier((here, last))[0]
             partial = 0.0
             for which, lead, first, size, weight, row in terms:
+                if isinstance(weight, tuple):
+                    right = jnp.concatenate([rights[half] for half in weight], axis=-1)
+                else:
+                    right = rights[weight] if row is None else rights[weight][:, row]
                 partial = partial + jnp.einsum(
                     "srh,pdh->srpd" if dims == NT else "srh,phd->srpd",
                     here[which][lead, :, :, first : first + size],
-                    rights[weight] if row is None else rights[weight][:, row],
+                    right,
                     preferred_element_type=F32,
                 )
             return partial.astype(BF16).reshape(seqs, rows, width)
@@ -1182,50 +1191,78 @@
     )(x, x, small, *weights, cosine, sine, pos, *hauls.operands)
 
 
-def experts_body(rep, experts, n_ref, g_ref, small_ref, other_ref, *refs):
-    weights, (ge_ref, hidden_ref, gate_ref, up_ref) = refs[:6], refs[6:]
+def experts_body(lay_sizes, rep, experts, hauls, *refs):
+    nf, nc, nt, seqs = lay_sizes
+    ins, outs, scratch, loads = hauls.split(refs, 10, 4)
+    n_ref, g_ref, small_ref, other_ref, gate0, up0, gate1, up1, down0, down1 = ins
+    ge_ref, hidden_ref, gate_ref, up_ref = outs
+    late, late_sem = scratch
+    greet(nf, nc, nt)
+    start_all(loads)
     c = lax.axis_index("ctx")
     lanes = lax.broadcasted_iota(jnp.int32, (1, small_ref.shape[1]), 1) - (2 + experts)
-    logits = chunk_dot(n_ref.at[0], small_ref, None, NT)
-    mine = jnp.sum(jnp.where(lanes == c // rep, logits, 0.0), axis=-1, keepdims=True)
-    theirs = jnp.where(lanes.astype(F32) == other_ref[0], logits, 0.0)
-    theirs = jnp.sum(theirs, axis=-1, keepdims=True)
-    ge_ref[0] = (jax.nn.sigmoid(mine - theirs) * g_ref[0].astype(F32)).astype(BF16)
-    for side in range(2):
-        gate_weight, up_weight, down_weight = weights[side::2]
-        gate_pre = chunk_dot(n_ref.at[0], gate_weight, None, NT)
-        up_pre = chunk_dot(n_ref.at[0], up_weight, None, NT)
-        grad_hidden = chunk_dot(ge_ref.at[0], down_weight, None, NT)
-        sigmoid_gate = jax.nn.sigmoid(gate_pre)
-        silu_gate = gate_pre * sigmoid_gate
-        hidden_ref[side, 0] = (silu_gate * up_pre).astype(BF16)
-        silu_slope = sigmoid_gate + silu_gate * (1.0 - sigmoid_gate)
-        gate_ref[side, 0] = (grad_hidden * up_pre * silu_slope).astype(BF16)
-        up_ref[side, 0] = (grad_hidden * silu_gate).astype(BF16)
-
-
-def experts_apply(lay, n2, g, small, other, *weights):
+
+    @pl.loop(0, seqs)
+    def _(slot):
+        logits = chunk_dot(n_ref.at[slot], small_ref, None, NT)
+        mine = jnp.sum(jnp.where(lanes == c // rep, logits, 0.0), axis=-1, keepdims=True)
+        theirs = jnp.where(lanes.astype(F32) == other_ref[slot], logits, 0.0)
+        theirs = jnp.sum(theirs, axis=-1, keepdims=True)
+        ge_ref[slot] = (jax.nn.sigmoid(mine - theirs) * g_ref[slot].astype(F32)).astype(BF16)
+        for side, (gate_weight, up_weight) in enumerate(((gate0, up0), (gate1, up1))):
+            gate_pre = chunk_dot(n_ref.at[slot], gate_weight, None, NT)
+            up_pre = chunk_dot(n_ref.at[slot], up_weight, None, NT)
+            sigmoid_gate = jax.nn.sigmoid(gate_pre)
+            silu_gate = gate_pre * sigmoid_gate
+            silu_slope = sigmoid_gate + silu_gate * (1.0 - sigmoid_gate)
+            hidden_ref[side, slot] = (silu_gate * up_pre).astype(BF16)
+            gate_ref[side, slot] = (up_pre * silu_slope).astype(BF16)
+            up_ref[side, slot] = silu_gate.astype(BF16)
+
+    finish_all(loads)
+    copies = [
+        pltpu.make_async_copy(loads[0].outs[side], late.at[side], late_sem.at[side])
+        for side in range(2)
+    ]
+    for copy in copies:
+        copy.start()
+    for copy in copies:
+        copy.wait()
+    half = late.shape[-1]
+
+    @pl.loop(0, seqs)
+    def _(slot):
+        for side, early in enumerate((down0, down1)):
+            grad_hidden = 0.0
+            for s in range(nc):
+                for at, weight in ((0, early[s]), (half, late[side, s])):
+                    first = 2 * half * s + at
+                    term = dot(ge_ref[slot, :, first : first + half], weight, NT)
+                    grad_hidden = grad_hidden + term
+            gate_ref[side, slot] = (grad_hidden * gate_ref[side, slot].astype(F32)).astype(BF16)
+            up_ref[side, slot] = (grad_hidden * up_ref[side, slot].astype(F32)).astype(BF16)
+
+
+def experts_apply(lay, n2, g, small, other, weights, call_id, haul):
     seqs, count, width = n2.shape
     ff = weights[0].shape[-2]
-    per_seq = lambda i: (i, 0, 0)
-    once = pl.Buffered(1)
-    wide = pl.BlockSpec((2, 1, count, ff), lambda i: (0, i, 0, 0))
+    hauls = Hauls(lay, [haul])
+    in_vmem = pl.BlockSpec(memory_space=pltpu.VMEM)
     return pl.pallas_call(
-        functools.partial(experts_body, lay.rep, lay.experts),
-        grid=(seqs,),
-        in_specs=[
-            pl.BlockSpec((1, count, width), per_seq),
-            pl.BlockSpec((1, count, width), per_seq),
-            pl.BlockSpec(small.shape, lambda i: (0, 0, 0)),
-            pl.BlockSpec((1, count, 1), per_seq),
+        functools.partial(experts_body, lay.sizes, lay.rep, lay.experts, hauls),
+        in_specs=[in_vmem] * 10 + hauls.in_specs,
+        out_specs=[in_vmem] * 4 + hauls.out_specs,
+        out_shape=[jax.ShapeDtypeStruct(n2.shape, BF16)]
+        + [jax.ShapeDtypeStruct((2, seqs, count, ff), BF16)] * 3
+        + hauls.shapes,
+        scratch_shapes=[
+            pltpu.VMEM((2,) + hauls.shapes[0].shape, BF16),
+            pltpu.SemaphoreType.DMA((2,)),
         ]
-        + [pl.BlockSpec(w.shape, lambda i: (0, 0, 0), pipeline_mode=once) for w in weights],
-        out_specs=[pl.BlockSpec((1, count, width), per_seq), wide, wide, wide],
-        out_shape=[jax.ShapeDtypeStruct(n2.shape, BF16)]
-        + [jax.ShapeDtypeStruct((2, seqs, count, ff), BF16)] * 3,
-        compiler_params=pltpu.CompilerParams(vmem_limit_bytes=VMEM_LIMIT),
+        + hauls.scratch,
+        compiler_params=params(call_id),
         name="experts",
-    )(n2, g, small, other, *weights)
+    )(n2, g, small, other, *weights, *hauls.operands)
 
 
 def core_exchange(refs, nt):
@@ -1252,10 +1289,9 @@
 
 
 def mlp_grads_body(nc, nt, n_ref, ge_ref, hidden_ref, gate_ref, up_ref, *refs):
-    outs, (away, came) = refs[:5], refs[5:7]
-    copy = core_exchange(refs[5:], nt)
-    wide = away.shape[-1]
-    half = outs[1].shape[1]
+    out, (away, came) = refs[0], refs[1:3]
+    copy = core_exchange(refs[1:], nt)
+    ff, wide = away.shape[-2:]
     pairs = ((gate_ref, n_ref), (up_ref, n_ref), (hidden_ref, ge_ref))
     greet_core(nt)
 
@@ -1272,12 +1308,7 @@
         copy(s).wait_recv()
         for i, (left, right) in enumerate(pairs):
             own = dot(left[0], right[:, columns], TN)
-            grad = (own + came[s, i].astype(F32)).astype(BF16)
-            if i == 0:
-                outs[0][s] = grad
-            else:
-                outs[2 * i - 1][s] = grad[:half]
-                outs[2 * i][s] = grad[half:]
+            out[s, i * ff : (i + 1) * ff] = (own + came[s, i].astype(F32)).astype(BF16)
 
     @pl.loop(0, nc)
     def _(s):
@@ -1288,13 +1319,11 @@
     width, ff, nc = n2.shape[1], hidden.shape[-1], lay.nc
     piece = (3, ff, width // nc)
     in_vmem = pl.BlockSpec(memory_space=pltpu.VMEM)
-    whole = jax.ShapeDtypeStruct((nc, ff, width // nc), BF16)
-    half = jax.ShapeDtypeStruct((nc, ff // 2, width // nc), BF16)
     return pl.pallas_call(
         functools.partial(mlp_grads_body, nc, lay.nt),
         in_specs=[in_vmem] * 5,
-        out_specs=[in_vmem] * 5,
-        out_shape=[whole] + [half] * 4,
+        out_specs=in_vmem,
+        out_shape=jax.ShapeDtypeStruct((nc, 3 * ff, width // nc), BF16),
         scratch_shapes=[
             pltpu.VMEM((nc,) + piece, BF16),
             pltpu.VMEM((nc,) + piece, BF16),
@@ -1439,24 +1468,25 @@
     )(q, k, v, g, *weights, qpos, kpos, cosine, sine, put, *hauls.operands)
 
 
-def unpack_body(gate, up_a, up_b, down_a, down_b, gate_up, down):
-    half = up_a.shape[1]
-
-    def total(ref):
-        return jnp.sum(ref[...].astype(F32), axis=0)
-
-    gate_up[0, 0] = total(gate)
-    gate_up[0, 1, 0:half] = total(up_a)
-    gate_up[0, 1, half:] = total(up_b)
-    down[0, 0:half] = total(down_a)
-    down[0, half:] = total(down_b)
-
-
-def unpack(lay, *parts):
-    ff, wide = parts[0].shape[1:]
+def unpack_body(bounds, *refs):
+    gate_up, down = refs[-2:]
+    ff = down.shape[1]
+    for part, first, last in zip(refs, bounds, bounds[1:]):
+        for i in range(3):
+            low, high = max(first, i * ff), min(last, (i + 1) * ff)
+            if low < high:
+                total = jnp.sum(part[:, low - first : high - first].astype(F32), axis=0)
+                if i < 2:
+                    gate_up[0, i, low - i * ff : high - i * ff] = total
+                else:
+                    down[0, low - i * ff : high - i * ff] = total
+
+
+def unpack(lay, parts, bounds):
+    ff, wide = bounds[-1] // 3, parts[0].shape[2]
     experts, rep = lay.experts, lay.rep
     return pl.pallas_call(
-        unpack_body,
+        functools.partial(unpack_body, bounds),
         grid=(experts,),
         in_specs=[pl.BlockSpec((rep,) + p.shape[1:], lambda e: (e, 0, 0)) for p in parts],
         out_specs=[
@@ -1749,49 +1779,64 @@
         branch_rows,
     )
 
-    n2, down_own, down_sib = spread(
+    wide, ff = width // nc, down_turned.shape[1]
+
+    def down_columns(half):
+        columns = pl.ds(half * (wide // 2), wide // 2)
+        return Haul(
+            down_turned, lambda ref, d: ref.at[d // rep, :, columns], (ff, wide // 2), True
+        )
+
+    n2, first_own, first_sib = spread(
         lay,
         n2_own.reshape(experts, cap, width),
         rep,
         3,
-        [to_planes(down_turned, by_plane(), True)],
+        [down_columns(0)],
     )
     n2 = n2.reshape(seqs, experts * cap, width)
-    grad_expert, hidden, grad_gate, grad_up = experts_apply(
+    grad_expert, hidden, grad_gate, grad_up, second_own, second_sib = experts_apply(
         lay,
         n2,
         g_blocks,
         small_all,
         other,
-        gate_own,
-        gate_sib,
-        up_own,
-        up_sib,
-        down_own,
-        down_sib,
+        [gate_own, up_own, gate_sib, up_sib, first_own, first_sib],
+        12,
+        down_columns(1),
     )
-    ff = hidden.shape[-1]
-    gate_grads, up_a, up_b, down_a, down_b = mlp_grads(
+    mlp_back = mlp_grads(
         lay,
         n2.reshape(-1, width),
         grad_expert.reshape(-1, width),
         *(a.reshape(2, -1, ff) for a in (hidden, grad_gate, grad_up)),
         4,
     )
+    shares = (480, 352, 432, 464, 384)
+    bounds = [0]
+    for share in shares:
+        bounds.append(bounds[-1] + share)
+    bounds = [3 * ff * bound // bounds[-1] // 16 * 16 for bound in bounds]
+
+    def carried(n):
+        first, last = bounds[n : n + 2]
+        rows_of = lambda ref, d: ref.at[d, pl.ds(first, last - first)]
+        return Haul(mlp_back, rows_of, (last - first, wide))
+
     by_piece = lambda d: (d,)
-    expert_rows, grad_rows, gate_back = collect(
+    expert_rows, grad_rows, back_a = collect(
         lay,
         [hidden, grad_gate, grad_up],
-        [gate_own, up_own, down_own, gate_sib, up_sib, down_sib],
+        [gate_own, up_own, first_own, second_own, gate_sib, up_sib, first_sib, second_sib],
         [
-            tuple((0, side, 0, ff, 3 * side + 2, None) for side in range(2)),
-            tuple((1 + i, side, 0, ff, 3 * side + i, None) for side in range(2) for i in range(2)),
+            tuple((0, side, 0, ff, (4 * side + 2, 4 * side + 3), None) for side in range(2)),
+            tuple((1 + i, side, 0, ff, 4 * side + i, None) for side in range(2) for i in range(2)),
         ],
         rep,
         experts,
         5,
         NN,
-        [to_planes(gate_grads, by_piece)],
+        [carried(0)],
     )
     lines = -(-(2 + 2 * experts) // 16) * 16
     layer_out, grad_residual, gb_own, logits_one, terms = own_kernel(
@@ -1814,9 +1859,9 @@
         grad_rows.reshape(-1, width),
     )
 
-    gb, up_a = spread(lay, gb_own.reshape(experts, cap, width), rep, 6, [to_planes(up_a, by_piece)])
+    gb, back_b = spread(lay, gb_own.reshape(experts, cap, width), rep, 6, [carried(1)])
     gb = gb.reshape(seqs, experts * cap, width)
-    dqkv, up_b = attend_back(
+    dqkv, back_c = attend_back(
         lay,
         q,
         k,
@@ -1829,18 +1874,18 @@
         sine,
         put,
         11,
-        [to_planes(up_b, by_piece)],
+        [carried(2)],
     )
-    q_grads, k_grads, v_grads, o_grads, down_a = attn_grads(
+    q_grads, k_grads, v_grads, o_grads, back_d = attn_grads(
         lay,
         normed_all.reshape(-1, width),
         dqkv.reshape(-1, 3 * heads),
         gb.reshape(-1, width),
         mixed.reshape(-1, heads),
         10,
-        [to_planes(down_a, by_piece)],
+        [carried(3)],
     )
-    grad_one_rows, down_b, o_back, q_back = collect(
+    grad_one_rows, back_e, o_back, q_back = collect(
         lay,
         [dqkv[None]],
         [q_own, kv_own, q_sib, kv_sib],
@@ -1854,7 +1899,7 @@
         1,
         nc,
         7,
-        hauls=[to_planes(grads, by_piece) for grads in (down_b, o_grads, q_grads)],
+        hauls=[carried(4), to_planes(o_grads, by_piece), to_planes(q_grads, by_piece)],
         by_plane=True,
     )
 
@@ -1883,7 +1928,7 @@
 
     grad_query_weight, grad_output_weight = by_expert(q_back), by_expert(o_back)
     grad_kv_weight = jnp.stack([jnp.sum(g.astype(F32), axis=0) for g in (k_back, v_back)])
-    grad_gate_up, grad_down = unpack(lay, gate_back, up_a, up_b, down_a, down_b)
+    grad_gate_up, grad_down = unpack(lay, [back_a, back_b, back_c, back_d, back_e], bounds)
     grad_gate_up, grad_down = grad_gate_up.swapaxes(-1, -2), grad_down.swapaxes(-1, -2)
     return (
         layer_out,

time: 1000 us -> 1030 us (1.030)
  Pallas kernels: 974 us -> 1000 us
    pallas_call x2, Pallas kernels: 44.9 us -> 80 us  [the longest x1 70.6 us: experts_apply(): pl.pallas_call(functools.partial(experts_body, lay.sizes, lay.rep, lay.ex...]
    pallas_call x2, Pallas kernels: 161 us -> 133 us  [spread(): pl.pallas_call(functools.partial(spread_body, lay.sizes, stride, blocks,...]
where the time goes in v4:
time: 1030 us
  Pallas kernels  1000 us (97%)
  other arithmetic  14.1 us (1%)
    pallas_call x3, Pallas kernels, collect(): pl.pallas_call(functools.partial(collect_body, lay.sizes, stride, blocks,...  352 us
    pallas_call x2, Pallas kernels, spread(): pl.pallas_call(functools.partial(spread_body, lay.sizes, stride, blocks,...  133 us
    pallas_call x1, Pallas kernels, opening(): pl.pallas_call(functools.partial(opening_body, lay.sizes, experts, hauls)...  115 us
    pallas_call x1, Pallas kernels, attend(): pl.pallas_call(functools.partial(attend_body, lay.sizes, lay.rep, hauls),...  102 us
    pallas_call x1, Pallas kernels, experts_apply(): pl.pallas_call(functools.partial(experts_body, lay.sizes, lay.rep, lay.ex...  70.6 us
    pallas_call x1, Pallas kernels, attend_back(): pl.pallas_call(functools.partial(attend_back_body, lay.sizes, hauls), gri...  56.2 us
    pallas_call x1, Pallas kernels, finish(): pl.pallas_call(functools.partial(finish_body, lay.sizes, hauls), out_shap...  52.8 us
    pallas_call x1, Pallas kernels, attn_grads(): pl.pallas_call(functools.partial(attn_grads_body, lay.sizes, hauls), in_s...  51.4 us

profile of v4, /device:TPU:0, one launch (start us, length us, event | category | flops | bytes accessed | tf_op | source)
XLA Modules:
  0.0 1026.4 jit_solution(12863734753892071820)
XLA Ops:
  0.7 0.8 compare_reduce_fusion
  1.4 0.7 convert.6
  2.1 0.7 convert.7
  2.8 0.8 multiply_bitcast_fusion.1
  3.6 0.7 broadcast_in_dim.18
  4.3 0.7 broadcast_in_dim.19
  5.3 1.3 fusion.14.refs_1_
  7.4 1.0 convert_element_type.56.refs_9_.refs_7_
  8.4 2.2 fusion.1.refs_0_
  10.6 1.4 fusion.7
  12.1 1.2 pad_maximum_fusion.1
  13.2 2.2 convolution_convert_fusion.refs_2_
  15.4 115.5 %opening1.1 = (bf16[2,4,192,2176]{3,2,1,0:T(8,128)(2,1)}, bf16[4,16,512]{2,1,0:T(8,128)(2,1)}, bf16[4,144,1024]{2,1,0:T(8,128)(2,1)}, bf16[4,96,2176]{2,1,0:T(8,...) custom-call(bf16[192,2176]{1,0:T(8,128)(2,1)} %fusion.1.refs_0_, ...), custom_call_target="tpu_custom_call" | custom-call | tf_op jit(solution)/shard_map/opening1/pallas_call | solution.py:598
  130.9 102.1 %attend.1 = (bf16[2,768,2048]{2,1,0:T(8,128)(2,1)}, bf16[2,576,512]{2,1,0:T(8,128)(2,1)}, bf16[2,768,512]{2,1,0:T(8,128)(2,1)}, bf16[2,768,512]{2,1,0:T(8,128)(2...) custom-call(bf16[2,768,2176]{2,1,0:T(8,128)(2,1)} %bitcast.48, ...), custom_call_target="tpu_custom_call" | custom-call | tf_op jit(solution)/shard_map/attend/pallas_call | solution.py:1172
  232.9 99.3 %collect2.1 = (bf16[4,144,2048]{2,1,0:T(8,128)(2,1)}, bf16[4,704,512]{2,1,0:T(8,128)(2,1)}, bf16[4,704,512]{2,1,0:T(8,128)(2,1)}) custom-call(bf16[1,2,576,512]{3,2,1,0:T(8,128)(2,1)} %bitcast.66, bf16[4,512,256]{2,1,0:T(8,128)(2,1)} %get-tuple-element.85.refs_1_.refs_4_, bf16[4,512,256]{2,1,0:T(8,128)(2,1)} %get-tuple-element.86.refs_2_.refs_5_, ...), custom_call_target="tpu_custom_call" | custom-call | tf_op jit(solution)/shard_map/collect2/pallas_call | solution.py:868
  332.3 6.6 owner_forward.1
  338.8 68.6 %spread3.1 = (bf16[2,4,144,2048]{3,2,1,0:T(8,128)(2,1)}, bf16[4,704,256]{2,1,0:T(8,128)(2,1)}, bf16[4,704,256]{2,1,0:T(8,128)(2,1)}) custom-call(bf16[4,144,2048]{2,1,0:T(8,128)(2,1)} %bitcast.72, bf16[4,704,512]{2,1,0:T(8,128)(2,1)} %bitcast.61), custom_call_target="tpu_custom_call" | custom-call | tf_op jit(solution)/shard_map/spread3/pallas_call | solution.py:705
  407.5 70.6 %experts.1 = (bf16[2,576,2048]{2,1,0:T(8,128)(2,1)}, bf16[2,2,576,704]{3,2,1,0:T(8,128)(2,1)}, bf16[2,2,576,704]{3,2,1,0:T(8,128)(2,1)}, bf16[2,2,576,704]{3,2,1...) custom-call(bf16[2,576,2048]{2,1,0:T(8,128)(2,1)} %bitcast.52, ...), custom_call_target="tpu_custom_call" | custom-call | tf_op jit(solution)/shard_map/experts/pallas_call | solution.py:1251
  478.0 34.8 %mlp_grads.1.refs_11_.refs_1_.refs_4_.refs_5_ = bf16[4,2112,512]{2,1,0:T(8,128)(2,1)} custom-call(bf16[1152,2048]{1,0:T(8,128)(2,1)} %bitcast.53, bf16[1152,2048]{1,0:T(8,128)(2,1)} %bitcast.68, bf16[2,1152,704]{2,1,0:T(8,128)(2,1)} %bitcast.58, bf16[2,1152,704]{2,1,0:T(8,128)(2,1)} %bitcast.59, bf16[2,1152,704]{2,1,0:T(8,128)(2,1)} %bitcast.60), custom_call_target="tpu_custom_call" | custom-call | tf_op jit(solution)/shard_map/mlp_grads/pallas_call | solution.py:1322
  512.8 130.8 %collect5.1 = (bf16[4,144,2048]{2,1,0:T(8,128)(2,1)}, bf16[4,144,2048]{2,1,0:T(8,128)(2,1)}, bf16[4,480,512]{2,1,0:T(8,128)(2,1)}) custom-call(bf16[2,2,576,704]{3,2,1,0:T(8,128)(2,1)} %get-tuple-element.99.refs_0_, bf16[2,2,576,704]{3,2,1,0:T(8,128)(2,1)} %get-tuple-element.100.refs_1_, bf16[2,2,576,704]{3,2,1,0:T(8,128)(2,1)} %get-tuple-element.101.refs_2_, ...), custom_call_target="tpu_custom_call" | custom-call | tf_op jit(solution)/shard_map/collect5/pallas_call | solution.py:868
  643.6 12.3 %owner_middle.1 = (bf16[192,2048]{1,0:T(8,128)(2,1)}, f32[192,2048]{1,0:T(8,128)}, bf16[576,2048]{1,0:T(8,128)(2,1)}, f32[192,128]{1,0:T(8,128)}, f32[16,2048]{1,0:T(8,128)}) custom-call(bf16[192,2048]{1,0:T(8,128)(2,1)} %x_ref.3, f32[192,4]{1,0:T(8,128)} %convert_element_type.51.ids_ref.refs_1_, bf16[4,16,512]{2,1,0:T(8,128)(2,1)} %get-tuple-element.74.refs_2_.small_ref, ...), custom_call_target="tpu_custom_call" | custom-call | tf_op jit(solution)/shard_map/owner_middle/pallas_call | solution.py:1650
  655.9 64.1 %spread6.1 = (bf16[2,4,144,2048]{3,2,1,0:T(8,128)(2,1)}, bf16[4,352,512]{2,1,0:T(8,128)(2,1)}) custom-call(bf16[4,144,2048]{2,1,0:T(8,128)(2,1)} %bitcast.73, bf16[4,2112,512]{2,1,0:T(8,128)(2,1)} %mlp_grads.1.refs_11_.refs_1_.refs_4_.refs_5_), custom_call_target="tpu_custom_call" | custom-call | tf_op jit(solution)/shard_map/spread6/pallas_call | solution.py:705
  720.0 56.2 %attend_back.1 = (bf16[2,768,1536]{2,1,0:T(8,128)(2,1)}, bf16[4,432,512]{2,1,0:T(8,128)(2,1)}) custom-call(bf16[2,576,512]{2,1,0:T(8,128)(2,1)} %get-tuple-element.81.refs_0_, bf16[2,768,512]{2,1,0:T(8,128)(2,1)} %get-tuple-element.82.refs_1_, bf16[2,768,512]{2,1,0:T(8,128)(2,1)} %get-tuple-element.83.refs_2_, bf16[2,576,2048]{2,1,0:T(8,128)(2,1)} %bitcast.56, ...), custom_call_target="tpu_custom_call" | custom-call | tf_op jit(solution)/shard_map/attend_back/pallas_call | solution.py:1446
  776.2 51.4 %attn_grads.1 = (bf16[4,512,256]{2,1,0:T(8,128)(2,1)}, bf16[4,512,256]{2,1,0:T(8,128)(2,1)}, bf16[4,512,256]{2,1,0:T(8,128)(2,1)}, bf16[4,512,256]{2,1,0:T(8,128)(2,1)}, bf16[4,464,512]{2,1,0:T(8,128)(2,1)}) custom-call(bf16[1536,2048]{1,0:T(8,128)(2,1)} %bitcast.65, bf16[1536,1536]{1,0:T(8,128)(2,1)} %bitcast.54, bf16[1152,2048]{1,0:T(8,128)(2,1)} %bitcast.57, ...), custom_call_target="tpu_custom_call" | custom-call | tf_op jit(solution)/shard_map/attn_grads/pallas_call | solution.py:1377
  827.6 121.8 %collect7.1 = (bf16[4,192,2048]{2,1,0:T(8,128)(2,1)}, bf16[4,384,512]{2,1,0:T(8,128)(2,1)}, bf16[4,512,256]{2,1,0:T(8,128)(2,1)}, bf16[4,512,256]{2,1,0:T(8,128)(2,1)}) custom-call(bf16[1,2,768,1536]{3,2,1,0:T(8,128)(2,1)} %bitcast.55, bf16[4,512,256]{2,1,0:T(8,128)(2,1)} %get-tuple-element.76.refs_3_.refs_1_, ...), custom_call_target="tpu_custom_call" | custom-call | tf_op jit(solution)/shard_map/collect7/pallas_call | solution.py:868
  949.4 5.8 owner_back.1
  955.1 52.8 %finish8.1 = (f32[16,128]{1,0:T(8,128)}, bf16[2,192,2048]{2,1,0:T(8,128)(2,1)}, bf16[4,512,256]{2,1,0:T(8,128)(2,1)}, bf16[4,512,256]{2,1,0:T(8,128)(2,1)}) custom-call(f32[4,4,16,128]{3,2,1,0:T(8,128)} %get-tuple-element.120.refs_0_, bf16[2,192,2048]{2,1,0:T(8,128)(2,1)} %get-tuple-element.121.refs_1_, bf16[4,512,256]{2,1,0:T(8,128)(2,1)} %get-tuple-element.122.refs_2_, ...), custom_call_target="tpu_custom_call" | custom-call | tf_op jit(solution)/shard_map/finish8/pallas_call | solution.py:1030
  1008.0 2.8 slice_bitcast_fusion
  1012.2 1.0 pad_maximum_fusion
  1013.5 1.5 convert_element_type.54
  1015.0 1.5 convert_element_type.55
  1016.5 9.4 unpack.1
  (25 shorter events, 2.7 us)
Async XLA Ops:
  8.4 4.8 copy-start
  1007.9 2.9 copy-start.5
  1008.0 4.0 copy-start.4
  1008.0 4.1 copy-start.3
  1012.1 1.4 copy-start.2
  1013.5 1.5 copy-start.1

commit v5 on v3

--- a/solution.py
+++ b/solution.py
@@ -1244,66 +1244,80 @@
     return copy
 
 
-def greet_core(nt):
-    barrier = pltpu.get_barrier_semaphore()
-    other = lax.rem(lax.axis_index("tp") + 1, nt)
-    pl.semaphore_signal(barrier, inc=1, device_id={"tp": other}, device_id_type=MESH)
-    pl.semaphore_wait(barrier, 1)
-
-
-def mlp_grads_body(nc, nt, n_ref, ge_ref, hidden_ref, gate_ref, up_ref, *refs):
-    outs, (away, came) = refs[:5], refs[5:7]
-    copy = core_exchange(refs[5:], nt)
-    wide = away.shape[-1]
-    half = outs[1].shape[1]
+def mlp_grads_body(lay_sizes, hauls, *refs):
+    nf, nc, nt, seqs = lay_sizes
+    ins, (out,), scratch, loads = hauls.split(refs, 5, 1)
+    n_ref, ge_ref, hidden_ref, gate_ref, up_ref = ins
+    away, came, send_sem, recv_sem = scratch
+    ff, wide = away.shape[-2:]
     pairs = ((gate_ref, n_ref), (up_ref, n_ref), (hidden_ref, ge_ref))
-    greet_core(nt)
-
-    @pl.loop(0, nc)
-    def _(s):
-        columns = pl.ds(pl.multiple_of(s * wide, wide), wide)
-        for i, (left, right) in enumerate(pairs):
-            away[s, i] = dot(left[1], right[:, columns], TN).astype(BF16)
-        copy(s).start()
-
-    @pl.loop(0, nc)
-    def _(s):
-        columns = pl.ds(pl.multiple_of(s * wide, wide), wide)
-        copy(s).wait_recv()
-        for i, (left, right) in enumerate(pairs):
-            own = dot(left[0], right[:, columns], TN)
-            grad = (own + came[s, i].astype(F32)).astype(BF16)
-            if i == 0:
-                outs[0][s] = grad
-            else:
-                outs[2 * i - 1][s] = grad[:half]
-                outs[2 * i][s] = grad[half:]
-
-    @pl.loop(0, nc)
-    def _(s):
-        copy(s).wait_send()
-
-
-def mlp_grads(lay, n2, ge, hidden, gate, up, call_id):
+    greet(nf, nc, nt)
+
+    def copy(first, last, s):
+        group = pl.ds(first, last - first)
+        return pltpu.make_async_remote_copy(
+            src_ref=away.at[s, group],
+            dst_ref=came.at[s, group],
+            send_sem=send_sem.at[min(first, 1), s],
+            recv_sem=recv_sem.at[min(first, 1), s],
+            device_id={"tp": lax.rem(lax.axis_index("tp") + 1, nt)},
+            device_id_type=MESH,
+        )
+
+    for first, last in ((0, 1), (1, 3)):
+
+        @pl.loop(0, nc)
+        def _(s):
+            columns = pl.ds(pl.multiple_of(s * wide, wide), wide)
+            for i in range(first, last):
+                left, right = pairs[i]
+                away[s, i] = dot(left[1], right[:, columns], TN).astype(BF16)
+            copy(first, last, s).start()
+
+        @pl.loop(0, nc)
+        def _(s):
+            columns = pl.ds(pl.multiple_of(s * wide, wide), wide)
+            copy(first, last, s).wait_recv()
+            for i in range(first, last):
+                left, right = pairs[i]
+                own = dot(left[0], right[:, columns], TN)
+                out[s, i * ff : (i + 1) * ff] = (own + came[s, i].astype(F32)).astype(BF16)
+
+        if first == 0:
+            for load in loads:
+                load.src = out
+                load.start()
+
+    for first, last in ((0, 1), (1, 3)):
+
+        @pl.loop(0, nc)
+        def _(s):
+            copy(first, last, s).wait_send()
+
+    finish_all(loads)
+
+
+def mlp_grads(lay, n2, ge, hidden, gate, up, early, call_id):
     width, ff, nc = n2.shape[1], hidden.shape[-1], lay.nc
-    piece = (3, ff, width // nc)
+    wide = width // nc
+    piece = (3, ff, wide)
     in_vmem = pl.BlockSpec(memory_space=pltpu.VMEM)
-    whole = jax.ShapeDtypeStruct((nc, ff, width // nc), BF16)
-    half = jax.ShapeDtypeStruct((nc, ff // 2, width // nc), BF16)
+    hauls = Hauls(lay, [Haul(n2, lambda ref, d: ref.at[d, pl.ds(0, early)], (early, wide))])
     return pl.pallas_call(
-        functools.partial(mlp_grads_body, nc, lay.nt),
-        in_specs=[in_vmem] * 5,
-        out_specs=[in_vmem] * 5,
-        out_shape=[whole] + [half] * 4,
+        functools.partial(mlp_grads_body, lay.sizes, hauls),
+        in_specs=[in_vmem] * 5 + hauls.in_specs,
+        out_specs=[in_vmem] + hauls.out_specs,
+        out_shape=[jax.ShapeDtypeStruct((nc, 3 * ff, wide), BF16)] + hauls.shapes,
         scratch_shapes=[
             pltpu.VMEM((nc,) + piece, BF16),
             pltpu.VMEM((nc,) + piece, BF16),
-            pltpu.SemaphoreType.DMA((nc,)),
-            pltpu.SemaphoreType.DMA((nc,)),
-        ],
+            pltpu.SemaphoreType.DMA((2, nc)),
+            pltpu.SemaphoreType.DMA((2, nc)),
+        ]
+        + hauls.scratch,
         compiler_params=params(call_id),
         name="mlp_grads",
-    )(n2, ge, hidden, gate, up)
+    )(n2, ge, hidden, gate, up, *hauls.operands)
 
 
 def attn_grads_body(lay_sizes, hauls, *refs):
@@ -1439,37 +1453,65 @@
     )(q, k, v, g, *weights, qpos, kpos, cosine, sine, put, *hauls.operands)
 
 
-def unpack_body(gate, up_a, up_b, down_a, down_b, gate_up, down):
-    half = up_a.shape[1]
-
-    def total(ref):
-        return jnp.sum(ref[...].astype(F32), axis=0)
-
-    gate_up[0, 0] = total(gate)
-    gate_up[0, 1, 0:half] = total(up_a)
-    gate_up[0, 1, half:] = total(up_b)
-    down[0, 0:half] = total(down_a)
-    down[0, half:] = total(down_b)
-
-
-def unpack(lay, *parts):
-    ff, wide = parts[0].shape[1:]
+def unpack_body(bounds, *refs):
+    count = len(bounds) - 1
+    parts, attention = refs[:count], refs[count : count + 4]
+    gate_up, down, query, output, key_value = refs[count + 4 :]
+    ff = down.shape[1]
+
+    def total(ref, rows=slice(None)):
+        return jnp.sum(ref[:, rows].astype(F32), axis=0)
+
+    for part, first, last in zip(parts, bounds, bounds[1:]):
+        for i in range(3):
+            low, high = max(first, i * ff), min(last, (i + 1) * ff)
+            if low < high:
+                values = total(part, slice(low - first, high - first))
+                if i < 2:
+                    gate_up[0, i, low - i * ff : high - i * ff] = values
+                else:
+                    down[0, low - i * ff : high - i * ff] = values
+    query[0] = total(attention[0])
+    output[0] = total(attention[1])
+    for i in range(2):
+        values = total(attention[2 + i])
+
+        @pl.when(pl.program_id(0) == 0)
+        def _():
+            key_value[i] = values
+
+        @pl.when(pl.program_id(0) > 0)
+        def _():
+            key_value[i] = key_value[i] + values
+
+
+def unpack(lay, parts, bounds, attention):
+    ff, wide = bounds[-1] // 3, parts[0].shape[2]
     experts, rep = lay.experts, lay.rep
+    dims = attention[0].shape[1:]
+    per_expert = pl.BlockSpec((1,) + dims, lambda e: (e, 0, 0))
+    operands = [*parts, *attention]
     return pl.pallas_call(
-        unpack_body,
+        functools.partial(unpack_body, bounds),
         grid=(experts,),
-        in_specs=[pl.BlockSpec((rep,) + p.shape[1:], lambda e: (e, 0, 0)) for p in parts],
+        in_specs=[pl.BlockSpec((rep,) + p.shape[1:], lambda e: (e, 0, 0)) for p in operands],
         out_specs=[
             pl.BlockSpec((1, 2, ff, wide), lambda e: (e, 0, 0, 0)),
             pl.BlockSpec((1, ff, wide), lambda e: (e, 0, 0)),
+            per_expert,
+            per_expert,
+            pl.BlockSpec((2,) + dims, lambda e: (0, 0, 0)),
         ],
         out_shape=[
             jax.ShapeDtypeStruct((experts, 2, ff, wide), F32),
             jax.ShapeDtypeStruct((experts, ff, wide), F32),
+            jax.ShapeDtypeStruct((experts,) + dims, F32),
+            jax.ShapeDtypeStruct((experts,) + dims, F32),
+            jax.ShapeDtypeStruct((2,) + dims, F32),
         ],
         compiler_params=pltpu.CompilerParams(vmem_limit_bytes=VMEM_LIMIT),
         name="unpack",
-    )(*parts)
+    )(*operands)
 
 
 def row_of(small_ref, line):
@@ -1771,15 +1813,27 @@
         down_sib,
     )
     ff = hidden.shape[-1]
-    gate_grads, up_a, up_b, down_a, down_b = mlp_grads(
+    shares = (240, 704, 336, 320, 256, 256)
+    bounds = [0]
+    for share in shares:
+        bounds.append(bounds[-1] + share)
+    bounds = [3 * ff * bound // bounds[-1] // 16 * 16 for bound in bounds]
+    mlp_back, back_a = mlp_grads(
         lay,
         n2.reshape(-1, width),
         grad_expert.reshape(-1, width),
         *(a.reshape(2, -1, ff) for a in (hidden, grad_gate, grad_up)),
+        bounds[1],
         4,
     )
+
+    def carried(n):
+        first, last = bounds[n : n + 2]
+        rows_of = lambda ref, d: ref.at[d, pl.ds(first, last - first)]
+        return Haul(mlp_back, rows_of, (last - first, width // nc))
+
     by_piece = lambda d: (d,)
-    expert_rows, grad_rows, gate_back = collect(
+    expert_rows, grad_rows, back_b = collect(
         lay,
         [hidden, grad_gate, grad_up],
         [gate_own, up_own, down_own, gate_sib, up_sib, down_sib],
@@ -1791,7 +1845,7 @@
         experts,
         5,
         NN,
-        [to_planes(gate_grads, by_piece)],
+        [carried(1)],
     )
     lines = -(-(2 + 2 * experts) // 16) * 16
     layer_out, grad_residual, gb_own, logits_one, terms = own_kernel(
@@ -1814,9 +1868,9 @@
         grad_rows.reshape(-1, width),
     )
 
-    gb, up_a = spread(lay, gb_own.reshape(experts, cap, width), rep, 6, [to_planes(up_a, by_piece)])
+    gb, back_c = spread(lay, gb_own.reshape(experts, cap, width), rep, 6, [carried(2)])
     gb = gb.reshape(seqs, experts * cap, width)
-    dqkv, up_b = attend_back(
+    dqkv, back_d = attend_back(
         lay,
         q,
         k,
@@ -1829,18 +1883,18 @@
         sine,
         put,
         11,
-        [to_planes(up_b, by_piece)],
-    )
-    q_grads, k_grads, v_grads, o_grads, down_a = attn_grads(
+        [carried(3)],
+    )
+    q_grads, k_grads, v_grads, o_grads, back_e = attn_grads(
         lay,
         normed_all.reshape(-1, width),
         dqkv.reshape(-1, 3 * heads),
         gb.reshape(-1, width),
         mixed.reshape(-1, heads),
         10,
-        [to_planes(down_a, by_piece)],
-    )
-    grad_one_rows, down_b, o_back, q_back = collect(
+        [carried(4)],
+    )
+    grad_one_rows, back_f, o_back, q_back = collect(
         lay,
         [dqkv[None]],
         [q_own, kv_own, q_sib, kv_sib],
@@ -1854,7 +1908,7 @@
         1,
         nc,
         7,
-        hauls=[to_planes(grads, by_piece) for grads in (down_b, o_grads, q_grads)],
+        hauls=[carried(5), to_planes(o_grads, by_piece), to_planes(q_grads, by_piece)],
         by_plane=True,
     )
 
@@ -1875,15 +1929,12 @@
     )
     layer_out, grad_tokens = both_out[0], both_out[1]
 
-    def by_expert(came):
-        out = came.astype(F32)
-        if rep > 1:
-            out = jnp.sum(out.reshape((experts, rep) + out.shape[1:]), axis=1)
-        return out
-
-    grad_query_weight, grad_output_weight = by_expert(q_back), by_expert(o_back)
-    grad_kv_weight = jnp.stack([jnp.sum(g.astype(F32), axis=0) for g in (k_back, v_back)])
-    grad_gate_up, grad_down = unpack(lay, gate_back, up_a, up_b, down_a, down_b)
+    grad_gate_up, grad_down, grad_query_weight, grad_output_weight, grad_kv_weight = unpack(
+        lay,
+        [back_a, back_b, back_c, back_d, back_e, back_f],
+        bounds,
+        [q_back, o_back, k_back, v_back],
+    )
     grad_gate_up, grad_down = grad_gate_up.swapaxes(-1, -2), grad_down.swapaxes(-1, -2)
     return (
         layer_out,

time: 1000 us -> 989 us (0.989)
    pallas_call x2, Pallas kernels: 44.3 us -> 57.6 us  [the longest x1 44.6 us: mlp_grads(): pl.pallas_call(functools.partial(mlp_grads_body, lay.sizes, hauls), in_sp...]
where the time goes in v5:
time: 989 us; the launch traced here: 986 us
  Pallas kernels  966 us (98%)
    pallas_call x3, Pallas kernels, collect(): pl.pallas_call(functools.partial(collect_body, lay.sizes, stride, blocks,...  337 us
    pallas_call x2, Pallas kernels, spread(): pl.pallas_call(functools.partial(spread_body, lay.sizes, stride, blocks,...  160 us
    pallas_call x1, Pallas kernels, opening(): pl.pallas_call(functools.partial(opening_body, lay.sizes, experts, hauls)...  115 us
    pallas_call x1, Pallas kernels, attend(): pl.pallas_call(functools.partial(attend_body, lay.sizes, lay.rep, hauls),...  102 us
    pallas_call x1, Pallas kernels, finish(): pl.pallas_call(functools.partial(finish_body, lay.sizes, hauls), out_shap...  51.3 us
    pallas_call x1, Pallas kernels, attend_back(): pl.pallas_call(functools.partial(attend_back_body, lay.sizes, hauls), gri...  47.7 us
    pallas_call x1, Pallas kernels, mlp_grads(): pl.pallas_call(functools.partial(mlp_grads_body, lay.sizes, hauls), in_sp...  44.6 us
    pallas_call x1, Pallas kernels, experts_apply(): pl.pallas_call(functools.partial(experts_body, lay.rep, lay.experts), gri...  35.5 us

profile of v5, /device:TPU:0, one launch (start us, length us, event | category | flops | bytes accessed | tf_op | source)
XLA Modules:
  0.0 985.6 jit_solution(468318497180920505)
XLA Ops:
  0.7 0.8 compare_reduce_fusion
  1.4 0.7 convert.6
  2.1 0.7 convert.7
  2.8 0.8 multiply_bitcast_fusion.1
  3.6 0.7 broadcast_in_dim.18
  4.3 0.7 broadcast_in_dim.19
  5.3 1.3 fusion.14.refs_1_
  6.7 0.7 convert_element_type.39.ids_ref.refs_1_
  7.4 1.1 convert_element_type.40.refs_9_.refs_7_
  8.5 2.2 fusion.1.refs_0_
  10.6 1.4 fusion.7
  12.1 1.2 pad_maximum_fusion
  13.2 2.2 convolution_convert_fusion.refs_2_
  15.4 115.5 %opening1.1 = (bf16[2,4,192,2176]{3,2,1,0:T(8,128)(2,1)}, bf16[4,16,512]{2,1,0:T(8,128)(2,1)}, bf16[4,144,1024]{2,1,0:T(8,128)(2,1)}, bf16[4,96,2176]{2,1,0:T(8,...) custom-call(bf16[192,2176]{1,0:T(8,128)(2,1)} %fusion.1.refs_0_, ...), custom_call_target="tpu_custom_call" | custom-call | tf_op jit(solution)/shard_map/opening1/pallas_call | solution.py:598
  130.9 102.2 %attend.1 = (bf16[2,768,2048]{2,1,0:T(8,128)(2,1)}, bf16[2,576,512]{2,1,0:T(8,128)(2,1)}, bf16[2,768,512]{2,1,0:T(8,128)(2,1)}, bf16[2,768,512]{2,1,0:T(8,128)(2...) custom-call(bf16[2,768,2176]{2,1,0:T(8,128)(2,1)} %bitcast.49, ...), custom_call_target="tpu_custom_call" | custom-call | tf_op jit(solution)/shard_map/attend/pallas_call | solution.py:1163
  233.1 99.4 %collect2.1 = (bf16[4,144,2048]{2,1,0:T(8,128)(2,1)}, bf16[4,704,512]{2,1,0:T(8,128)(2,1)}, bf16[4,704,512]{2,1,0:T(8,128)(2,1)}) custom-call(bf16[1,2,576,512]{3,2,1,0:T(8,128)(2,1)} %bitcast.63, bf16[4,512,256]{2,1,0:T(8,128)(2,1)} %get-tuple-element.88.refs_1_.refs_4_, bf16[4,512,256]{2,1,0:T(8,128)(2,1)} %get-tuple-element.89.refs_2_.refs_5_, ...), custom_call_target="tpu_custom_call" | custom-call | tf_op jit(solution)/shard_map/collect2/pallas_call | solution.py:859
  332.5 6.6 owner_forward.1
  339.0 93.9 %spread3.1 = (bf16[2,4,144,2048]{3,2,1,0:T(8,128)(2,1)}, bf16[4,704,512]{2,1,0:T(8,128)(2,1)}, bf16[4,704,512]{2,1,0:T(8,128)(2,1)}) custom-call(bf16[4,144,2048]{2,1,0:T(8,128)(2,1)} %bitcast.70, bf16[4,704,512]{2,1,0:T(8,128)(2,1)} %bitcast.67), custom_call_target="tpu_custom_call" | custom-call | tf_op jit(solution)/shard_map/spread3/pallas_call | solution.py:705
  433.0 35.5 %experts.1 = (bf16[2,576,2048]{2,1,0:T(8,128)(2,1)}, bf16[2,2,576,704]{3,2,1,0:T(8,128)(2,1)}, bf16[2,2,576,704]{3,2,1,0:T(8,128)(2,1)}, bf16[2,2,576,704]{3,2,1,0:T(8,128)(2,1)}) custom-call(bf16[2,576,2048]{2,1,0:T(8,128)(2,1)} %bitcast.46, bf16[2,576,2048]{2,1,0:T(8,128)(2,1)} %bitcast.65, bf16[4,16,512]{2,1,0:T(8,128)(2,1)} %get-tuple-element.77.refs_2_.small_ref, ...), custom_call_target="tpu_custom_call" | custom-call | tf_op jit(solution)/shard_map/experts/pallas_call | solution.py:1213
  468.4 44.6 %mlp_grads.1 = (bf16[4,2112,512]{2,1,0:T(8,128)(2,1)}, bf16[4,240,512]{2,1,0:T(8,128)(2,1)}) custom-call(bf16[1152,2048]{1,0:T(8,128)(2,1)} %bitcast.47, bf16[1152,2048]{1,0:T(8,128)(2,1)} %bitcast.66, bf16[2,1152,704]{2,1,0:T(8,128)(2,1)} %bitcast.57, bf16[2,1152,704]{2,1,0:T(8,128)(2,1)} %bitcast.58, bf16[2,1152,704]{2,1,0:T(8,128)(2,1)} %bitcast.59, ...), custom_call_target="tpu_custom_call" | custom-call | tf_op jit(solution)/shard_map/mlp_grads/pallas_call | solution.py:1306
  513.0 127.0 %collect5.1 = (bf16[4,144,2048]{2,1,0:T(8,128)(2,1)}, bf16[4,144,2048]{2,1,0:T(8,128)(2,1)}, bf16[4,704,512]{2,1,0:T(8,128)(2,1)}) custom-call(bf16[2,2,576,704]{3,2,1,0:T(8,128)(2,1)} %get-tuple-element.102.refs_0_, bf16[2,2,576,704]{3,2,1,0:T(8,128)(2,1)} %get-tuple-element.103.refs_1_, bf16[2,2,576,704]{3,2,1,0:T(8,128)(2,1)} %get-tuple-element.104.refs_2_, ...), custom_call_target="tpu_custom_call" | custom-call | tf_op jit(solution)/shard_map/collect5/pallas_call | solution.py:859
  640.1 12.3 %owner_middle.1 = (bf16[192,2048]{1,0:T(8,128)(2,1)}, f32[192,2048]{1,0:T(8,128)}, bf16[576,2048]{1,0:T(8,128)(2,1)}, f32[192,128]{1,0:T(8,128)}, f32[16,2048]{1,0:T(8,128)}) custom-call(bf16[192,2048]{1,0:T(8,128)(2,1)} %x_ref.3, f32[192,4]{1,0:T(8,128)} %convert_element_type.39.ids_ref.refs_1_, bf16[4,16,512]{2,1,0:T(8,128)(2,1)} %get-tuple-element.77.refs_2_.small_ref, ...), custom_call_target="tpu_custom_call" | custom-call | tf_op jit(solution)/shard_map/owner_middle/pallas_call | solution.py:1662
  652.4 66.0 %spread6.1 = (bf16[2,4,144,2048]{3,2,1,0:T(8,128)(2,1)}, bf16[4,336,512]{2,1,0:T(8,128)(2,1)}) custom-call(bf16[4,144,2048]{2,1,0:T(8,128)(2,1)} %bitcast.71, bf16[4,2112,512]{2,1,0:T(8,128)(2,1)} %get-tuple-element.106.refs_9_.refs_1_.refs_11_.refs_4_.refs_5_), custom_call_target="tpu_custom_call" | custom-call | tf_op jit(solution)/shard_map/spread6/pallas_call | solution.py:705
  718.4 47.7 %attend_back.1 = (bf16[2,768,1536]{2,1,0:T(8,128)(2,1)}, bf16[4,320,512]{2,1,0:T(8,128)(2,1)}) custom-call(bf16[2,576,512]{2,1,0:T(8,128)(2,1)} %get-tuple-element.84.refs_0_, bf16[2,768,512]{2,1,0:T(8,128)(2,1)} %get-tuple-element.85.refs_1_, bf16[2,768,512]{2,1,0:T(8,128)(2,1)} %get-tuple-element.86.refs_2_, bf16[2,576,2048]{2,1,0:T(8,128)(2,1)} %bitcast.55, ...), custom_call_target="tpu_custom_call" | custom-call | tf_op jit(solution)/shard_map/attend_back/pallas_call | solution.py:1431
  766.1 34.3 %attn_grads.1 = (bf16[4,512,256]{2,1,0:T(8,128)(2,1)}, bf16[4,512,256]{2,1,0:T(8,128)(2,1)}, bf16[4,512,256]{2,1,0:T(8,128)(2,1)}, bf16[4,512,256]{2,1,0:T(8,128)(2,1)}, bf16[4,256,512]{2,1,0:T(8,128)(2,1)}) custom-call(bf16[1536,2048]{1,0:T(8,128)(2,1)} %bitcast.62, bf16[1536,1536]{1,0:T(8,128)(2,1)} %bitcast.53, bf16[1152,2048]{1,0:T(8,128)(2,1)} %bitcast.56, ...), custom_call_target="tpu_custom_call" | custom-call | tf_op jit(solution)/shard_map/attn_grads/pallas_call | solution.py:1362
  800.5 110.8 %collect7.1 = (bf16[4,192,2048]{2,1,0:T(8,128)(2,1)}, bf16[4,256,512]{2,1,0:T(8,128)(2,1)}, bf16[4,512,256]{2,1,0:T(8,128)(2,1)}, bf16[4,512,256]{2,1,0:T(8,128)(2,1)}) custom-call(bf16[1,2,768,1536]{3,2,1,0:T(8,128)(2,1)} %bitcast.54, bf16[4,512,256]{2,1,0:T(8,128)(2,1)} %get-tuple-element.79.refs_3_.refs_1_, ...), custom_call_target="tpu_custom_call" | custom-call | tf_op jit(solution)/shard_map/collect7/pallas_call | solution.py:859
  911.2 5.8 owner_back.1
  917.0 51.3 %finish8.1 = (f32[16,128]{1,0:T(8,128)}, bf16[2,192,2048]{2,1,0:T(8,128)(2,1)}, bf16[4,512,256]{2,1,0:T(8,128)(2,1)}, bf16[4,512,256]{2,1,0:T(8,128)(2,1)}) custom-call(f32[4,4,16,128]{3,2,1,0:T(8,128)} %get-tuple-element.122.refs_0_, bf16[2,192,2048]{2,1,0:T(8,128)(2,1)} %get-tuple-element.123.refs_1_, bf16[4,512,256]{2,1,0:T(8,128)(2,1)} %get-tuple-element.124.refs_2_, ...), custom_call_target="tpu_custom_call" | custom-call | tf_op jit(solution)/shard_map/finish8/pallas_call | solution.py:1021
  968.3 2.7 slice_bitcast_fusion
  971.0 0.5 slice_bitcast_fusion.4
  971.5 0.6 slice_bitcast_fusion.2
  972.1 13.0 %unpack.1 = (f32[4,2,704,512]{3,2,1,0:T(8,128)}, f32[4,704,512]{2,1,0:T(8,128)}, f32[4,512,256]{2,1,0:T(8,128)}, f32[4,512,256]{2,1,0:T(8,128)}, f32[2,512,256]{2,1,0:T(8,128)}) custom-call(bf16[4,240,512]{2,1,0:T(8,128)(2,1)} %get-tuple-element.128.refs_0_, bf16[4,704,512]{2,1,0:T(8,128)(2,1)} %get-tuple-element.129.refs_1_, ...), custom_call_target="tpu_custom_call" | custom-call | tf_op jit(solution)/shard_map/unpack/pallas_call | solution.py:1494
  (12 shorter events, 0.5 us)
Async XLA Ops:
  8.5 4.8 copy-start
  968.3 2.7 copy-start.1
